TPU v7x, 32 devices: a whole 2x2x4 slice. The times are simulated.
32 devices in a mesh: fsdp: 32 (over z, y, x, core).
Axes of the slice: x: 2, y: 2, z: 4, core: 2. Of those that a mesh axis runs over, the one named last changes fastest.
Arguments:
- x_vit: bfloat16 [18432, 1024], P('fsdp'), may hold values from -6 to 6
- x_hires: bfloat16 [32768, 1536], P('fsdp'), may hold values from -6 to 6
- image_live: int32 [32], P('fsdp'), may hold values 0 or 1
- grad_vit: bfloat16 [18432, 1024], P('fsdp'), may hold values from -6 to 6
- grad_hires: bfloat16 [32768, 1536], P('fsdp'), may hold values from -6 to 6
- gain_one: bfloat16 [1024], P('fsdp'), may hold values from 0.25 to 1.75
- w_qkv: bfloat16 [1024, 3072], P('fsdp'), may hold values from -0.1875 to 0.1875
- w_out: bfloat16 [1024, 1024], P('fsdp'), may hold values from -1.5 to 1.5
- gain_two: bfloat16 [1024], P('fsdp'), may hold values from 0.25 to 1.75
- w_up: bfloat16 [1024, 4096], P('fsdp'), may hold values from -0.1875 to 0.1875
- w_down: bfloat16 [4096, 1024], P('fsdp'), may hold values from -0.1875 to 0.1875
- conv_seven: bfloat16 [49, 1536], P(None, 'fsdp'), may hold values from -0.875 to 0.875
- gain_three: bfloat16 [1536], P('fsdp'), may hold values from 0.25 to 1.75
- w_expand: bfloat16 [1536, 6144], P('fsdp'), may hold values from -0.15625 to 0.15625
- w_shrink: bfloat16 [6144, 1536], P('fsdp'), may hold values from -0.15625 to 0.15625
- layer_scale: bfloat16 [1536], P('fsdp'), may hold values from 0.29882812 to 1.5
- w_adapt: bfloat16 [1536, 1024], P('fsdp'), may hold values from -0.3125 to 0.3125
- conv_three: bfloat16 [9, 1024], P(None, 'fsdp'), may hold values from -2 to 2
- w_gate_in: bfloat16 [1024, 1024], P('fsdp'), may hold values from -0.1875 to 0.1875
- w_gate_out: bfloat16 [1024, 1024], P('fsdp'), may hold values from -0.25 to 0.25
Outputs:
- joined: bfloat16 [18432, 1024], P('fsdp')
- hires_next: bfloat16 [32768, 1536], P('fsdp')
- grad_x_vit: float32 [18432, 1024], P('fsdp')
- grad_x_hires: float32 [32768, 1536], P('fsdp')
- grad_gain_one: float32 [1024], P('fsdp')
- grad_w_qkv: float32 [1024, 3072], P('fsdp')
- grad_w_out: float32 [1024, 1024], P('fsdp')
- grad_gain_two: float32 [1024], P('fsdp')
- grad_w_up: float32 [1024, 4096], P('fsdp')
- grad_w_down: float32 [4096, 1024], P('fsdp')
- grad_conv_seven: float32 [49, 1536], P(None, 'fsdp')
- grad_gain_three: float32 [1536], P('fsdp')
- grad_w_expand: float32 [1536, 6144], P('fsdp')
- grad_w_shrink: float32 [6144, 1536], P('fsdp')
- grad_layer_scale: float32 [1536], P('fsdp')
- grad_w_adapt: float32 [1536, 1024], P('fsdp')
- grad_conv_three: float32 [9, 1024], P(None, 'fsdp')
- grad_w_gate_in: float32 [1024, 1024], P('fsdp')
- grad_w_gate_out: float32 [1024, 1024], P('fsdp')
All inputs are finite; a program needn't handle non-finite values. No bound on the sum of `image_live` on one device may be relied on, other than what follows from the above.
Results may differ from a plain program's by a relative error of at most 0.02.
Values may be sent and summed in bfloat16 or wider, within the bound.
No kernel may reach another device: no remote copies, remote signals or barrier semaphores. Data moves between devices by JAX's collectives and lax.ppermute only.
A program may use at most 448 MiB of HBM per device.

v0:
```python
import math

import jax
import jax.numpy as jnp
from jax import lax
from jax.sharding import PartitionSpec as P

D = 1024
HEADS = 16
HEAD_DIM = 64
C = 1536
KS = 7
KA = 3
GRID_LR = 24
GRID_HR = 32
PATCHES = 576


def dense(operand, weight):
    return jnp.einsum("...i,ij->...j", operand, weight, preferred_element_type=jnp.float32)


def dense_back(gradient, weight):
    return jnp.einsum("...j,ij->...i", gradient, weight, preferred_element_type=jnp.float32)


def outer_sum(operand, gradient):
    flat_left = operand.reshape(-1, operand.shape[-1])
    flat_right = gradient.reshape(-1, gradient.shape[-1])
    return jnp.einsum("ri,rj->ij", flat_left, flat_right, preferred_element_type=jnp.float32)


def norm_rows(values, epsilon):
    average = jnp.mean(values, axis=-1, keepdims=True)
    centred = values - average
    spread = jnp.mean(centred * centred, axis=-1, keepdims=True)
    inverse = lax.rsqrt(spread + epsilon)
    return (centred * inverse, inverse)


def norm_back(grad_normed, normed, inverse):
    first_mean = jnp.mean(grad_normed, axis=-1, keepdims=True)
    second_mean = jnp.mean(grad_normed * normed, axis=-1, keepdims=True)
    return inverse * (grad_normed - first_mean - normed * second_mean)


def gelu_exact(values):
    return jax.nn.gelu(values, approximate=False)


def gelu_slope(values):
    normal_cdf = 0.5 * (1.0 + jax.scipy.special.erf(values * (1.0 / math.sqrt(2.0))))
    density = jnp.exp(-0.5 * values * values) * (1.0 / math.sqrt(2.0 * math.pi))
    return normal_cdf + values * density


def pool_table(fine_cells, coarse_cells):
    coarse_index = jnp.arange(coarse_cells, dtype=jnp.int32)[:, None]
    fine_index = jnp.arange(fine_cells, dtype=jnp.int32)[None, :]
    window_start = coarse_index * fine_cells // coarse_cells
    window_end = ((coarse_index + 1) * fine_cells + coarse_cells - 1) // coarse_cells
    inside = ((fine_index >= window_start) & (fine_index < window_end)).astype(jnp.float32)
    return inside / jnp.sum(inside, axis=1, keepdims=True)


def pad_grid(grid_field, tap_reach):
    return jnp.pad(grid_field, ((0, 0), (tap_reach, tap_reach), (tap_reach, tap_reach), (0, 0)))


def depthwise(grid_field, tap_weights, kernel_width):
    tap_reach = kernel_width // 2
    edge_cells = grid_field.shape[1]
    padded = pad_grid(grid_field, tap_reach)
    summed = jnp.zeros_like(grid_field)
    for tap_row in range(kernel_width):
        for tap_col in range(kernel_width):
            summed = (
                summed
                + padded[:, tap_row : tap_row + edge_cells, tap_col : tap_col + edge_cells]
                * tap_weights[tap_row * kernel_width + tap_col]
            )
    return summed


def depthwise_back(grid_field, tap_weights, grad_out, kernel_width):
    tap_reach = kernel_width // 2
    edge_cells = grid_field.shape[1]
    padded = pad_grid(grid_field, tap_reach)
    padded_grad = pad_grid(grad_out, tap_reach)
    grad_field = jnp.zeros_like(grid_field)
    tap_grads = []
    for tap_row in range(kernel_width):
        for tap_col in range(kernel_width):
            window = padded[:, tap_row : tap_row + edge_cells, tap_col : tap_col + edge_cells]
            tap_grads.append(jnp.sum(window * grad_out, axis=(0, 1, 2)))
            back_row = 2 * tap_reach - tap_row
            back_col = 2 * tap_reach - tap_col
            grad_field = (
                grad_field
                + padded_grad[:, back_row : back_row + edge_cells, back_col : back_col + edge_cells]
                * tap_weights[tap_row * kernel_width + tap_col]
            )
    return (grad_field, jnp.stack(tap_grads))


def conv_forward(hires_in, conv_set):
    seven_taps = conv_set[0].astype(jnp.float32)
    gain_conv = conv_set[1].astype(jnp.float32)
    conved = depthwise(hires_in, seven_taps, KS)
    normed, inverse = norm_rows(conved, 1e-06)
    normed_low = (normed * gain_conv).astype(jnp.bfloat16)
    expanded = dense(normed_low, conv_set[2])
    activated = gelu_exact(expanded).astype(jnp.bfloat16)
    shrunk = dense(activated, conv_set[3])
    return (normed, inverse, normed_low, expanded, activated, shrunk)


def shards(
    x_vit,
    x_hires,
    image_live,
    grad_vit,
    grad_hires,
    gain_one,
    w_qkv,
    w_out,
    gain_two,
    w_up,
    w_down,
    conv_seven,
    gain_three,
    w_expand,
    w_shrink,
    layer_scale,
    w_adapt,
    conv_three,
    w_gate_in,
    w_gate_out,
):
    images = image_live.shape[0]
    attend_scale = HEAD_DIM ** (-0.5)
    conv_set = (
        lax.all_gather(conv_seven, "fsdp", axis=1, tiled=True),
        lax.all_gather(gain_three, "fsdp", axis=0, tiled=True),
        lax.all_gather(w_expand, "fsdp", axis=0, tiled=True),
        lax.all_gather(w_shrink, "fsdp", axis=0, tiled=True),
        lax.all_gather(layer_scale, "fsdp", axis=0, tiled=True),
    )
    adapter_set = (
        lax.all_gather(w_adapt, "fsdp", axis=0, tiled=True),
        lax.all_gather(conv_three, "fsdp", axis=1, tiled=True),
        lax.all_gather(w_gate_in, "fsdp", axis=0, tiled=True),
        lax.all_gather(w_gate_out, "fsdp", axis=0, tiled=True),
    )
    vit_set = (
        lax.all_gather(gain_one, "fsdp", axis=0, tiled=True),
        lax.all_gather(w_qkv, "fsdp", axis=0, tiled=True),
        lax.all_gather(w_out, "fsdp", axis=0, tiled=True),
        lax.all_gather(gain_two, "fsdp", axis=0, tiled=True),
        lax.all_gather(w_up, "fsdp", axis=0, tiled=True),
        lax.all_gather(w_down, "fsdp", axis=0, tiled=True),
    )
    live_tokens = image_live.astype(jnp.float32)[:, None, None]
    live_maps = image_live.astype(jnp.float32)[:, None, None, None]
    table = pool_table(GRID_HR, GRID_LR)
    patch_in = x_vit.astype(jnp.float32).reshape(images, PATCHES, D)
    normed_a, inverse_a = norm_rows(patch_in, 1e-05)
    normed_a_low = (normed_a * vit_set[0].astype(jnp.float32)).astype(jnp.bfloat16)
    qkv_low = dense(normed_a_low, vit_set[1]).astype(jnp.bfloat16)
    queries = qkv_low[..., :D].reshape(images, PATCHES, HEADS, HEAD_DIM)
    keys_part = qkv_low[..., D : 2 * D].reshape(images, PATCHES, HEADS, HEAD_DIM)
    values_part = qkv_low[..., 2 * D :].reshape(images, PATCHES, HEADS, HEAD_DIM)
    scores = (
        jnp.einsum("nphe,nkhe->nhpk", queries, keys_part, preferred_element_type=jnp.float32)
        * attend_scale
    )
    logsum = jax.nn.logsumexp(scores, axis=-1, keepdims=True)
    probs_low = jnp.exp(scores - logsum).astype(jnp.bfloat16)
    attended_low = (
        jnp.einsum("nhpk,nkhe->nphe", probs_low, values_part, preferred_element_type=jnp.float32)
        .reshape(images, PATCHES, D)
        .astype(jnp.bfloat16)
    )
    resid_one = patch_in + dense(attended_low, vit_set[2])
    normed_b, inverse_b = norm_rows(resid_one, 1e-05)
    normed_b_low = (normed_b * vit_set[3].astype(jnp.float32)).astype(jnp.bfloat16)
    hidden_up = dense(normed_b_low, vit_set[4])
    hidden_act = gelu_exact(hidden_up).astype(jnp.bfloat16)
    resid_two = resid_one + dense(hidden_act, vit_set[5])
    hires_in = x_hires.astype(jnp.float32).reshape(images, GRID_HR, GRID_HR, C)
    shrunk_fwd = conv_forward(hires_in, conv_set)[5]
    hires_out = hires_in + conv_set[4].astype(jnp.float32) * shrunk_fwd
    pooled_rows = jnp.einsum("ia,nabc->nibc", table, hires_out, precision=lax.Precision.HIGHEST)
    pooled = jnp.einsum("jb,nibc->nijc", table, pooled_rows, precision=lax.Precision.HIGHEST)
    pooled_low = pooled.astype(jnp.bfloat16)
    adapted = dense(pooled_low, adapter_set[0])
    mixed = depthwise(adapted, adapter_set[1].astype(jnp.float32), KA).reshape(images, PATCHES, D)
    mixed_low = mixed.astype(jnp.bfloat16)
    gate_hidden = dense(mixed_low, adapter_set[2])
    gate_act = gelu_exact(gate_hidden).astype(jnp.bfloat16)
    gate_value = jnp.tanh(dense(gate_act, adapter_set[3]))
    joined = live_tokens * (resid_two + gate_value * mixed)
    hires_next = live_maps * hires_out
    adapter_back = (
        lax.all_gather(w_adapt, "fsdp", axis=0, tiled=True),
        lax.all_gather(conv_three, "fsdp", axis=1, tiled=True),
        lax.all_gather(w_gate_in, "fsdp", axis=0, tiled=True),
        lax.all_gather(w_gate_out, "fsdp", axis=0, tiled=True),
    )
    conv_back = (
        lax.all_gather(conv_seven, "fsdp", axis=1, tiled=True),
        lax.all_gather(gain_three, "fsdp", axis=0, tiled=True),
        lax.all_gather(w_expand, "fsdp", axis=0, tiled=True),
        lax.all_gather(w_shrink, "fsdp", axis=0, tiled=True),
        lax.all_gather(layer_scale, "fsdp", axis=0, tiled=True),
    )
    vit_back = (
        lax.all_gather(gain_one, "fsdp", axis=0, tiled=True),
        lax.all_gather(w_qkv, "fsdp", axis=0, tiled=True),
        lax.all_gather(w_out, "fsdp", axis=0, tiled=True),
        lax.all_gather(gain_two, "fsdp", axis=0, tiled=True),
        lax.all_gather(w_up, "fsdp", axis=0, tiled=True),
        lax.all_gather(w_down, "fsdp", axis=0, tiled=True),
    )
    grad_joined = grad_vit.astype(jnp.float32).reshape(images, PATCHES, D) * live_tokens
    grad_next = grad_hires.astype(jnp.float32).reshape(images, GRID_HR, GRID_HR, C) * live_maps
    grad_mixed = grad_joined * gate_value
    grad_logit = (grad_joined * mixed * (1.0 - gate_value * gate_value)).astype(jnp.bfloat16)
    d_gate_out = outer_sum(gate_act, grad_logit)
    grad_gate_low = (dense_back(grad_logit, adapter_back[3]) * gelu_slope(gate_hidden)).astype(
        jnp.bfloat16
    )
    d_gate_in = outer_sum(mixed_low, grad_gate_low)
    grad_mixed = grad_mixed + dense_back(grad_gate_low, adapter_back[2])
    grad_adapted, d_conv_three = depthwise_back(
        adapted,
        adapter_back[1].astype(jnp.float32),
        grad_mixed.reshape(images, GRID_LR, GRID_LR, D),
        KA,
    )
    grad_adapted_low = grad_adapted.astype(jnp.bfloat16)
    d_adapt = outer_sum(pooled_low, grad_adapted_low)
    grad_pooled = dense_back(grad_adapted_low, adapter_back[0])
    grad_rows = jnp.einsum("jb,nijc->nibc", table, grad_pooled, precision=lax.Precision.HIGHEST)
    grad_hires_out = grad_next + jnp.einsum(
        "ia,nibc->nabc", table, grad_rows, precision=lax.Precision.HIGHEST
    )
    adapter_grads = (
        lax.psum_scatter(d_adapt, "fsdp", scatter_dimension=0, tiled=True),
        lax.psum_scatter(d_conv_three, "fsdp", scatter_dimension=1, tiled=True),
        lax.psum_scatter(d_gate_in, "fsdp", scatter_dimension=0, tiled=True),
        lax.psum_scatter(d_gate_out, "fsdp", scatter_dimension=0, tiled=True),
    )
    normed_c, inverse_c, normed_c_low, expanded, activated, shrunk = conv_forward(
        hires_in, conv_back
    )
    d_layer_scale = jnp.sum(grad_hires_out * shrunk, axis=(0, 1, 2))
    grad_shrunk_low = (grad_hires_out * conv_back[4].astype(jnp.float32)).astype(jnp.bfloat16)
    d_shrink = outer_sum(activated, grad_shrunk_low)
    grad_expanded_low = (dense_back(grad_shrunk_low, conv_back[3]) * gelu_slope(expanded)).astype(
        jnp.bfloat16
    )
    d_expand = outer_sum(normed_c_low, grad_expanded_low)
    grad_normed_c = dense_back(grad_expanded_low, conv_back[2])
    d_gain_three = jnp.sum(grad_normed_c * normed_c, axis=(0, 1, 2))
    grad_conved = norm_back(grad_normed_c * conv_back[1].astype(jnp.float32), normed_c, inverse_c)
    grad_through, d_conv_seven = depthwise_back(
        hires_in, conv_back[0].astype(jnp.float32), grad_conved, KS
    )
    grad_hires_in = grad_hires_out + grad_through
    conv_grads = (
        lax.psum_scatter(d_conv_seven, "fsdp", scatter_dimension=1, tiled=True),
        lax.psum_scatter(d_gain_three, "fsdp", scatter_dimension=0, tiled=True),
        lax.psum_scatter(d_expand, "fsdp", scatter_dimension=0, tiled=True),
        lax.psum_scatter(d_shrink, "fsdp", scatter_dimension=0, tiled=True),
        lax.psum_scatter(d_layer_scale, "fsdp", scatter_dimension=0, tiled=True),
    )
    grad_down_low = grad_joined.astype(jnp.bfloat16)
    d_down = outer_sum(hidden_act, grad_down_low)
    grad_hidden_low = (dense_back(grad_down_low, vit_back[5]) * gelu_slope(hidden_up)).astype(
        jnp.bfloat16
    )
    d_up = outer_sum(normed_b_low, grad_hidden_low)
    grad_normed_b = dense_back(grad_hidden_low, vit_back[4])
    d_gain_two = jnp.sum(grad_normed_b * normed_b, axis=(0, 1))
    grad_first = grad_joined + norm_back(
        grad_normed_b * vit_back[3].astype(jnp.float32), normed_b, inverse_b
    )
    grad_first_low = grad_first.astype(jnp.bfloat16)
    d_out = outer_sum(attended_low, grad_first_low)
    grad_att_low = (
        dense_back(grad_first_low, vit_back[2])
        .astype(jnp.bfloat16)
        .reshape(images, PATCHES, HEADS, HEAD_DIM)
    )
    scores_again = (
        jnp.einsum("nphe,nkhe->nhpk", queries, keys_part, preferred_element_type=jnp.float32)
        * attend_scale
    )
    probs_again = jnp.exp(scores_again - logsum)
    probs_again_low = probs_again.astype(jnp.bfloat16)
    grad_probs = jnp.einsum(
        "nphe,nkhe->nhpk", grad_att_low, values_part, preferred_element_type=jnp.float32
    )
    grad_values = jnp.einsum(
        "nhpk,nphe->nkhe", probs_again_low, grad_att_low, preferred_element_type=jnp.float32
    )
    row_total = jnp.sum(probs_again * grad_probs, axis=-1, keepdims=True)
    grad_scores_low = (probs_again * (grad_probs - row_total)).astype(jnp.bfloat16)
    grad_queries = (
        jnp.einsum(
            "nhpk,nkhe->nphe", grad_scores_low, keys_part, preferred_element_type=jnp.float32
        )
        * attend_scale
    )
    grad_keys = (
        jnp.einsum("nhpk,nphe->nkhe", grad_scores_low, queries, preferred_element_type=jnp.float32)
        * attend_scale
    )
    grad_qkv_low = jnp.concatenate(
        (
            grad_queries.reshape(images, PATCHES, D),
            grad_keys.reshape(images, PATCHES, D),
            grad_values.reshape(images, PATCHES, D),
        ),
        axis=-1,
    ).astype(jnp.bfloat16)
    d_qkv = outer_sum(normed_a_low, grad_qkv_low)
    grad_normed_a = dense_back(grad_qkv_low, vit_back[1])
    d_gain_one = jnp.sum(grad_normed_a * normed_a, axis=(0, 1))
    grad_patches = grad_first + norm_back(
        grad_normed_a * vit_back[0].astype(jnp.float32), normed_a, inverse_a
    )
    vit_grads = (
        lax.psum_scatter(d_gain_one, "fsdp", scatter_dimension=0, tiled=True),
        lax.psum_scatter(d_qkv, "fsdp", scatter_dimension=0, tiled=True),
        lax.psum_scatter(d_out, "fsdp", scatter_dimension=0, tiled=True),
        lax.psum_scatter(d_gain_two, "fsdp", scatter_dimension=0, tiled=True),
        lax.psum_scatter(d_up, "fsdp", scatter_dimension=0, tiled=True),
        lax.psum_scatter(d_down, "fsdp", scatter_dimension=0, tiled=True),
    )
    return (
        joined.reshape(images * PATCHES, D).astype(jnp.bfloat16),
        hires_next.reshape(images * GRID_HR * GRID_HR, C).astype(jnp.bfloat16),
        grad_patches.reshape(images * PATCHES, D),
        grad_hires_in.reshape(images * GRID_HR * GRID_HR, C),
        vit_grads[0],
        vit_grads[1],
        vit_grads[2],
        vit_grads[3],
        vit_grads[4],
        vit_grads[5],
        conv_grads[0],
        conv_grads[1],
        conv_grads[2],
        conv_grads[3],
        conv_grads[4],
        adapter_grads[0],
        adapter_grads[1],
        adapter_grads[2],
        adapter_grads[3],
    )


def solution(mesh):
    in_specs = (
        P("fsdp", None),
        P("fsdp", None),
        P("fsdp"),
        P("fsdp", None),
        P("fsdp", None),
        P("fsdp"),
        P("fsdp", None),
        P("fsdp", None),
        P("fsdp"),
        P("fsdp", None),
        P("fsdp", None),
        P(None, "fsdp"),
        P("fsdp"),
        P("fsdp", None),
        P("fsdp", None),
        P("fsdp"),
        P("fsdp", None),
        P(None, "fsdp"),
        P("fsdp", None),
        P("fsdp", None),
    )
    out_specs = (
        P("fsdp", None),
        P("fsdp", None),
        P("fsdp", None),
        P("fsdp", None),
        P("fsdp"),
        P("fsdp", None),
        P("fsdp", None),
        P("fsdp"),
        P("fsdp", None),
        P("fsdp", None),
        P(None, "fsdp"),
        P("fsdp"),
        P("fsdp", None),
        P("fsdp", None),
        P("fsdp"),
        P("fsdp", None),
        P(None, "fsdp"),
        P("fsdp", None),
        P("fsdp", None),
    )
    return jax.shard_map(shards, mesh=mesh, in_specs=in_specs, out_specs=out_specs, check_vma=False)
```

profile of v0, /device:TPU:0, one launch (start us, length us, event | category | flops | bytes accessed | tf_op | source)
XLA Modules:
  0.0 2868.7 jit_solution(9520529159110429016)
XLA Ops:
  14.0 45.1 %all_gather.67 = bf16[49,1536]{0,1:T(8,128)(2,1)S(1)} all-gather(bf16[49,48]{0,1:T(8,128)(2,1)} %param.31), channel_id=1, replica_groups=mesh['fsdp'=32] {'fsdp'}, dimensions={1}, use_global_device_ids=true | all-gather | bytes 155232 | tf_op jit(solution)/shard_map/all_gather | solution.py:143
  84.5 37.2 %all-reduce.13 = (bf16[1536]{0:T(1024)(128)(2,1)S(1)}, bf16[1536]{0:T(1024)(128)(2,1)S(1)}, bf16[1024]{0:T(1024)(128)(2,1)S(1)}, bf16[1024]{0:T(1024)(128)(2,1)S(1)}) all-reduce(bf16[1536]{0:T(1024)(128)(2,1)S(1)} %dynamic-update-slice.3, bf16[1536]{0:T(1024)(128)(2,1)S(1)} %dynamic-update-slice.2, ...), channel_id=1, replica_groups=mesh['fsdp'=32] {'fsdp'}, use_global_device_ids=true, to_apply=%add.7 | all-reduce | flops 5120 | bytes 20480
  123.5 40.6 %all-gather = bf16[32,32,9]{1,2,0:T(8,128)(2,1)S(1)} all-gather(bf16[1,32,9]{1,2,0:T(8,128)(2,1)S(1)} %bitcast.282), channel_id=1, replica_groups=mesh['fsdp'=32] {'fsdp'}, dimensions={0}, use_global_device_ids=true | all-gather | bytes 19008 | tf_op jit(solution)/shard_map/all_gather | solution.py:151
  167.9 72.1 %fusion.270 = (f32[32,32]{1,0:T(8,128)S(1)}, f32[1,32,32,1536]{3,2,1,0:T(8,128)}) fusion(f32[1536]{0:T(1024)S(1)} %get-tuple-element.144, f32[1536]{0:T(1024)S(1)} %get-tuple-element.145, f32[1536]{0:T(1024)S(1)} %get-tuple-element.146, f32[1536]{0:T(1024)S(1)} %get-tuple-element.147, f32[1536]{0:T(1024)S(1)} %get-tuple-element.148, ...), kind=kLoop, calls=%fused_computation.557 | loop fusion | flops 154139648 | bytes 12888064 | tf_op jit(solution)/shard_map/reduce_sum | solution.py:34
  271.9 13.7 fusion.227
  289.6 29.9 %fusion.26 = (bf16[576,4096]{1,0:T(8,128)(2,1)}, f32[576,4096]{1,0:T(8,128)}) fusion(bf16[1024,4096]{1,0:T(8,128)(2,1)} %all-gather.15.cloned.1.call-done, f32[576,1024]{1,0:T(8,128)S(1)} %get-tuple-element.231, f32[1024]{0:T(1024)S(1)} %convert_element_type.195, f32[576]{0:T(1024)S(1)} %add_rsqrt_fusion.1, f32[576]{0:T(1024)S(1)} %broadcast_multiply_fusion.7), kind=kOutput, calls=%fused_computation.145 | convolution fusion | flops 4987551744 | bytes 24912384 | tf_op jit(solution)/shard_map/...i,ij->...j/dot_general | solution.py:20
  339.2 86.6 %all-gather.19.cloned.1.call-done = bf16[1536,6144]{1,0:T(8,128)(2,1)} async-done(((bf16[48,6144]{1,0:T(8,128)(2,1)}), bf16[1536,6144]{1,0:T(8,128)(2,1)}) %all-gather.19.cloned.1.call-update) | async-done | bytes 18874384 | tf_op jit(solution)/shard_map/all_gather | solution.py:145
  425.8 31.2 %convert_reduce_fusion.1 = (u32[32,6144]{1,0:T(8,128)S(1)}, u32[32,6144]{1,0:T(8,128)S(1)}, f32[32,32,6144]{2,1,0:T(8,128)}) fusion(bf16[1536,6144]{1,0:T(8,128)(2,1)} %all-gather.19.cloned.1.call-done, f32[1,32,32,1536]{3,2,1,0:T(8,128)} %get-tuple-element.208, f32[1536]{0:T(1024)S(1)} %copy-done.43, f32[32,32]{1,0:T(8,128)S(1)} %copy-done.120, ...), kind=kOutput, calls=%fused_computation.113 | convolution fusion | flops 19402457088 | bytes 51918848 | tf_op jit(solution)/shard_map/...i,ij->...j/dot_general | solution.py:20
  457.0 58.8 %fusion.2 = bf16[32,32,6144]{2,1,0:T(8,128)(2,1)} fusion(f32[32,32,6144]{2,1,0:T(8,128)} %get-tuple-element.224, u32[32,6144]{1,0:T(8,128)S(1)} %get-tuple-element.77, u32[32,6144]{1,0:T(8,128)S(1)} %get-tuple-element.76), kind=kLoop, calls=%fused_computation.102 | loop fusion | flops 427819008 | bytes 39321600 | tf_op jit(solution)/shard_map/convert_element_type | solution.py:113
  515.8 35.6 %all-gather.21.cloned.1.call-done = bf16[6144,1536]{1,0:T(8,128)(2,1)} async-done(((bf16[192,1536]{1,0:T(8,128)(2,1)}), bf16[6144,1536]{1,0:T(8,128)(2,1)}) %all-gather.21.cloned.1.call-update) | async-done | bytes 18874384 | tf_op jit(solution)/shard_map/all_gather | solution.py:146
  551.5 29.0 %multiply_convert_fusion.2 = (bf16[32,32,1536]{2,1,0:T(8,128)(2,1)}, f32[32,32,1536]{2,1,0:T(8,128)S(1)}, f32[32,32,1536]{2,1,0:T(8,128)}) fusion(f32[]{:T(128)} %bitcast, f32[32,32,1536]{2,1,0:T(8,128)} %bitcast.225, f32[1536]{0:T(1024)S(1)} %copy-done.144, bf16[32,32,6144]{2,1,0:T(8,128)(2,1)} %fusion.2, bf16[6144,1536]{1,0:T(8,128)(2,1)} %all-gather.21.cloned.1.call-done), kind=kOutput, calls=%fused_computation.326 | convolution fusion | flops 19333644288 | bytes 53483524 | tf_op jit(solution)/shard_map/...i,ij->...j/dot_general | solution.py:20
  597.8 13.8 all-gather.23.cloned.1.call-done
  623.4 46.1 %all-gather.25.cloned.1.call-done = bf16[1024,1024]{1,0:T(8,128)(2,1)} async-done(((bf16[32,1024]{1,0:T(8,128)(2,1)}), bf16[1024,1024]{1,0:T(8,128)(2,1)}) %all-gather.25.cloned.1.call-update) | async-done | bytes 2097168 | tf_op jit(solution)/shard_map/all_gather | solution.py:152
  678.5 49.2 %all-gather.27.cloned.1.call-done = bf16[1024,1024]{1,0:T(8,128)(2,1)} async-done(((bf16[32,1024]{1,0:T(8,128)(2,1)}), bf16[1024,1024]{1,0:T(8,128)(2,1)}) %all-gather.27.cloned.1.call-update) | async-done | bytes 2097168 | tf_op jit(solution)/shard_map/all_gather | solution.py:153
  782.8 31.2 %fusion.8 = bf16[32,32,6144]{2,1,0:T(8,128)(2,1)} fusion(f32[32,32,6144]{2,1,0:T(8,128)} %get-tuple-element.224, bf16[6144,1536]{1,0:T(8,128)(2,1)} %all-gather.21.cloned.1.call-done, f32[1,32,32,1536]{3,2,1,0:T(8,128)S(1)} %get-tuple-element.204, f32[1536]{0:T(1024)S(1)} %copy-done.145), kind=kOutput, calls=%fused_computation.108 | convolution fusion | flops 19393413120 | bytes 62920704 | tf_op jit(solution)/shard_map/...j,ij->...i/dot_general | solution.py:24
  814.1 30.0 %fusion.140 = (f32[1536]{0:T(1024)}, f32[32,32]{1,0:T(8,128)S(1)}, f32[32,32,1536]{2,1,0:T(8,128)}) fusion(f32[1,32,32,1536]{3,2,1,0:T(8,128)} %get-tuple-element.208, f32[32,32]{1,0:T(8,128)S(1)} %copy-done.121, f32[32,32]{1,0:T(8,128)S(1)} %copy-done.42, f32[1536]{0:T(1024)S(1)} %copy-done.44, bf16[32,32,6144]{2,1,0:T(8,128)(2,1)} %fusion.8, ...), kind=kOutput, calls=%fused_computation.268 | convolution fusion | flops 19338358784 | bytes 44064768 | tf_op jit(solution)/shard_map/...j,ij->...i/dot_general | solution.py:24
  847.4 53.3 %multiply_reduce_fusion.2 = (f32[1536]{0:T(1024)S(1)}, f32[1536]{0:T(1024)S(1)}, f32[1536]{0:T(1024)S(1)}, f32[1536]{0:T(1024)S(1)}, f32[1536]{0:T(1024)S(1)}, /...) fusion(f32[1,32,32,1536]{3,2,1,0:T(8,128)} %bitcast.226, ...), kind=kLoop, calls=%fused_computation.275 | loop fusion | flops 67605504 | bytes 25298944 | tf_op jit(solution)/shard_map/reduce_sum | solution.py:95
  900.6 47.2 %multiply_reduce_fusion.20 = (f32[1536]{0:T(1024)}, f32[1536]{0:T(1024)S(1)}, f32[1536]{0:T(1024)S(1)}, f32[1536]{0:T(1024)S(1)}, f32[1536]{0:T(1024)S(1)}, /*in...) fusion(f32[1,32,32,1536]{3,2,1,0:T(8,128)} %get-tuple-element.2, ...), kind=kLoop, calls=%fused_computation.293 | loop fusion | flops 56595456 | bytes 12693504 | tf_op jit(solution)/shard_map/reduce_sum | solution.py:95
  947.9 30.3 %multiply_reduce_fusion.39 = (f32[1536]{0:T(1024)S(1)}, f32[1536]{0:T(1024)S(1)}, f32[1536]{0:T(1024)S(1)}, f32[1536]{0:T(1024)S(1)}, f32[1536]{0:T(1024)S(1)}, ...) fusion(f32[1,32,32,1536]{3,2,1,0:T(8,128)} %get-tuple-element.2, ...), kind=kLoop, calls=%fused_computation.312 | loop fusion | flops 42447360 | bytes 15808512 | tf_op jit(solution)/shard_map/reduce_sum | solution.py:95
  1039.1 15.0 multiply_reduce_fusion
  1054.1 20.6 multiply_convert_fusion
  1117.6 30.1 %convolution_bitcast_fusion.1 = f32[1536,6144]{1,0:T(8,128)} fusion(bf16[32,32,6144]{2,1,0:T(8,128)(2,1)} %fusion.8, f32[1,32,32,1536]{3,2,1,0:T(8,128)} %get-tuple-element.208, f32[1536]{0:T(1024)S(1)} %copy-done.45, f32[32,32]{1,0:T(8,128)S(1)} %copy-done.122, f32[32,32]{1,0:T(8,128)S(1)} %copy-done.42), kind=kOutput, calls=%fused_computation.99 | convolution fusion | flops 19333644288 | bytes 56637440 | tf_op jit(solution)/shard_map/ri,rj->ij/dot_general | solution.py:30
  1148.4 29.4 %convolution_bitcast_fusion = f32[6144,1536]{1,0:T(8,128)} fusion(bf16[32,32,6144]{2,1,0:T(8,128)(2,1)} %fusion.2, f32[1,32,32,1536]{3,2,1,0:T(8,128)} %copy-done.2, f32[1536]{0:T(1024)S(1)} %copy-done.146), kind=kOutput, calls=%fused_computation.98 | convolution fusion | flops 19330498560 | bytes 56629248 | tf_op jit(solution)/shard_map/ri,rj->ij/dot_general | solution.py:30
  1189.8 39.7 %all-reduce.12 = (f32[1024]{0:T(1024)}, f32[1024]{0:T(1024)}, f32[1536]{0:T(1024)}, f32[1536]{0:T(1024)}) all-reduce(f32[1024]{0:T(1024)} %get-tuple-element.139, f32[1024]{0:T(1024)} %get-tuple-element.129, f32[1536]{0:T(1024)S(1)} %copy-done.143, f32[1536]{0:T(1024)S(1)} %copy-done.140), channel_id=2, replica_groups=mesh['fsdp'=32] {'fsdp'}, use_global_device_ids=true, to_apply=%region_17.18.clone | all-reduce | flops 5120 | bytes 40960
  1251.3 140.0 %fusion.135 = f32[1,32,32,1536]{3,2,1,0:T(8,128)} fusion(f32[1,32,32,1536]{3,2,1,0:T(8,128)} %copy-done.2, f32[1,32,32,1536]{3,2,1,0:T(8,128)} %get-tuple-element.202, f32[1536]{0:T(1024)S(1)} %copy-done.109, f32[1536]{0:T(1024)S(1)} %copy-done.111, f32[1536]{0:T(1024)S(1)} %copy-done.113, f32[1536]{0:T(1024)S(1)} %copy-done.115, f32[1536]{0:T(1024)S(1)} %copy-done.117, ...), kind=kLoop, calls=%fused_computation.260 | loop fusion | flops 154140672 | bytes 19175424 | tf_op jit(solution)/shard_map/add | solution.py:270
  1392.7 105.7 %reduce-scatter.18.cloned.1.call-done = f32[32,1024]{1,0:T(8,128)} async-done(((f32[1024,1024]{1,0:T(8,128)}), f32[32,1024]{1,0:T(8,128)}) %reduce-scatter.18.cloned.1.call-update) | async-done | bytes 131088 | tf_op jit(solution)/shard_map/reduce_scatter | solution.py:337
  1498.4 117.3 %reduce-scatter.28.cloned.1.call-done = f32[48,1024]{1,0:T(8,128)} async-done(((f32[1536,1024]{1,0:T(8,128)}), f32[48,1024]{1,0:T(8,128)}) %reduce-scatter.28.cloned.1.call-update) | async-done | bytes 196624 | tf_op jit(solution)/shard_map/reduce_scatter | solution.py:249
  1615.7 184.9 %reduce-scatter.20.cloned.1.call-done = f32[32,4096]{1,0:T(8,128)} async-done(((f32[1024,4096]{1,0:T(8,128)}), f32[32,4096]{1,0:T(8,128)}) %reduce-scatter.20.cloned.1.call-update) | async-done | bytes 524304 | tf_op jit(solution)/shard_map/reduce_scatter | solution.py:339
  1800.6 187.2 %reduce-scatter.22.cloned.1.call-done = f32[128,1024]{1,0:T(8,128)} async-done(((f32[4096,1024]{1,0:T(8,128)}), f32[128,1024]{1,0:T(8,128)}) %reduce-scatter.22.cloned.1.call-update) | async-done | bytes 524304 | tf_op jit(solution)/shard_map/reduce_scatter | solution.py:340
  1987.8 163.4 %reduce-scatter.16.cloned.1.call-done = f32[32,3072]{1,0:T(8,128)} async-done(((f32[1024,3072]{1,0:T(8,128)}), f32[32,3072]{1,0:T(8,128)}) %reduce-scatter.16.cloned.1.call-update) | async-done | bytes 393232 | tf_op jit(solution)/shard_map/reduce_scatter | solution.py:336
  2151.3 356.0 %reduce-scatter.24.cloned.1.call-done = f32[48,6144]{1,0:T(8,128)} async-done(((f32[1536,6144]{1,0:T(8,128)}), f32[48,6144]{1,0:T(8,128)}) %reduce-scatter.24.cloned.1.call-update) | async-done | bytes 1179664 | tf_op jit(solution)/shard_map/reduce_scatter | solution.py:274
  2507.3 354.4 %reduce-scatter.26.cloned.1.call-done = f32[192,1536]{1,0:T(8,128)} async-done(((f32[6144,1536]{1,0:T(8,128)}), f32[192,1536]{1,0:T(8,128)}) %reduce-scatter.26.cloned.1.call-update) | async-done | bytes 1179664 | tf_op jit(solution)/shard_map/reduce_scatter | solution.py:275
  (498 shorter events, 326.4 us)
Async XLA Ops:
  7.2 238.5 %all-gather.11.cloned.1.call-start = ((), (), s32[]{:S(2)}) async-start(), calls=%async_computation.11 | async-start | bytes 6488064 | tf_op jit(solution)/shard_map/all_gather | solution.py:157
  7.9 277.7 %all-gather.13.cloned.1.call-start = ((), (), s32[]{:S(2)}) async-start(), calls=%async_computation.12 | async-start | bytes 2162688 | tf_op jit(solution)/shard_map/all_gather | solution.py:158
  8.7 280.9 %all-gather.15.cloned.1.call-start = ((), (), s32[]{:S(2)}) async-start(), calls=%async_computation.13 | async-start | bytes 8650752 | tf_op jit(solution)/shard_map/all_gather | solution.py:160
  9.4 310.1 %all-gather.17.cloned.1.call-start = ((), (), s32[]{:S(2)}) async-start(), calls=%async_computation.14 | async-start | bytes 8650752 | tf_op jit(solution)/shard_map/all_gather | solution.py:161
  10.0 415.8 %all-gather.19.cloned.1.call-start = ((), (), s32[]{:S(2)}) async-start(), calls=%async_computation.15 | async-start | bytes 19464192 | tf_op jit(solution)/shard_map/all_gather | solution.py:145
  10.6 540.9 %all-gather.21.cloned.1.call-start = ((), (), s32[]{:S(2)}) async-start(), calls=%async_computation.16 | async-start | bytes 19464192 | tf_op jit(solution)/shard_map/all_gather | solution.py:146
  11.1 600.4 %all-gather.23.cloned.1.call-start = ((), (), s32[]{:S(2)}) async-start(), calls=%async_computation.17 | async-start | bytes 3244032 | tf_op jit(solution)/shard_map/all_gather | solution.py:150
  11.9 657.7 %all-gather.25.cloned.1.call-start = ((), (), s32[]{:S(2)}) async-start(), calls=%async_computation.18 | async-start | bytes 2162688 | tf_op jit(solution)/shard_map/all_gather | solution.py:152
  12.6 715.1 %all-gather.27.cloned.1.call-start = ((), (), s32[]{:S(2)}) async-start(), calls=%async_computation.19 | async-start | bytes 2162688 | tf_op jit(solution)/shard_map/all_gather | solution.py:153
  13.4 1377.9 %reduce-scatter.36.cloned.1.call-start = ((), (), s32[]{:S(2)}) async-start(), calls=%async_computation.30 | async-start | bytes 540672
  63.7 103.9 %copy-start.46 = (f32[1536]{0:T(1024)}, f32[1536]{0:T(1024)S(1)}, u32[]{:S(2)}) copy-start(f32[1536]{0:T(1024)S(1)} %get-tuple-element.181) | copy-start | bytes 18436
  63.7 103.9 %copy-start.48 = (f32[1536]{0:T(1024)}, f32[1536]{0:T(1024)S(1)}, u32[]{:S(2)}) copy-start(f32[1536]{0:T(1024)S(1)} %get-tuple-element.182) | copy-start | bytes 18436
  63.7 103.9 %copy-start.50 = (f32[1536]{0:T(1024)}, f32[1536]{0:T(1024)S(1)}, u32[]{:S(2)}) copy-start(f32[1536]{0:T(1024)S(1)} %get-tuple-element.183) | copy-start | bytes 18436
  63.7 103.9 %copy-start.52 = (f32[1536]{0:T(1024)}, f32[1536]{0:T(1024)S(1)}, u32[]{:S(2)}) copy-start(f32[1536]{0:T(1024)S(1)} %get-tuple-element.184) | copy-start | bytes 18436
  63.7 103.9 %copy-start.54 = (f32[1536]{0:T(1024)}, f32[1536]{0:T(1024)S(1)}, u32[]{:S(2)}) copy-start(f32[1536]{0:T(1024)S(1)} %get-tuple-element.185) | copy-start | bytes 18436
  63.7 103.9 %copy-start.56 = (f32[1536]{0:T(1024)}, f32[1536]{0:T(1024)S(1)}, u32[]{:S(2)}) copy-start(f32[1536]{0:T(1024)S(1)} %get-tuple-element.186) | copy-start | bytes 18436
  63.7 103.9 %copy-start.58 = (f32[1536]{0:T(1024)}, f32[1536]{0:T(1024)S(1)}, u32[]{:S(2)}) copy-start(f32[1536]{0:T(1024)S(1)} %get-tuple-element.187) | copy-start | bytes 18436
  122.8 208.3 %copy-start.34 = (f32[1024]{0:T(1024)}, f32[1024]{0:T(1024)S(1)}, u32[]{:S(2)}) copy-start(f32[1024]{0:T(1024)S(1)} %convert_element_type.195) | copy-start | bytes 12292
  623.4 104.3 %copy-start.24 = (bf16[576,1024]{1,0:T(8,128)(2,1)S(1)}, bf16[576,1024]{1,0:T(8,128)(2,1)}, u32[]{:S(2)}) copy-start(bf16[576,1024]{1,0:T(8,128)(2,1)} %param.23) | copy-start | bytes 3538948
  623.4 104.3 %copy-start.32 = (f32[576]{0:T(1024)S(1)}, f32[576]{0:T(1024)}, u32[]{:S(2)}) copy-start(f32[576]{0:T(1024)} %copy-done.31) | copy-start | bytes 6916
  623.4 104.3 %copy-start.35 = (f32[1024]{0:T(1024)S(1)}, f32[1024]{0:T(1024)}, u32[]{:S(2)}) copy-start(f32[1024]{0:T(1024)} %copy-done.34) | copy-start | bytes 12292
  623.4 104.3 %copy-start.38 = (f32[576]{0:T(1024)S(1)}, f32[576]{0:T(1024)}, u32[]{:S(2)}) copy-start(f32[576]{0:T(1024)} %copy-done.37) | copy-start | bytes 6916
  751.9 640.9 %reduce-scatter.34.cloned.1.call-start = ((), (), s32[]{:S(2)}) async-start(), calls=%async_computation.29 | async-start | bytes 811008
  981.3 411.4 %reduce-scatter.30.cloned.1.call-start = ((), (), s32[]{:S(2)}) async-start(), calls=%async_computation.27 | async-start | bytes 4325376 | tf_op jit(solution)/shard_map/reduce_scatter | solution.py:251
  987.2 405.5 %reduce-scatter.32.cloned.1.call-start = ((), (), s32[]{:S(2)}) async-start(), calls=%async_computation.28 | async-start | bytes 4325376 | tf_op jit(solution)/shard_map/reduce_scatter | solution.py:252
  992.5 505.9 %reduce-scatter.18.cloned.1.call-start = ((), (), s32[]{:S(2)}) async-start(), calls=%async_computation.21 | async-start | bytes 4325376 | tf_op jit(solution)/shard_map/reduce_scatter | solution.py:337
  997.9 617.8 %reduce-scatter.28.cloned.1.call-start = ((), (), s32[]{:S(2)}) async-start(), calls=%async_computation.26 | async-start | bytes 6488064 | tf_op jit(solution)/shard_map/reduce_scatter | solution.py:249
  1004.1 796.6 %reduce-scatter.20.cloned.1.call-start = ((), (), s32[]{:S(2)}) async-start(), calls=%async_computation.22 | async-start | bytes 17301504 | tf_op jit(solution)/shard_map/reduce_scatter | solution.py:339
  1018.6 969.2 %reduce-scatter.22.cloned.1.call-start = ((), (), s32[]{:S(2)}) async-start(), calls=%async_computation.23 | async-start | bytes 17301504 | tf_op jit(solution)/shard_map/reduce_scatter | solution.py:340
  1032.5 1118.8 %reduce-scatter.16.cloned.1.call-start = ((), (), s32[]{:S(2)}) async-start(), calls=%async_computation.20 | async-start | bytes 12976128 | tf_op jit(solution)/shard_map/reduce_scatter | solution.py:336
  1116.9 1390.4 %reduce-scatter.24.cloned.1.call-start = ((), (), s32[]{:S(2)}) async-start(), calls=%async_computation.24 | async-start | bytes 38928384 | tf_op jit(solution)/shard_map/reduce_scatter | solution.py:274
  1147.7 1714.0 %reduce-scatter.26.cloned.1.call-start = ((), (), s32[]{:S(2)}) async-start(), calls=%async_computation.25 | async-start | bytes 38928384 | tf_op jit(solution)/shard_map/reduce_scatter | solution.py:275
  (144 other events, 4592.7 us)
Sparse Core Ops, SparseCore 0:
  10.9 72.7 all-gather.10
  86.5 55.1 all-gather.12
  144.5 76.3 all-gather.14
  223.6 76.1 all-gather.16
  302.5 123.2 all-gather.18
  428.6 122.8 all-gather.20
  554.3 57.1 all-gather.22
  614.4 55.1 all-gather.24
  672.4 55.2 all-gather.26
  752.0 132.8 reduce-scatter.35
  981.4 94.3 reduce-scatter.33
  1078.6 140.1 reduce-scatter.29
  1221.8 136.8 reduce-scatter.31
  1361.5 136.9 reduce-scatter.17
  1505.4 110.2 reduce-scatter.27
  1618.4 182.1 reduce-scatter.19
  1803.3 184.4 reduce-scatter.21
  1994.3 156.9 reduce-scatter.15
  2159.4 347.8 reduce-scatter.23
  2514.1 347.5 reduce-scatter.25
where the time goes:
time: 2880 us; the launch traced here: 2870 us
  waiting for transfers between devices  1710 us (59%)
  other arithmetic  474 us (16%)
  matrix products  451 us (16%)
  blocking collectives  163 us (6%)
  local copies, waits for them, and re-layouts  55.8 us (2%)
    reduce_scatter x1, waiting for transfers between devices, shards(): lax.psum_scatter(d_expand, 'fsdp', scatter_dimension=0, tiled=True)  356 us
    reduce_scatter x1, waiting for transfers between devices, shards(): lax.psum_scatter(d_shrink, 'fsdp', scatter_dimension=0, tiled=True)  354 us
    reduce_scatter x1, waiting for transfers between devices, shards(): lax.psum_scatter(d_down, 'fsdp', scatter_dimension=0, tiled=True)  187 us
    reduce_scatter x1, waiting for transfers between devices, shards(): lax.psum_scatter(d_up, 'fsdp', scatter_dimension=0, tiled=True)  185 us
    reduce_scatter x1, waiting for transfers between devices, shards(): lax.psum_scatter(d_qkv, 'fsdp', scatter_dimension=0, tiled=True)  163 us
    add x1, other arithmetic, shards(): grad_hires_in = grad_hires_out + grad_through  140 us
    reduce_sum x5, other arithmetic, depthwise_back(): tap_grads.append(jnp.sum(window * grad_out, axis=(0, 1, 2)))  140 us
    dot_general x9, matrix products, dense(): jnp.einsum('...i,ij->...j', operand, weight, preferred_element_type=jnp.f...  132 us
  transfers between devices with their start and end apart: 20, of which 12 were waited for; matrix products, arithmetic and copies ran while one was open for 33% of the time, Pallas kernels for 0%

commit v1 on v0

v1 whole, which is shorter than its diff:
```python
import functools
import math

import jax
import jax.numpy as jnp
from jax import lax
from jax.experimental import pallas as pl
from jax.experimental.pallas import tpu as pltpu
from jax.sharding import PartitionSpec as P

D = 1024
HEAD_DIM = 64
C = 1536
KS = 7
KA = 3
GRID_LR = 24
GRID_HR = 32
LANES = 128
GROUP = 8
NN = ((1,), (0,))
NT = ((1,), (1,))
TN = ((0,), (0,))
BF16 = jnp.bfloat16
F32 = jnp.float32


def dot(left, right, dims):
    return lax.dot_general(left, right, (dims, ((), ())), preferred_element_type=F32)


def kernel_limits(mebibytes):
    return pltpu.CompilerParams(vmem_limit_bytes=mebibytes * 2**20)


def estimate(flops, moved):
    return pl.CostEstimate(flops=flops, bytes_accessed=moved, transcendentals=0)


def norm_rows(values, epsilon):
    average = jnp.mean(values, axis=-1, keepdims=True)
    centred = values - average
    spread = jnp.mean(centred * centred, axis=-1, keepdims=True)
    inverse = lax.rsqrt(spread + epsilon)
    return (centred * inverse, inverse)


def norm_back(grad_normed, normed, inverse):
    first_mean = jnp.mean(grad_normed, axis=-1, keepdims=True)
    second_mean = jnp.mean(grad_normed * normed, axis=-1, keepdims=True)
    return inverse * (grad_normed - first_mean - normed * second_mean)


def gelu_pair(values):
    cdf = 0.5 * (1.0 + lax.erf(values * (1.0 / math.sqrt(2.0))))
    density = jnp.exp(-0.5 * values * values) * (1.0 / math.sqrt(2.0 * math.pi))
    return (values * cdf, cdf + values * density)


def pool_table(fine_cells, coarse_cells):
    coarse_index = jnp.arange(coarse_cells, dtype=jnp.int32)[:, None]
    fine_index = jnp.arange(fine_cells, dtype=jnp.int32)[None, :]
    window_start = coarse_index * fine_cells // coarse_cells
    window_end = ((coarse_index + 1) * fine_cells + coarse_cells - 1) // coarse_cells
    inside = ((fine_index >= window_start) & (fine_index < window_end)).astype(jnp.float32)
    return inside / jnp.sum(inside, axis=1, keepdims=True)


def fill_shifted(shifted, field, width, edge):
    reach = width // 2
    cells, lanes = field.shape
    column = lax.broadcasted_iota(jnp.int32, (cells, lanes), 0) % edge
    for step in range(width):
        offset = step - reach
        moved = field
        if offset != 0:
            moved = pltpu.roll(field, (-offset) % cells, 0)
            inside = (column + offset >= 0) & (column + offset < edge)
            moved = jnp.where(inside, moved, 0.0)
        shifted[step, reach : reach + edge] = moved.reshape(edge, edge, lanes)


def clear_edges(shifted, width, edge):
    reach = width // 2
    border = jnp.zeros((width, reach) + shifted.shape[2:], F32)
    shifted[:, 0:reach] = border
    shifted[:, reach + edge :] = border


def depthwise_kernel(width, edge, field_ref, taps_ref, out_ref, shifted, wide):
    @pl.when(pl.program_id(0) == 0)
    def _():
        clear_edges(shifted, width, edge)

    fill_shifted(shifted, field_ref[...].astype(F32), width, edge)
    wide[...] = jnp.broadcast_to(taps_ref[...].astype(F32)[:, None, :], wide.shape)
    strips = edge // 8

    def body(index, carry):
        base = (index // strips) * GROUP
        column = pl.multiple_of((index % strips) * 8, 8)
        sums = [jnp.zeros((8, LANES), F32)] * GROUP
        for step in range(width):
            taps = [wide[tap * width + step] for tap in range(width)]
            for row in range(GROUP + width - 1):
                value = shifted[step, base + row, pl.ds(column, 8), :]
                for place in range(GROUP):
                    if 0 <= row - place < width:
                        sums[place] = sums[place] + value * taps[row - place]
        for place in range(GROUP):
            start = pl.multiple_of((base + place) * edge + column, 8)
            out_ref[pl.ds(start, 8), :] = sums[place]
        return carry

    lax.fori_loop(0, (edge // GROUP) * strips, body, 0)


def depthwise(field, taps, width, edge):
    cells, channels = field.shape
    return pl.pallas_call(
        functools.partial(depthwise_kernel, width, edge),
        grid=(channels // LANES,),
        in_specs=[
            pl.BlockSpec((cells, LANES), lambda i: (0, i)),
            pl.BlockSpec((width * width, LANES), lambda i: (0, i)),
        ],
        out_specs=pl.BlockSpec((cells, LANES), lambda i: (0, i)),
        out_shape=jax.ShapeDtypeStruct((cells, channels), F32),
        scratch_shapes=[
            pltpu.VMEM((width, edge + width - 1, edge, LANES), F32),
            pltpu.VMEM((width * width, 8, LANES), F32),
        ],
        compiler_params=kernel_limits(32),
        cost_estimate=estimate(600 * width * width * cells * channels, 8 * cells * channels),
        name="depthwise",
    )(field, taps)


def depthwise_back_kernel(
    width, edge, grad_ref, field_ref, base_ref, taps_ref, out_ref, tap_out_ref, shifted, wide, cells_ref, sums_ref
):
    @pl.when(pl.program_id(0) == 0)
    def _():
        clear_edges(shifted, width, edge)

    fill_shifted(shifted, grad_ref[...], width, edge)
    cells_ref[...] = field_ref[...].astype(F32)
    sums_ref[...] = base_ref[...]
    wide[...] = jnp.broadcast_to(taps_ref[...].astype(F32)[:, None, :], wide.shape)
    strips = edge // 8
    last = width - 1

    for step in range(width):
        taps = [wide[(last - tap) * width + (last - step)] for tap in range(width)]

        def body(index, tap_sums):
            tap_sums = list(tap_sums)
            base = (index // strips) * GROUP
            column = pl.multiple_of((index % strips) * 8, 8)
            spots = [
                pl.ds(pl.multiple_of((base + place) * edge + column, 8), 8)
                for place in range(GROUP)
            ]
            sums = [sums_ref[spot, :] for spot in spots]
            cells = [cells_ref[spot, :] for spot in spots]
            for row in range(GROUP + width - 1):
                value = shifted[step, base + row, pl.ds(column, 8), :]
                for place in range(GROUP):
                    tap = row - place
                    if 0 <= tap < width:
                        sums[place] = sums[place] + value * taps[tap]
                        tap_sums[tap] = tap_sums[tap] + value * cells[place]
            for place in range(GROUP):
                sums_ref[spots[place], :] = sums[place]
            return tuple(tap_sums)

        tap_sums = lax.fori_loop(
            0, (edge // GROUP) * strips, body, (jnp.zeros((8, LANES), F32),) * width
        )
        for tap in range(width):
            spot = (last - tap) * width + (last - step)
            tap_out_ref[spot : spot + 1, :] = jnp.sum(tap_sums[tap], axis=0, keepdims=True)
    out_ref[...] = sums_ref[...].astype(out_ref.dtype)


def depthwise_back(grad, field, base, taps, width, edge, out_type):
    cells, channels = field.shape
    full = pl.BlockSpec((cells, LANES), lambda i: (0, i))
    small = pl.BlockSpec((width * width, LANES), lambda i: (0, i))
    return pl.pallas_call(
        functools.partial(depthwise_back_kernel, width, edge),
        grid=(channels // LANES,),
        in_specs=[full, full, full, small],
        out_specs=[full, small],
        out_shape=[
            jax.ShapeDtypeStruct((cells, channels), out_type),
            jax.ShapeDtypeStruct((width * width, channels), F32),
        ],
        scratch_shapes=[
            pltpu.VMEM((width, edge + width - 1, edge, LANES), F32),
            pltpu.VMEM((width * width, 8, LANES), F32),
            pltpu.VMEM((cells, LANES), F32),
            pltpu.VMEM((cells, LANES), F32),
        ],
        compiler_params=kernel_limits(32),
        cost_estimate=estimate(1200 * width * width * cells * channels, 14 * cells * channels),
        name="depthwise_back",
    )(grad, field, base, taps)


def softmax_rows(query, key):
    scores = dot(query, key, NT) * HEAD_DIM ** (-0.5)
    raised = jnp.exp(scores - jnp.max(scores, axis=-1, keepdims=True))
    return raised * (1.0 / jnp.sum(raised, axis=-1, keepdims=True))


def attend_kernel(q_ref, k_ref, v_ref, out_ref):
    outs = []
    for head in range(out_ref.shape[1] // HEAD_DIM):
        lanes = slice(head * HEAD_DIM, (head + 1) * HEAD_DIM)
        probs = softmax_rows(q_ref[:, lanes], k_ref[:, lanes]).astype(BF16)
        outs.append(dot(probs, v_ref[:, lanes], NN))
    out_ref[...] = jnp.concatenate(outs, axis=1).astype(BF16)


def attend(qkv, width=256):
    rows = qkv.shape[0]
    steps = D // width

    def spec(part):
        return pl.BlockSpec((rows, width), lambda i: (0, i + part * steps))

    return pl.pallas_call(
        attend_kernel,
        grid=(steps,),
        in_specs=[spec(0), spec(1), spec(2)],
        out_specs=spec(0),
        out_shape=jax.ShapeDtypeStruct((rows, D), BF16),
        compiler_params=kernel_limits(48),
        cost_estimate=estimate(40 * rows * rows * D, 8 * rows * D),
        name="attend",
    )(qkv, qkv, qkv)


def attend_back_kernel(q_ref, k_ref, v_ref, g_ref, dq_ref, dk_ref, dv_ref):
    scale = HEAD_DIM ** (-0.5)
    dqs, dks, dvs = ([], [], [])
    for head in range(dq_ref.shape[1] // HEAD_DIM):
        lanes = slice(head * HEAD_DIM, (head + 1) * HEAD_DIM)
        query, key, value, grad = (q_ref[:, lanes], k_ref[:, lanes], v_ref[:, lanes], g_ref[:, lanes])
        probs = softmax_rows(query, key)
        grad_probs = dot(grad, value, NT)
        dvs.append(dot(probs.astype(BF16), grad, TN))
        total = jnp.sum(probs * grad_probs, axis=-1, keepdims=True)
        low = (probs * (grad_probs - total)).astype(BF16)
        dqs.append(dot(low, key, NN) * scale)
        dks.append(dot(low, query, TN) * scale)
    dq_ref[...] = jnp.concatenate(dqs, axis=1).astype(BF16)
    dk_ref[...] = jnp.concatenate(dks, axis=1).astype(BF16)
    dv_ref[...] = jnp.concatenate(dvs, axis=1).astype(BF16)


def attend_back(qkv, grad, width=256):
    rows = qkv.shape[0]
    steps = D // width

    def spec(part):
        return pl.BlockSpec((rows, width), lambda i: (0, i + part * steps))

    return pl.pallas_call(
        attend_back_kernel,
        grid=(steps,),
        in_specs=[spec(0), spec(1), spec(2), spec(0)],
        out_specs=[spec(0)] * 3,
        out_shape=[jax.ShapeDtypeStruct((rows, D), BF16)] * 3,
        compiler_params=kernel_limits(48),
        cost_estimate=estimate(70 * rows * rows * D, 14 * rows * D),
        name="attend_back",
    )(qkv, qkv, qkv, grad)


def mlp_both_kernel(g_ref, h_ref, wi_ref, wo_ref, out_ref, dh_ref, dwi_ref, dwo_ref):
    @pl.when(pl.program_id(0) == 0)
    def _():
        out_ref[...] = jnp.zeros_like(out_ref)
        dh_ref[...] = jnp.zeros_like(dh_ref)

    hidden = dot(h_ref[...], wi_ref[...], NN)
    back = dot(g_ref[...], wo_ref[...], NT)
    act, slope = gelu_pair(hidden)
    act = act.astype(BF16)
    out_ref[...] += dot(act, wo_ref[...], NN)
    low = (back * slope).astype(BF16)
    dh_ref[...] += dot(low, wi_ref[...], NT)
    dwi_ref[...] = dot(h_ref[...], low, TN).astype(BF16)
    dwo_ref[...] = dot(act, g_ref[...], TN).astype(BF16)


def mlp_both(grad, field, w_in, w_out, tile):
    rows, wide = field.shape
    hidden = w_out.shape[0]
    whole = pl.BlockSpec((rows, wide), lambda i: (0, 0))
    columns = pl.BlockSpec((wide, tile), lambda i: (0, i))
    lines = pl.BlockSpec((tile, wide), lambda i: (i, 0))
    return pl.pallas_call(
        mlp_both_kernel,
        grid=(hidden // tile,),
        in_specs=[whole, whole, columns, lines],
        out_specs=[whole, whole, columns, lines],
        out_shape=[
            jax.ShapeDtypeStruct((rows, wide), F32),
            jax.ShapeDtypeStruct((rows, wide), F32),
            jax.ShapeDtypeStruct((wide, hidden), BF16),
            jax.ShapeDtypeStruct((hidden, wide), BF16),
        ],
        compiler_params=kernel_limits(60),
        cost_estimate=estimate(12 * rows * wide * hidden, 8 * wide * hidden),
        name="mlp_both",
    )(grad, field, w_in, w_out)


def mlp_forward_kernel(rows, h_ref, wi_ref, wo_ref, act_ref, slope_ref, out_ref):
    @pl.when(pl.program_id(0) == 0)
    def _():
        out_ref[...] = jnp.zeros_like(out_ref)

    def body(index, carry):
        spot = pl.ds(pl.multiple_of(index * rows, rows), rows)
        act, slope = gelu_pair(dot(h_ref[spot, :], wi_ref[...], NN))
        act = act.astype(BF16)
        act_ref[spot, :] = act
        slope_ref[spot, :] = slope.astype(BF16)
        out_ref[spot, :] += dot(act, wo_ref[...], NN)
        return carry

    lax.fori_loop(0, h_ref.shape[0] // rows, body, 0)


def mlp_forward(field, w_in, w_out, tile, step):
    rows, wide = field.shape
    hidden = w_out.shape[0]
    whole = pl.BlockSpec((rows, wide), lambda i: (0, 0))
    tiles = pl.BlockSpec((rows, tile), lambda i: (0, i))
    return pl.pallas_call(
        functools.partial(mlp_forward_kernel, step),
        grid=(hidden // tile,),
        in_specs=[
            whole,
            pl.BlockSpec((wide, tile), lambda i: (0, i)),
            pl.BlockSpec((tile, wide), lambda i: (i, 0)),
        ],
        out_specs=[tiles, tiles, whole],
        out_shape=[
            jax.ShapeDtypeStruct((rows, hidden), BF16),
            jax.ShapeDtypeStruct((rows, hidden), BF16),
            jax.ShapeDtypeStruct((rows, wide), F32),
        ],
        compiler_params=kernel_limits(60),
        cost_estimate=estimate(6 * rows * wide * hidden, 4 * wide * hidden + 4 * rows * hidden),
        name="mlp_forward",
    )(field, w_in, w_out)


def outer_kernel(left_ref, right_ref, out_ref):
    out_ref[...] = dot(left_ref[...], right_ref[...], TN).astype(BF16)


def outer_sum(left, right, tile):
    rows, lines = left.shape
    columns = right.shape[1]
    return pl.pallas_call(
        outer_kernel,
        grid=(lines // tile,),
        in_specs=[
            pl.BlockSpec((rows, tile), lambda i: (0, i)),
            pl.BlockSpec((rows, columns), lambda i: (0, 0)),
        ],
        out_specs=pl.BlockSpec((tile, columns), lambda i: (i, 0)),
        out_shape=jax.ShapeDtypeStruct((lines, columns), BF16),
        compiler_params=kernel_limits(48),
        cost_estimate=estimate(3 * rows * lines * columns, 2 * lines * columns),
        name="outer_sum",
    )(left, right)


def mlp_back_kernel(step, g_ref, h_ref, slope_ref, wi_ref, wo_ref, start_ref, dh_ref, dwi_ref, low_ref):
    @pl.when(pl.program_id(0) == 0)
    def _():
        dh_ref[...] = start_ref[...]

    def body(index, carry):
        spot = pl.ds(pl.multiple_of(index * step, step), step)
        back = dot(g_ref[spot, :], wo_ref[...], NT)
        low = (back * slope_ref[spot, :].astype(F32)).astype(BF16)
        low_ref[spot, :] = low
        dh_ref[spot, :] += dot(low, wi_ref[...], NT)
        return carry

    lax.fori_loop(0, h_ref.shape[0] // step, body, 0)
    block = 256

    def outer(index, carry):
        spot = pl.ds(pl.multiple_of(index * block, block), block)
        dwi_ref[spot, :] = dot(h_ref[:, spot], low_ref[...], TN).astype(BF16)
        return carry

    lax.fori_loop(0, dwi_ref.shape[0] // block, outer, 0)


def mlp_back(grad, field, slope, w_in, w_out, start, tile, step, first, last):
    rows, wide = field.shape
    whole = pl.BlockSpec((rows, wide), lambda i: (0, 0))
    return pl.pallas_call(
        functools.partial(mlp_back_kernel, step),
        grid=(last - first,),
        in_specs=[
            whole,
            whole,
            pl.BlockSpec((rows, tile), lambda i: (0, i + first)),
            pl.BlockSpec((wide, tile), lambda i: (0, i + first)),
            pl.BlockSpec((tile, wide), lambda i: (i + first, 0)),
            whole,
        ],
        out_specs=[whole, pl.BlockSpec((wide, tile), lambda i: (0, i))],
        out_shape=[
            jax.ShapeDtypeStruct((rows, wide), F32),
            jax.ShapeDtypeStruct((wide, (last - first) * tile), BF16),
        ],
        scratch_shapes=[pltpu.VMEM((rows, tile), BF16)],
        compiler_params=kernel_limits(60),
        cost_estimate=estimate(
            7 * rows * wide * tile * (last - first), 6 * wide * tile * (last - first)
        ),
        name="mlp_back",
    )(grad, field, slope, w_in, w_out, start)


def gate_kernel(
    mixed_ref, resid_ref, gv_ref, live_ref, wi_ref, wo_ref, joined_ref, dmix_ref, dwi_ref, dwo_ref
):
    live = live_ref[0].astype(F32)
    mixed = mixed_ref[...]
    mixed_low = mixed.astype(BF16)
    act, slope = gelu_pair(dot(mixed_low, wi_ref[...], NN))
    act = act.astype(BF16)
    gate = jnp.tanh(dot(act, wo_ref[...], NN))
    joined_ref[...] = (live * (resid_ref[...] + gate * mixed)).astype(BF16)
    grad = live * gv_ref[...].astype(F32)
    logit = (grad * mixed * (1.0 - gate * gate)).astype(BF16)
    dwo_ref[...] = dot(act, logit, TN).astype(BF16)
    low = (dot(logit, wo_ref[...], NT) * slope).astype(BF16)
    dwi_ref[...] = dot(mixed_low, low, TN).astype(BF16)
    dmix_ref[...] = grad * gate + dot(low, wi_ref[...], NT)


def gate_both(mixed, resid, grad, live, w_in, w_out):
    rows, wide = mixed.shape
    place = pl.BlockSpec(memory_space=pltpu.VMEM)
    return pl.pallas_call(
        gate_kernel,
        in_specs=[place, place, place, pl.BlockSpec(memory_space=pltpu.SMEM), place, place],
        out_specs=[place] * 4,
        out_shape=[
            jax.ShapeDtypeStruct((rows, wide), BF16),
            jax.ShapeDtypeStruct((rows, wide), F32),
            jax.ShapeDtypeStruct(w_in.shape, BF16),
            jax.ShapeDtypeStruct(w_out.shape, BF16),
        ],
        compiler_params=kernel_limits(60),
        cost_estimate=estimate(20 * rows * wide * w_in.shape[1], 30 * rows * wide),
        name="gate_both",
    )(mixed, resid, grad, live, w_in, w_out)


def bit_pairs(devices, bit):
    return [(index, index ^ (1 << bit)) for index in range(devices)]


def own_bit(bit):
    return (lax.axis_index("fsdp") >> bit) & 1


def gather_small(block, devices):
    gathered = block[None]
    for bit in range(devices.bit_length() - 1):
        other = lax.ppermute(gathered, "fsdp", bit_pairs(devices, bit))
        high = own_bit(bit) == 1
        gathered = jnp.where(
            high,
            jnp.concatenate((other, gathered), axis=0),
            jnp.concatenate((gathered, other), axis=0),
        )
    return gathered


def scatter_sum(partial, bit_order, devices, link_type=jnp.bfloat16):
    bits = devices.bit_length() - 1
    rest = partial.shape[1:]
    field = partial.astype(link_type).reshape((2,) * bits + rest)
    held = list(range(bits - 1, -1, -1))
    for bit in bit_order:
        axis = held.index(bit)
        mine = own_bit(bit)
        sent = lax.dynamic_index_in_dim(field, 1 - mine, axis, keepdims=False)
        kept = lax.dynamic_index_in_dim(field, mine, axis, keepdims=False)
        arrived = lax.ppermute(sent, "fsdp", bit_pairs(devices, bit))
        total = kept.astype(jnp.float32) + arrived.astype(jnp.float32)
        held.pop(axis)
        field = total.astype(link_type) if held else total
    return field


def scatter_orders(devices):
    bits = devices.bit_length() - 1
    if bits == 5:
        x_bits, y_bits, z_bits = (1,), (2,), (3, 4)
    else:
        span = (bits - 1 + 2) // 3
        places = tuple(range(1, bits))
        x_bits, y_bits, z_bits = places[:span], places[span : 2 * span], places[2 * span :]
    return (
        (0,) + y_bits + z_bits + x_bits,
        (0,) + x_bits + z_bits + y_bits,
        (0,) + y_bits + x_bits + z_bits,
        (0,) + x_bits + y_bits + z_bits,
    )


def scatter_weight(gradient, devices, turn):
    orders = scatter_orders(devices)
    rows, columns = gradient.shape
    split = gradient.astype(jnp.bfloat16).reshape(devices, rows // devices, columns)
    third = columns // 3 // 128 * 128
    cuts = (0, third, 2 * third, columns)
    chosen = (orders[0], orders[1], orders[2 + turn % 2])
    parts = [
        scatter_sum(split[:, :, cuts[place] : cuts[place + 1]], chosen[place], devices)
        for place in range(3)
    ]
    return jnp.concatenate(parts, axis=-1)


def after(value, *earlier):
    return lax.optimization_barrier((value,) + earlier)[0]


def shards(
    x_vit,
    x_hires,
    image_live,
    grad_vit,
    grad_hires,
    gain_one,
    w_qkv,
    w_out,
    gain_two,
    w_up,
    w_down,
    conv_seven,
    gain_three,
    w_expand,
    w_shrink,
    layer_scale,
    w_adapt,
    conv_three,
    w_gate_in,
    w_gate_out,
):
    devices = lax.axis_size("fsdp")
    edge_c, edge_d = (gain_three.shape[0], gain_one.shape[0])
    small = jnp.concatenate(
        (
            conv_seven.reshape(-1),
            gain_three,
            layer_scale,
            conv_three.reshape(-1),
            gain_one,
            gain_two,
        )
    )
    small_all = gather_small(small, devices)
    marks = [0]
    for length in (KS * KS * edge_c, edge_c, edge_c, KA * KA * edge_d, edge_d, edge_d):
        marks.append(marks[-1] + length)
    small_parts = [small_all[:, marks[place] : marks[place + 1]] for place in range(6)]
    seven_taps = small_parts[0].reshape(devices, KS * KS, edge_c).swapaxes(0, 1).reshape(KS * KS, C)
    three_taps = small_parts[3].reshape(devices, KA * KA, edge_d).swapaxes(0, 1).reshape(KA * KA, D)
    gain_c, scale_c = (small_parts[1].reshape(C).astype(F32), small_parts[2].reshape(C).astype(F32))
    gain_a, gain_b = (small_parts[4].reshape(D).astype(F32), small_parts[5].reshape(D).astype(F32))

    def gathered(block):
        return lax.all_gather(block, "fsdp", axis=0, tiled=True)

    vit_all = gathered(jnp.concatenate((w_qkv, w_out, w_gate_in, w_gate_out), axis=1))
    qkv_all = vit_all[:, : 3 * D]
    out_all = vit_all[:, 3 * D : 4 * D]
    gate_in_all = vit_all[:, 4 * D : 5 * D]
    gate_out_all = vit_all[:, 5 * D :]
    up_all = gathered(w_up)
    down_all = gathered(w_down)
    expand_all = gathered(jnp.concatenate((w_expand, w_adapt), axis=1))
    adapt_all = expand_all[:, w_expand.shape[1] :]
    shrink_all = gathered(w_shrink)

    live = image_live.astype(F32)
    grad_joined_low = (grad_vit.astype(F32) * live).astype(BF16)

    patch_in = x_vit.astype(F32)
    normed_a, inverse_a = norm_rows(patch_in, 1e-05)
    normed_a_low = (normed_a * gain_a).astype(BF16)
    qkv_low = dot(normed_a_low, qkv_all, NN).astype(BF16)
    attended_low = attend(qkv_low)
    resid_one = patch_in + dot(attended_low, out_all, NN)
    normed_b, inverse_b = norm_rows(resid_one, 1e-05)
    normed_b_low = (normed_b * gain_b).astype(BF16)
    mlp_out, grad_b, d_up, d_down = mlp_both(grad_joined_low, normed_b_low, up_all, down_all, 1024)
    resid_two = resid_one + mlp_out
    d_gain_two = jnp.sum(grad_b * normed_b, axis=0)
    grad_first = grad_joined_low.astype(F32) + norm_back(grad_b * gain_b, normed_b, inverse_b)
    grad_first_low = grad_first.astype(BF16)
    d_out = dot(attended_low, grad_first_low, TN).astype(BF16)
    grad_att_low = dot(grad_first_low, out_all, NT).astype(BF16)
    grad_qkv_low = jnp.concatenate(attend_back(qkv_low, grad_att_low), axis=1)
    d_qkv = dot(normed_a_low, grad_qkv_low, TN).astype(BF16)
    grad_a = dot(grad_qkv_low, qkv_all, NT)
    d_gain_one = jnp.sum(grad_a * normed_a, axis=0)
    grad_patches = grad_first + norm_back(grad_a * gain_a, normed_a, inverse_a)

    conved = depthwise(x_hires, seven_taps, KS, GRID_HR)
    normed_c, inverse_c = norm_rows(conved, 1e-06)
    normed_c_low = (normed_c * gain_c).astype(BF16)
    activated, slope, shrunk = mlp_forward(normed_c_low, expand_all, shrink_all, 1024, 256)
    hires_out = x_hires.astype(F32) + scale_c * shrunk
    hires_next = (live * hires_out).astype(BF16)

    table = pool_table(GRID_HR, GRID_LR)
    pool = jnp.einsum("ia,jb->ijab", table, table).reshape(GRID_LR**2, GRID_HR**2).astype(BF16)
    pooled_low = dot(pool, hires_out.astype(BF16), NN).astype(BF16)
    adapted = dot(pooled_low, adapt_all, NN)
    mixed = depthwise(adapted, three_taps, KA, GRID_LR)
    joined, grad_mixed, d_gate_in, d_gate_out = gate_both(
        mixed, resid_two, grad_vit, image_live, gate_in_all, gate_out_all
    )
    grad_adapted_low, d_conv_three = depthwise_back(
        grad_mixed, adapted, jnp.zeros_like(adapted), three_taps, KA, GRID_LR, BF16
    )
    d_adapt = dot(pooled_low, grad_adapted_low, TN).astype(BF16)
    grad_pooled_low = dot(grad_adapted_low, adapt_all, NT).astype(BF16)
    grad_hires_out = live * grad_hires.astype(F32) + dot(pool, grad_pooled_low, TN)

    d_layer_scale = jnp.sum(grad_hires_out * shrunk, axis=0)
    grad_shrunk_low = (grad_hires_out * scale_c).astype(BF16)
    d_shrink = outer_sum(activated, grad_shrunk_low, 512)
    tile = 1024
    tiles = activated.shape[1] // tile
    grad_c, d_expand = mlp_back(
        grad_shrunk_low,
        normed_c_low,
        slope,
        expand_all,
        shrink_all,
        jnp.zeros((x_hires.shape[0], C), F32),
        tile,
        256,
        0,
        tiles,
    )
    d_gain_three = jnp.sum(grad_c * normed_c, axis=0)
    grad_conved = norm_back(grad_c * gain_c, normed_c, inverse_c)
    grad_hires_in, d_conv_seven = depthwise_back(
        grad_conved, x_hires, grad_hires_out, seven_taps, KS, GRID_HR, F32
    )

    def shares(gradient):
        return gradient.reshape(devices, gradient.shape[0] // devices, gradient.shape[1])

    g_down = scatter_weight(d_down, devices, 0)
    g_up = scatter_weight(d_up, devices, 1)
    g_square = scatter_weight(
        jnp.concatenate((shares(d_out), shares(d_gate_in), shares(d_gate_out), shares(d_adapt)), axis=1).reshape(-1, D),
        devices,
        0,
    )
    g_qkv = scatter_weight(d_qkv, devices, 1)
    g_shrink = scatter_weight(d_shrink, devices, 0)
    g_expand = scatter_weight(d_expand, devices, 1)
    small_grads = jnp.concatenate(
        (
            d_conv_seven.reshape(KS * KS, devices, edge_c).swapaxes(0, 1).reshape(devices, -1),
            d_gain_three.reshape(devices, edge_c),
            d_layer_scale.reshape(devices, edge_c),
            d_conv_three.reshape(KA * KA, devices, edge_d).swapaxes(0, 1).reshape(devices, -1),
            d_gain_one.reshape(devices, edge_d),
            d_gain_two.reshape(devices, edge_d),
        ),
        axis=1,
    )
    small_sums = scatter_sum(small_grads, scatter_orders(devices)[0], devices, F32)
    small_outs = [small_sums[marks[place] : marks[place + 1]] for place in range(6)]
    return (
        joined,
        hires_next,
        grad_patches,
        grad_hires_in,
        small_outs[4],
        g_qkv,
        g_square[:edge_d],
        small_outs[5],
        g_up,
        g_down,
        small_outs[0].reshape(KS * KS, edge_c),
        small_outs[1],
        g_expand,
        g_shrink,
        small_outs[2],
        g_square[3 * edge_d :],
        small_outs[3].reshape(KA * KA, edge_d),
        g_square[edge_d : 2 * edge_d],
        g_square[2 * edge_d : 3 * edge_d],
    )


def solution(mesh):
    in_specs = (
        P("fsdp", None),
        P("fsdp", None),
        P("fsdp"),
        P("fsdp", None),
        P("fsdp", None),
        P("fsdp"),
        P("fsdp", None),
        P("fsdp", None),
        P("fsdp"),
        P("fsdp", None),
        P("fsdp", None),
        P(None, "fsdp"),
        P("fsdp"),
        P("fsdp", None),
        P("fsdp", None),
        P("fsdp"),
        P("fsdp", None),
        P(None, "fsdp"),
        P("fsdp", None),
        P("fsdp", None),
    )
    out_specs = (
        P("fsdp", None),
        P("fsdp", None),
        P("fsdp", None),
        P("fsdp", None),
        P("fsdp"),
        P("fsdp", None),
        P("fsdp", None),
        P("fsdp"),
        P("fsdp", None),
        P("fsdp", None),
        P(None, "fsdp"),
        P("fsdp"),
        P("fsdp", None),
        P("fsdp", None),
        P("fsdp"),
        P("fsdp", None),
        P(None, "fsdp"),
        P("fsdp", None),
        P("fsdp", None),
    )
    return jax.shard_map(shards, mesh=mesh, in_specs=in_specs, out_specs=out_specs, check_vma=False)
```

time: 2880 us -> 1350 us (0.47)
  waiting for transfers between devices: 1710 us -> 532 us
  matrix products: 451 us -> 60.1 us
  Pallas kernels: 0 us -> 386 us
  other arithmetic: 474 us -> 107 us
  blocking collectives: 163 us -> 0 us
  starting transfers between devices: 1.59 us -> 108 us
  local copies, waits for them, and re-layouts: 55.8 us -> 130 us
    reduce_scatter x9 -> x0, waiting for transfers between devices: 1470 us -> none  [the longest x1 356 us: shards(): lax.psum_scatter(d_expand, 'fsdp', scatter_dimension=0, tiled=True)]
    ppermute x0 -> x100, waiting for transfers between devices: none -> 396 us  [the longest x95 390 us: scatter_sum(): arrived = lax.ppermute(sent, 'fsdp', bit_pairs(devices, bit))]
    dot_general x37 -> x10, matrix products: 451 us -> 60.1 us  [dot(): lax.dot_general(left, right, (dims, ((), ())), preferred_element_type=F32)]
    pallas_call x0 -> x11, Pallas kernels: none -> 386 us  [the longest x2 85.4 us: depthwise_back(): pl.pallas_call(functools.partial(depthwise_back_kernel, width, edge), gri...]
    reduce_sum x8 -> x2, other arithmetic: 156 us -> 9.16 us  [the longest x1 5.86 us: shards(): d_gain_three = jnp.sum(grad_c * normed_c, axis=0)]
    add x3 -> x25, other arithmetic: 145 us -> 7.86 us  [the longest x1 4.89 us: shards(): grad_joined_low.astype(F32)]
    ppermute x0 -> x100, starting transfers between devices: none -> 108 us  [the longest x95 97.9 us: scatter_sum(): arrived = lax.ppermute(sent, 'fsdp', bit_pairs(devices, bit))]
    all_gather x9 -> x5, waiting for transfers between devices: 231 us -> 134 us  [gathered(): return lax.all_gather(block, 'fsdp', axis=0, tiled=True)]
  transfers between devices with their start and end apart: 20 -> 105, of which waited for: 12 -> 56; matrix products, arithmetic and copies ran while one was open for 33% -> 16% of each run, Pallas kernels for 0% -> 11%
where the time goes in v1:
time: 1350 us; the launch traced here: 1340 us
  waiting for transfers between devices  532 us (39%)
  Pallas kernels  386 us (29%)
  local copies, waits for them, and re-layouts  130 us (10%)
  starting transfers between devices  108 us (8%)
  other arithmetic  107 us (8%)
  matrix products  60.1 us (4%)
  between operations  17.1 us (1%)
    ppermute x95, waiting for transfers between devices, scatter_sum(): arrived = lax.ppermute(sent, 'fsdp', bit_pairs(devices, bit))  390 us
    all_gather x5, waiting for transfers between devices, gathered(): return lax.all_gather(block, 'fsdp', axis=0, tiled=True)  134 us
    ppermute x95, starting transfers between devices, scatter_sum(): arrived = lax.ppermute(sent, 'fsdp', bit_pairs(devices, bit))  97.9 us
    pallas_call x2, Pallas kernels, depthwise_back(): pl.pallas_call(functools.partial(depthwise_back_kernel, width, edge), gri...  85.4 us
    pallas_call x1, Pallas kernels, mlp_back(): pl.pallas_call(functools.partial(mlp_back_kernel, step), grid=(last - fir...  83.1 us
    dot_general x10, matrix products, dot(): lax.dot_general(left, right, (dims, ((), ())), preferred_element_type=F32)  60.1 us
    pallas_call x1, Pallas kernels, mlp_forward(): pl.pallas_call(functools.partial(mlp_forward_kernel, step), grid=(hidden...  55.1 us
    convert_element_type x72, other arithmetic, scatter_sum(): field = total.astype(link_type) if held else total  50.9 us
  transfers between devices with their start and end apart: 105, of which 56 were waited for; matrix products, arithmetic and copies ran while one was open for 16% of the time, Pallas kernels for 11%

profile of v1, /device:TPU:0, one launch (start us, length us, event | category | flops | bytes accessed | tf_op | source)
XLA Modules:
  0.0 1341.4 jit_solution(2729999011706088716)
XLA Ops:
  52.2 36.4 %depthwise.2 = f32[1024,1536]{1,0:T(8,128)S(1)} custom-call(bf16[1024,1536]{1,0:T(8,128)(2,1)S(1)} %copy-done.3, bf16[49,1536]{1,0:T(8,128)(2,1)S(1)} %reshape.494.taps_ref), custom_call_target="tpu_custom_call" | custom-call | flops 46242201600 | bytes 12582912 | tf_op jit(solution)/shard_map/depthwise/pallas_call | solution.py:119
  119.0 15.5 %attend.1 = bf16[576,1024]{1,0:T(8,128)(2,1)S(1)} custom-call(bf16[576,3072]{1,0:T(8,128)(2,1)S(1)} %fusion.12.q_ref.k_ref.v_ref, bf16[576,3072]{1,0:T(8,128)(2,1)S(1)} %fusion.12.q_ref.k_ref.v_ref, bf16[576,3072]{1,0:T(8,128)(2,1)S(1)} %fusion.12.q_ref.k_ref.v_ref), custom_call_target="tpu_custom_call" | custom-call | flops 13589544960 | bytes 4718592 | tf_op jit(solution)/shard_map/attend/pallas_call | solution.py:232
  142.0 48.6 %all-gather.12.cloned.1.call-done.wi_ref = bf16[1024,4096]{1,0:T(8,128)(2,1)} async-done(((bf16[32,4096]{1,0:T(8,128)(2,1)}), bf16[1024,4096]{1,0:T(8,128)(2,1)}) %all-gather.12.cloned.1.call-update) | async-done | bytes 8388624 | tf_op jit(solution)/shard_map/all_gather | solution.py:591
  190.6 78.9 %all-gather.14.cloned.1.call-done.wo_ref = bf16[4096,1024]{1,0:T(8,128)(2,1)} async-done(((bf16[128,1024]{1,0:T(8,128)(2,1)}), bf16[4096,1024]{1,0:T(8,128)(2,1)}) %all-gather.14.cloned.1.call-update) | async-done | bytes 8388624 | tf_op jit(solution)/shard_map/all_gather | solution.py:591
  269.5 38.4 %mlp_both.1 = (f32[576,1024]{1,0:T(8,128)}, f32[576,1024]{1,0:T(8,128)}, bf16[1024,4096]{1,0:T(8,128)(2,1)}, bf16[4096,1024]{1,0:T(8,128)(2,1)}) custom-call(bf16[576,1024]{1,0:T(8,128)(2,1)} %get-tuple-element.162.g_ref, bf16[576,1024]{1,0:T(8,128)(2,1)} %get-tuple-element.161.h_ref, bf16[1024,4096]{1,0:T(8,128)(2,1)} %all-gather.12.cloned.1.call-done.wi_ref, ...), custom_call_target="tpu_custom_call" | custom-call | flops 28991029248 | bytes 33554432 | tf_op jit(solution)/shard_map/mlp_both/pallas_call | solution.py:304
  320.8 27.7 %attend_back.1 = (bf16[576,1024]{1,0:T(8,128)(2,1)S(1)}, bf16[576,1024]{1,0:T(8,128)(2,1)S(1)}, bf16[576,1024]{1,0:T(8,128)(2,1)S(1)}) custom-call(bf16[576,3072]{1,0:T(8,128)(2,1)} %copy-done.13, bf16[576,3072]{1,0:T(8,128)(2,1)} %copy-done.13, bf16[576,3072]{1,0:T(8,128)(2,1)} %copy-done.13, bf16[576,1024]{1,0:T(8,128)(2,1)S(1)} %fusion.70.g_ref), custom_call_target="tpu_custom_call" | custom-call | flops 23781703680 | bytes 8257536 | tf_op jit(solution)/shard_map/attend_back/pallas_call | solution.py:269
  349.9 9.6 fusion.46
  413.0 10.9 collective-permute-done.16
  426.5 9.7 collective-permute-done.21
  439.1 19.5 %collective-permute-done.61 = bf16[2,2,2,128,256]{4,3,2,1,0:T(8,128)(2,1)S(1)} collective-permute-done((bf16[2,2,2,128,256]{4,3,2,1,0:T(8,128)(2,1)S(1)}, bf16[2,2,2,128,256]{4,3,2,1,0:T(8,128)(2,1)S(1)}, u32[]{:S(2)}, u32[]{:S(2)}) %collective-permute-start.61) | collective-permute-done | bytes 524320 | tf_op jit(solution)/shard_map/ppermute | solution.py:505
  475.0 9.7 collective-permute-start.51
  496.1 13.5 %collective-permute-done.13 = bf16[2,32,1024]{2,1,0:T(8,128)(2,1)S(1)} collective-permute-done((bf16[2,32,1024]{2,1,0:T(8,128)(2,1)S(1)}, bf16[2,32,1024]{2,1,0:T(8,128)(2,1)S(1)}, u32[]{:S(2)}, u32[]{:S(2)}) %collective-permute-start.13) | collective-permute-done | bytes 131104 | tf_op jit(solution)/shard_map/ppermute | solution.py:505
  511.3 14.1 %collective-permute-done.23 = bf16[2,32,1024]{2,1,0:T(8,128)(2,1)S(1)} collective-permute-done((bf16[2,32,1024]{2,1,0:T(8,128)(2,1)S(1)}, bf16[2,32,1024]{2,1,0:T(8,128)(2,1)S(1)}, u32[]{:S(2)}, u32[]{:S(2)}) %collective-permute-start.23) | collective-permute-done | bytes 131104 | tf_op jit(solution)/shard_map/ppermute | solution.py:505
  527.5 16.0 %collective-permute-done.58 = bf16[2,128,256]{2,1,0:T(8,128)(2,1)S(1)} collective-permute-done((bf16[2,128,256]{2,1,0:T(8,128)(2,1)S(1)}, bf16[2,128,256]{2,1,0:T(8,128)(2,1)S(1)}, u32[]{:S(2)}, u32[]{:S(2)}) %collective-permute-start.58) | collective-permute-done | bytes 131104 | tf_op jit(solution)/shard_map/ppermute | solution.py:505
  543.6 17.3 %collective-permute-done.63 = bf16[2,128,256]{2,1,0:T(8,128)(2,1)S(1)} collective-permute-done((bf16[2,128,256]{2,1,0:T(8,128)(2,1)S(1)}, bf16[2,128,256]{2,1,0:T(8,128)(2,1)S(1)}, u32[]{:S(2)}, u32[]{:S(2)}) %collective-permute-start.63) | collective-permute-done | bytes 131104 | tf_op jit(solution)/shard_map/ppermute | solution.py:505
  636.5 55.1 %mlp_forward.1 = (bf16[1024,6144]{1,0:T(8,128)(2,1)}, bf16[1024,6144]{1,0:T(8,128)(2,1)}, f32[1024,1536]{1,0:T(8,128)}) custom-call(bf16[1024,1536]{1,0:T(8,128)(2,1)} %multiply_convert_fusion.3.h_ref, bf16[1536,7168]{1,0:T(8,128)(2,1)} %all-gather.6.cloned.1.call-done.wi_ref, bf16[6144,1536]{1,0:T(8,128)(2,1)} %all-gather.8.cloned.1.call-done.wo_ref), custom_call_target="tpu_custom_call" | custom-call | flops 57982058496 | bytes 62914560 | tf_op jit(solution)/shard_map/mlp_forward/pallas_call | solution.py:343
  709.2 14.4 %gate_both.1 = (bf16[576,1024]{1,0:T(8,128)(2,1)}, f32[576,1024]{1,0:T(8,128)}, bf16[1024,1024]{1,0:T(8,128)(2,1)}, bf16[1024,1024]{1,0:T(8,128)(2,1)}) custom-call(f32[576,1024]{1,0:T(8,128)} %copy-done.12, f32[576,1024]{1,0:T(8,128)} %get-tuple-element.137.resid_ref, bf16[576,1024]{1,0:T(8,128)(2,1)} %gv_ref.1, s32[1]{0:T(128)S(6)} %copy.122.live_ref, ...), custom_call_target="tpu_custom_call" | custom-call | flops 12079595520 | bytes 17694720 | tf_op jit(solution)/shard_map/gate_both/pallas_call | solution.py:458
  727.0 11.1 depthwise_back.2
  747.2 12.9 multiply_reduce_fusion
  763.5 83.1 %mlp_back.1 = (f32[1024,1536]{1,0:T(8,128)}, bf16[1536,6144]{1,0:T(8,128)(2,1)}) custom-call(bf16[1024,1536]{1,0:T(8,128)(2,1)} %get-tuple-element.135.g_ref.right_ref, bf16[1024,1536]{1,0:T(8,128)(2,1)} %multiply_convert_fusion.3.h_ref, bf16[1024,6144]{1,0:T(8,128)(2,1)} %get-tuple-element.48.slope_ref, ...), custom_call_target="tpu_custom_call" | custom-call | flops 67645734912 | bytes 56623104 | tf_op jit(solution)/shard_map/mlp_back/pallas_call | solution.py:412
  846.6 12.7 fusion.128
  877.2 74.3 %depthwise_back.3 = (f32[1024,1536]{1,0:T(8,128)}, f32[49,1536]{1,0:T(8,128)S(1)}) custom-call(f32[1024,1536]{1,0:T(8,128)S(1)} %subtract_multiply_fusion.grad_ref, bf16[1024,1536]{1,0:T(8,128)(2,1)S(1)} %copy-done.4, f32[1024,1536]{1,0:T(8,128)S(1)} %copy-done.5, bf16[49,1536]{1,0:T(8,128)(2,1)S(1)} %copy-done.2), custom_call_target="tpu_custom_call" | custom-call | flops 92484403200 | bytes 22020096 | tf_op jit(solution)/shard_map/depthwise_back/pallas_call | solution.py:189
  972.7 24.5 %outer_sum.1 = bf16[6144,1536]{1,0:T(8,128)(2,1)} custom-call(bf16[1024,6144]{1,0:T(8,128)(2,1)} %get-tuple-element.58.left_ref, bf16[1024,1536]{1,0:T(8,128)(2,1)S(1)} %copy-done.6), custom_call_target="tpu_custom_call" | custom-call | flops 28991029248 | bytes 18874368 | tf_op jit(solution)/shard_map/outer_sum/pallas_call | solution.py:370
  1115.9 13.5 %collective-permute-done.36 = bf16[2,2,2,144,512]{4,3,2,1,0:T(8,128)(2,1)} collective-permute-done((bf16[2,2,2,144,512]{4,3,2,1,0:T(8,128)(2,1)}, bf16[2,2,2,144,512]{4,3,2,1,0:T(8,128)(2,1)}, u32[]{:S(2)}, u32[]{:S(2)}) %collective-permute-start.36) | collective-permute-done | bytes 1179680 | tf_op jit(solution)/shard_map/ppermute | solution.py:505
  1137.8 17.5 %collective-permute-done.37 = bf16[2,2,144,512]{3,2,1,0:T(8,128)(2,1)S(1)} collective-permute-done((bf16[2,2,144,512]{3,2,1,0:T(8,128)(2,1)S(1)}, bf16[2,2,144,512]{3,2,1,0:T(8,128)(2,1)S(1)}, u32[]{:S(2)}, u32[]{:S(2)}) %collective-permute-start.37) | collective-permute-done | bytes 589856 | tf_op jit(solution)/shard_map/ppermute | solution.py:505
  1178.1 11.0 collective-permute-done.81
  1191.2 30.8 %collective-permute-done.91 = bf16[2,2,2,192,512]{4,3,2,0,1:T(8,128)(2,1)S(1)} collective-permute-done((bf16[2,2,2,192,512]{4,3,2,0,1:T(8,128)(2,1)}, bf16[2,2,2,192,512]{4,3,2,0,1:T(8,128)(2,1)S(1)}, u32[]{:S(2)}, u32[]{:S(2)}) %collective-permute-start.91) | collective-permute-done | bytes 1572896 | tf_op jit(solution)/shard_map/ppermute | solution.py:505
  1224.9 17.7 %collective-permute-done.96 = bf16[2,2,2,192,512]{4,3,0,1,2:T(8,128)(2,1)S(1)} collective-permute-done((bf16[2,2,2,192,512]{4,3,0,1,2:T(8,128)(2,1)S(1)}, bf16[2,2,2,192,512]{4,3,0,1,2:T(8,128)(2,1)S(1)}, u32[]{:S(2)}, u32[]{:S(2)}) %collective-permute-start.96) | collective-permute-done | bytes 1572896 | tf_op jit(solution)/shard_map/ppermute | solution.py:505
  1247.3 10.1 collective-permute-done.82
  1258.1 13.7 %collective-permute-done.87 = bf16[2,2,192,512]{3,2,1,0:T(8,128)(2,1)S(1)} collective-permute-done((bf16[2,2,192,512]{3,2,1,0:T(8,128)(2,1)S(1)}, bf16[2,2,192,512]{3,2,1,0:T(8,128)(2,1)S(1)}, u32[]{:S(2)}, u32[]{:S(2)}) %collective-permute-start.87) | collective-permute-done | bytes 786464 | tf_op jit(solution)/shard_map/ppermute | solution.py:505
  1292.2 19.7 %collective-permute-done.93 = bf16[2,192,512]{2,1,0:T(8,128)(2,1)S(1)} collective-permute-done((bf16[2,192,512]{2,1,0:T(8,128)(2,1)S(1)}, bf16[2,192,512]{2,1,0:T(8,128)(2,1)S(1)}, u32[]{:S(2)}, u32[]{:S(2)}) %collective-permute-start.93) | collective-permute-done | bytes 393248 | tf_op jit(solution)/shard_map/ppermute | solution.py:505
  1312.0 12.5 collective-permute-done.88
  (642 shorter events, 523.8 us)
Async XLA Ops:
  7.2 104.7 %all-gather.10.cloned.1.call-start = ((), (), s32[]{:S(2)}) async-start(), calls=%async_computation.2 | async-start | bytes 12976128 | tf_op jit(solution)/shard_map/all_gather | solution.py:591
  9.1 181.5 %all-gather.12.cloned.1.call-start = ((), (), s32[]{:S(2)}) async-start(), calls=%async_computation.3 | async-start | bytes 8650752 | tf_op jit(solution)/shard_map/all_gather | solution.py:591
  9.9 259.7 %all-gather.14.cloned.1.call-start = ((), (), s32[]{:S(2)}) async-start(), calls=%async_computation.4 | async-start | bytes 8650752 | tf_op jit(solution)/shard_map/all_gather | solution.py:591
  10.6 625.8 %all-gather.8.cloned.1.call-start = ((), (), s32[]{:S(2)}) async-start(), calls=%async_computation.1 | async-start | bytes 19464192 | tf_op jit(solution)/shard_map/all_gather | solution.py:591
  11.2 625.3 %all-gather.6.cloned.1.call-start = ((), (), s32[]{:S(2)}) async-start(), calls=%async_computation | async-start | bytes 22708224 | tf_op jit(solution)/shard_map/all_gather | solution.py:591
  403.4 178.6 %collective-permute-start.65 = (bf16[2,2,2,2,128,512]{5,4,3,2,1,0:T(8,128)(2,1)S(1)}, bf16[2,2,2,2,128,512]{5,4,3,2,1,0:T(8,128)(2,1)S(1)}, u32[]{:S(2)}, u32[]{:S(2)}) collective-permute-start(bf16[2,2,2,2,128,512]{5,4,3,2,1,0:T(8,128)(2,1)S(1)} %dynamic-slice_bitcast_fusion.3), channel_id=1, source_target_pairs={{0,1},{1,0},{2,3},{3,2},{4,5},{5,4},{6,7},{7,6},{8,9},{9,8},{10,11... | collective-permute-start | bytes 6291464 | tf_op jit(solution)/shard_map/ppermute | solution.py:505
  424.7 136.3 %collective-permute-start.41 = (bf16[2,2,2,32,1280]{4,3,2,1,0:T(8,128)(2,1)S(1)}, bf16[2,2,2,32,1280]{4,3,2,1,0:T(8,128)(2,1)S(1)}, u32[]{:S(2)}, u32[]{:S(2)}) collective-permute-start(bf16[2,2,2,32,1280]{4,3,2,1,0:T(8,128)(2,1)S(1)} %dynamic-slice_bitcast_fusion.28), channel_id=1, source_target_pairs={{0,4},{1,5},{2,6},{3,7},{4,0},{5,1},{6,2},{7,3},{8,12},{9,13},{10,... | collective-permute-start | bytes 1966088 | tf_op jit(solution)/shard_map/ppermute | solution.py:505
  436.1 129.1 %collective-permute-start.46 = (bf16[2,2,2,32,1280]{4,3,2,1,0:T(8,128)(2,1)S(1)}, bf16[2,2,2,32,1280]{4,3,2,1,0:T(8,128)(2,1)S(1)}, u32[]{:S(2)}, u32[]{:S(2)}) collective-permute-start(bf16[2,2,2,32,1280]{4,3,2,1,0:T(8,128)(2,1)S(1)} %dynamic-slice_bitcast_fusion.27), channel_id=1, source_target_pairs={{0,2},{1,3},{2,0},{3,1},{4,6},{5,7},{6,4},{7,5},{8,10},{9,11},{10,... | collective-permute-start | bytes 1966088 | tf_op jit(solution)/shard_map/ppermute | solution.py:505
  475.0 115.2 %collective-permute-start.51 = (bf16[2,2,2,32,1536]{4,3,2,1,0:T(8,128)(2,1)S(1)}, bf16[2,2,2,32,1536]{4,3,2,1,0:T(8,128)(2,1)S(1)}, u32[]{:S(2)}, u32[]{:S(2)}) collective-permute-start(bf16[2,2,2,32,1536]{4,3,2,1,0:T(8,128)(2,1)S(1)} %dynamic-slice_bitcast_fusion.26), channel_id=1, source_target_pairs={{0,2},{1,3},{2,0},{3,1},{4,6},{5,7},{6,4},{7,5},{8,10},{9,11},{10,... | collective-permute-start | bytes 2359304 | tf_op jit(solution)/shard_map/ppermute | solution.py:505
  956.2 48.7 %collective-permute-start.5 = (f32[2,2,2,2,2800]{4,3,2,1,0:T(2,128)S(1)}, f32[2,2,2,2,2800]{4,3,2,1,0:T(2,128)S(1)}, u32[]{:S(2)}, u32[]{:S(2)}) collective-permute-start(f32[2,2,2,2,2800]{4,3,2,1,0:T(2,128)S(1)} %bitcast.602), channel_id=1, source_target_pairs={{0,1},{1,0},{2,3},{3,2},{4,5},{5,4},{6,7},{7,6},{8,9},{9,8},{10,11... | collective-permute-start | bytes 537608 | tf_op jit(solution)/shard_map/ppermute | solution.py:505
  968.8 128.0 %collective-permute-start.75 = (bf16[2,2,2,2,48,2048]{5,4,2,0,1,3:T(8,128)(2,1)}, bf16[2,2,2,2,48,2048]{5,4,2,0,1,3:T(8,128)(2,1)}, u32[]{:S(2)}, u32[]{:S(2)}) collective-permute-start(bf16[2,2,2,2,48,2048]{5,4,2,0,1,3:T(8,128)(2,1)} %bitcast.534), channel_id=1, source_target_pairs={{0,1},{1,0},{2,3},{3,2},{4,5},{5,4},{6,7},{7,6},{8,9},{9,8},{10,11... | collective-permute-start | bytes 9437192 | tf_op jit(solution)/shard_map/ppermute | solution.py:505
  969.3 136.0 %collective-permute-start.70 = (bf16[2,2,2,2,48,2048]{5,4,3,2,1,0:T(8,128)(2,1)}, bf16[2,2,2,2,48,2048]{5,4,3,2,1,0:T(8,128)(2,1)}, u32[]{:S(2)}, u32[]{:S(2)}) collective-permute-start(bf16[2,2,2,2,48,2048]{5,4,3,2,1,0:T(8,128)(2,1)} %dynamic-slice_bitcast_fusion.1), channel_id=1, source_target_pairs={{0,1},{1,0},{2,3},{3,2},{4,5},{5,4},{6,7},{7,6},{8,9},{9,8},{10,11... | collective-permute-start | bytes 9437192 | tf_op jit(solution)/shard_map/ppermute | solution.py:505
  971.5 56.5 %collective-permute-start.25 = (bf16[2,2,2,2,144,256]{5,4,3,2,1,0:T(8,128)(2,1)}, bf16[2,2,2,2,144,256]{5,4,3,2,1,0:T(8,128)(2,1)}, u32[]{:S(2)}, u32[]{:S(2)}) collective-permute-start(bf16[2,2,2,2,144,256]{5,4,3,2,1,0:T(8,128)(2,1)} %dynamic-slice_bitcast_fusion.15), channel_id=1, source_target_pairs={{0,1},{1,0},{2,3},{3,2},{4,5},{5,4},{6,7},{7,6},{8,9},{9,8},{10,11... | collective-permute-start | bytes 3538952 | tf_op jit(solution)/shard_map/ppermute | solution.py:505
  972.0 60.4 %collective-permute-start.30 = (bf16[2,2,2,2,144,256]{5,4,3,2,1,0:T(8,128)(2,1)}, bf16[2,2,2,2,144,256]{5,4,3,2,1,0:T(8,128)(2,1)}, u32[]{:S(2)}, u32[]{:S(2)}) collective-permute-start(bf16[2,2,2,2,144,256]{5,4,3,2,1,0:T(8,128)(2,1)} %dynamic-slice_bitcast_fusion.14), channel_id=1, source_target_pairs={{0,1},{1,0},{2,3},{3,2},{4,5},{5,4},{6,7},{7,6},{8,9},{9,8},{10,11... | collective-permute-start | bytes 3538952 | tf_op jit(solution)/shard_map/ppermute | solution.py:505
  1027.3 72.9 %collective-permute-start.80 = (bf16[2,2,2,2,48,2048]{5,4,0,1,2,3:T(8,128)(2,1)}, bf16[2,2,2,2,48,2048]{5,4,0,1,2,3:T(8,128)(2,1)}, u32[]{:S(2)}, u32[]{:S(2)}) collective-permute-start(bf16[2,2,2,2,48,2048]{5,4,0,1,2,3:T(8,128)(2,1)} %bitcast.533), channel_id=1, source_target_pairs={{0,1},{1,0},{2,3},{3,2},{4,5},{5,4},{6,7},{7,6},{8,9},{9,8},{10,11... | collective-permute-start | bytes 9437192 | tf_op jit(solution)/shard_map/ppermute | solution.py:505
  1046.7 45.7 %collective-permute-start.35 = (bf16[2,2,2,2,144,512]{5,4,3,2,1,0:T(8,128)(2,1)}, bf16[2,2,2,2,144,512]{5,4,3,2,1,0:T(8,128)(2,1)S(1)}, u32[]{:S(2)}, u32[]{:S(2)}) collective-permute-start(bf16[2,2,2,2,144,512]{5,4,3,2,1,0:T(8,128)(2,1)} %dynamic-slice_bitcast_fusion.2), channel_id=1, source_target_pairs={{0,1},{1,0},{2,3},{3,2},{4,5},{5,4},{6,7},{7,6},{8,9},{9,8},{10,11... | collective-permute-start | bytes 7077896 | tf_op jit(solution)/shard_map/ppermute | solution.py:505
  1092.5 63.0 %collective-permute-start.85 = (bf16[2,2,2,2,192,512]{5,4,3,2,1,0:T(8,128)(2,1)}, bf16[2,2,2,2,192,512]{5,4,3,2,1,0:T(8,128)(2,1)}, u32[]{:S(2)}, u32[]{:S(2)}) collective-permute-start(bf16[2,2,2,2,192,512]{5,4,3,2,1,0:T(8,128)(2,1)} %dynamic-slice_bitcast_fusion), channel_id=1, source_target_pairs={{0,1},{1,0},{2,3},{3,2},{4,5},{5,4},{6,7},{7,6},{8,9},{9,8},{10,11... | collective-permute-start | bytes 9437192 | tf_op jit(solution)/shard_map/ppermute | solution.py:505
  1096.8 36.2 %collective-permute-start.95 = (bf16[2,2,2,2,192,512]{5,4,0,1,3,2:T(8,128)(2,1)}, bf16[2,2,2,2,192,512]{5,4,0,1,3,2:T(8,128)(2,1)}, u32[]{:S(2)}, u32[]{:S(2)}) collective-permute-start(bf16[2,2,2,2,192,512]{5,4,0,1,3,2:T(8,128)(2,1)} %bitcast.531), channel_id=1, source_target_pairs={{0,1},{1,0},{2,3},{3,2},{4,5},{5,4},{6,7},{7,6},{8,9},{9,8},{10,11... | collective-permute-start | bytes 9437192 | tf_op jit(solution)/shard_map/ppermute | solution.py:505
  1105.2 68.9 %collective-permute-start.76 = (bf16[2,2,2,48,2048]{4,3,2,0,1:T(8,128)(2,1)}, bf16[2,2,2,48,2048]{4,3,2,0,1:T(8,128)(2,1)}, u32[]{:S(2)}, u32[]{:S(2)}) collective-permute-start(bf16[2,2,2,48,2048]{4,3,2,0,1:T(8,128)(2,1)} %dynamic-slice_bitcast_fusion.8), channel_id=1, source_target_pairs={{0,2},{1,3},{2,0},{3,1},{4,6},{5,7},{6,4},{7,5},{8,10},{9,11},{10,... | collective-permute-start | bytes 4718600 | tf_op jit(solution)/shard_map/ppermute | solution.py:505
  1111.1 66.2 %collective-permute-start.71 = (bf16[2,2,2,48,2048]{4,3,2,1,0:T(8,128)(2,1)}, bf16[2,2,2,48,2048]{4,3,2,1,0:T(8,128)(2,1)S(1)}, u32[]{:S(2)}, u32[]{:S(2)}) collective-permute-start(bf16[2,2,2,48,2048]{4,3,2,1,0:T(8,128)(2,1)} %dynamic-slice_bitcast_fusion.9), channel_id=1, source_target_pairs={{0,4},{1,5},{2,6},{3,7},{4,0},{5,1},{6,2},{7,3},{8,12},{9,13},{10,... | collective-permute-start | bytes 4718600 | tf_op jit(solution)/shard_map/ppermute | solution.py:505
  1132.9 56.2 %collective-permute-start.81 = (bf16[2,2,2,48,2048]{4,3,0,1,2:T(8,128)(2,1)}, bf16[2,2,2,48,2048]{4,3,0,1,2:T(8,128)(2,1)}, u32[]{:S(2)}, u32[]{:S(2)}) collective-permute-start(bf16[2,2,2,48,2048]{4,3,0,1,2:T(8,128)(2,1)} %dynamic-slice_bitcast_fusion.7), channel_id=1, source_target_pairs={{0,2},{1,3},{2,0},{3,1},{4,6},{5,7},{6,4},{7,5},{8,10},{9,11},{10,... | collective-permute-start | bytes 4718600 | tf_op jit(solution)/shard_map/ppermute | solution.py:505
  1155.3 66.7 %collective-permute-start.91 = (bf16[2,2,2,192,512]{4,3,2,0,1:T(8,128)(2,1)}, bf16[2,2,2,192,512]{4,3,2,0,1:T(8,128)(2,1)S(1)}, u32[]{:S(2)}, u32[]{:S(2)}) collective-permute-start(bf16[2,2,2,192,512]{4,3,2,0,1:T(8,128)(2,1)} %dynamic-slice_bitcast_fusion.5), channel_id=1, source_target_pairs={{0,2},{1,3},{2,0},{3,1},{4,6},{5,7},{6,4},{7,5},{8,10},{9,11},{10,... | collective-permute-start | bytes 4718600 | tf_op jit(solution)/shard_map/ppermute | solution.py:505
  1171.6 52.7 %collective-permute-start.86 = (bf16[2,2,2,192,512]{4,3,2,1,0:T(8,128)(2,1)S(1)}, bf16[2,2,2,192,512]{4,3,2,1,0:T(8,128)(2,1)S(1)}, u32[]{:S(2)}, u32[]{:S(2)}) collective-permute-start(bf16[2,2,2,192,512]{4,3,2,1,0:T(8,128)(2,1)S(1)} %dynamic-slice_bitcast_fusion.6), channel_id=1, source_target_pairs={{0,4},{1,5},{2,6},{3,7},{4,0},{5,1},{6,2},{7,3},{8,12},{9,13},{10,... | collective-permute-start | bytes 4718600 | tf_op jit(solution)/shard_map/ppermute | solution.py:505
  1174.2 68.5 %collective-permute-start.96 = (bf16[2,2,2,192,512]{4,3,0,1,2:T(8,128)(2,1)S(1)}, bf16[2,2,2,192,512]{4,3,0,1,2:T(8,128)(2,1)S(1)}, u32[]{:S(2)}, u32[]{:S(2)}) collective-permute-start(bf16[2,2,2,192,512]{4,3,0,1,2:T(8,128)(2,1)S(1)} %dynamic-slice_bitcast_fusion.4), channel_id=1, source_target_pairs={{0,4},{1,5},{2,6},{3,7},{4,0},{5,1},{6,2},{7,3},{8,12},{9,13},{10,... | collective-permute-start | bytes 4718600 | tf_op jit(solution)/shard_map/ppermute | solution.py:505
  1177.3 65.9 %collective-permute-start.77 = (bf16[2,2,48,2048]{3,2,1,0:T(8,128)(2,1)S(1)}, bf16[2,2,48,2048]{3,2,1,0:T(8,128)(2,1)S(1)}, u32[]{:S(2)}, u32[]{:S(2)}) collective-permute-start(bf16[2,2,48,2048]{3,2,1,0:T(8,128)(2,1)S(1)} %dynamic-slice_bitcast_fusion.24), channel_id=1, source_target_pairs={{0,8},{1,9},{2,10},{3,11},{4,12},{5,13},{6,14},{7,15},{8,0},{9,1},... | collective-permute-start | bytes 2359304 | tf_op jit(solution)/shard_map/ppermute | solution.py:505
  1189.1 55.3 %collective-permute-start.72 = (bf16[2,2,48,2048]{3,2,1,0:T(8,128)(2,1)S(1)}, bf16[2,2,48,2048]{3,2,1,0:T(8,128)(2,1)S(1)}, u32[]{:S(2)}, u32[]{:S(2)}) collective-permute-start(bf16[2,2,48,2048]{3,2,1,0:T(8,128)(2,1)S(1)} %dynamic-slice_bitcast_fusion.25), channel_id=1, source_target_pairs={{0,8},{1,9},{2,10},{3,11},{4,12},{5,13},{6,14},{7,15},{8,0},{9,1},... | collective-permute-start | bytes 2359304 | tf_op jit(solution)/shard_map/ppermute | solution.py:505
  1222.0 35.4 %collective-permute-start.82 = (bf16[2,2,48,2048]{3,2,0,1:T(8,128)(2,1)S(1)}, bf16[2,2,48,2048]{3,2,0,1:T(8,128)(2,1)S(1)}, u32[]{:S(2)}, u32[]{:S(2)}) collective-permute-start(bf16[2,2,48,2048]{3,2,0,1:T(8,128)(2,1)S(1)} %dynamic-slice_bitcast_fusion.23), channel_id=1, source_target_pairs={{0,4},{1,5},{2,6},{3,7},{4,0},{5,1},{6,2},{7,3},{8,12},{9,13},{10,... | collective-permute-start | bytes 2359304 | tf_op jit(solution)/shard_map/ppermute | solution.py:505
  1271.7 40.1 %collective-permute-start.93 = (bf16[2,192,512]{2,1,0:T(8,128)(2,1)S(1)}, bf16[2,192,512]{2,1,0:T(8,128)(2,1)S(1)}, u32[]{:S(2)}, u32[]{:S(2)}) collective-permute-start(bf16[2,192,512]{2,1,0:T(8,128)(2,1)S(1)} %dynamic-slice_bitcast_fusion.39), channel_id=1, source_target_pairs={{0,16},{1,17},{2,18},{3,19},{4,20},{5,21},{6,22},{7,23},{8,24},{9,... | collective-permute-start | bytes 1179656 | tf_op jit(solution)/shard_map/ppermute | solution.py:505
  1277.5 47.0 %collective-permute-start.88 = (bf16[2,192,512]{2,1,0:T(8,128)(2,1)S(1)}, bf16[2,192,512]{2,1,0:T(8,128)(2,1)S(1)}, u32[]{:S(2)}, u32[]{:S(2)}) collective-permute-start(bf16[2,192,512]{2,1,0:T(8,128)(2,1)S(1)} %dynamic-slice_bitcast_fusion.40), channel_id=1, source_target_pairs={{0,16},{1,17},{2,18},{3,19},{4,20},{5,21},{6,22},{7,23},{8,24},{9,... | collective-permute-start | bytes 1179656 | tf_op jit(solution)/shard_map/ppermute | solution.py:505
  1277.9 47.1 %collective-permute-start.98 = (bf16[2,192,512]{2,1,0:T(8,128)(2,1)S(1)}, bf16[2,192,512]{2,1,0:T(8,128)(2,1)S(1)}, u32[]{:S(2)}, u32[]{:S(2)}) collective-permute-start(bf16[2,192,512]{2,1,0:T(8,128)(2,1)S(1)} %dynamic-slice_bitcast_fusion.38), channel_id=1, source_target_pairs={{0,8},{1,9},{2,10},{3,11},{4,12},{5,13},{6,14},{7,15},{8,0},{9,1},... | collective-permute-start | bytes 1179656 | tf_op jit(solution)/shard_map/ppermute | solution.py:505
  1287.3 38.0 %collective-permute-start.79 = (bf16[48,2048]{1,0:T(8,128)(2,1)S(1)}, bf16[48,2048]{1,0:T(8,128)(2,1)S(1)}, u32[]{:S(2)}, u32[]{:S(2)}) collective-permute-start(bf16[48,2048]{1,0:T(8,128)(2,1)S(1)} %dynamic-slice_bitcast_fusion.60), channel_id=1, source_target_pairs={{0,4},{1,5},{2,6},{3,7},{4,0},{5,1},{6,2},{7,3},{8,12},{9,13},{10,... | collective-permute-start | bytes 589832 | tf_op jit(solution)/shard_map/ppermute | solution.py:505
  1288.6 36.8 %collective-permute-start.74 = (bf16[48,2048]{1,0:T(8,128)(2,1)S(1)}, bf16[48,2048]{1,0:T(8,128)(2,1)S(1)}, u32[]{:S(2)}, u32[]{:S(2)}) collective-permute-start(bf16[48,2048]{1,0:T(8,128)(2,1)S(1)} %dynamic-slice_bitcast_fusion.61), channel_id=1, source_target_pairs={{0,2},{1,3},{2,0},{3,1},{4,6},{5,7},{6,4},{7,5},{8,10},{9,11},{10,... | collective-permute-start | bytes 589832 | tf_op jit(solution)/shard_map/ppermute | solution.py:505
  (143 other events, 1640.1 us)
Sparse Core Ops, SparseCore 0:
  11.5 100.3 all-gather.9
  114.8 75.7 all-gather.11
  193.5 76.0 all-gather.13
  272.3 123.2 all-gather.7
  398.3 179.4 all-gather.5

commit v2 on v1

--- a/solution.py
+++ b/solution.py
@@ -144,7 +144,7 @@
 
     fill_shifted(shifted, grad_ref[...], width, edge)
     cells_ref[...] = field_ref[...].astype(F32)
-    sums_ref[...] = base_ref[...]
+    sums_ref[...] = base_ref[...].astype(F32)
     wide[...] = jnp.broadcast_to(taps_ref[...].astype(F32)[:, None, :], wide.shape)
     strips = edge // 8
     last = width - 1
@@ -182,18 +182,19 @@
     out_ref[...] = sums_ref[...].astype(out_ref.dtype)
 
 
-def depthwise_back(grad, field, base, taps, width, edge, out_type):
+def depthwise_back(grad, field, base, taps, width, edge, first, last):
     cells, channels = field.shape
-    full = pl.BlockSpec((cells, LANES), lambda i: (0, i))
-    small = pl.BlockSpec((width * width, LANES), lambda i: (0, i))
+    skip = first // LANES
+    full = pl.BlockSpec((cells, LANES), lambda i: (0, i + skip))
+    small = pl.BlockSpec((width * width, LANES), lambda i: (0, i + skip))
     return pl.pallas_call(
         functools.partial(depthwise_back_kernel, width, edge),
-        grid=(channels // LANES,),
+        grid=((last - first) // LANES,),
         in_specs=[full, full, full, small],
-        out_specs=[full, small],
+        out_specs=[full, pl.BlockSpec((width * width, LANES), lambda i: (0, i))],
         out_shape=[
-            jax.ShapeDtypeStruct((cells, channels), out_type),
-            jax.ShapeDtypeStruct((width * width, channels), F32),
+            jax.ShapeDtypeStruct((cells, channels), base.dtype),
+            jax.ShapeDtypeStruct((width * width, last - first), F32),
         ],
         scratch_shapes=[
             pltpu.VMEM((width, edge + width - 1, edge, LANES), F32),
@@ -201,8 +202,11 @@
             pltpu.VMEM((cells, LANES), F32),
             pltpu.VMEM((cells, LANES), F32),
         ],
+        input_output_aliases={2: 0},
         compiler_params=kernel_limits(32),
-        cost_estimate=estimate(1200 * width * width * cells * channels, 14 * cells * channels),
+        cost_estimate=estimate(
+            1200 * width * width * cells * (last - first), 14 * cells * (last - first)
+        ),
         name="depthwise_back",
     )(grad, field, base, taps)
 
@@ -278,7 +282,44 @@
     )(qkv, qkv, qkv, grad)
 
 
-def mlp_both_kernel(g_ref, h_ref, wi_ref, wo_ref, out_ref, dh_ref, dwi_ref, dwo_ref):
+def start_copies(plan, me, sources, target, semaphore, first=0, last=None):
+    for source, (slots, rows, offset, begin, end) in zip(sources, plan):
+        left, right = (max(begin, first), end if last is None else min(end, last))
+        if left >= right:
+            continue
+        for place, slot in enumerate(slots):
+            line = 0 if slot is None else pl.multiple_of((me ^ slot) * rows, rows)
+            pltpu.make_async_copy(
+                source.at[place, :, pl.ds(left - begin + offset, right - left)],
+                target.at[pl.ds(line, rows), pl.ds(left - first, right - left)],
+                semaphore,
+            ).start()
+
+
+def store_shares(value, rows, even, mine_ref, theirs_ref, lines=slice(None)):
+    low = value.astype(BF16).reshape(-1, 2, rows, value.shape[-1])
+
+    @pl.when(even)
+    def _():
+        mine_ref[lines] = low[:, 0]
+        theirs_ref[lines] = low[:, 1]
+
+    @pl.when(jnp.logical_not(even))
+    def _():
+        mine_ref[lines] = low[:, 1]
+        theirs_ref[lines] = low[:, 0]
+
+
+def share_type(devices, rows, columns):
+    return jax.ShapeDtypeStruct((devices // 2, rows, columns), BF16)
+
+
+SCALARS = pl.BlockSpec(memory_space=pltpu.SMEM)
+ANYWHERE = pl.BlockSpec(memory_space=pl.ANY)
+LOCAL = pl.BlockSpec(memory_space=pltpu.VMEM)
+
+
+def mlp_both_kernel(shares, me_ref, g_ref, h_ref, wi_ref, wo_ref, out_ref, dh_ref, *grads):
     @pl.when(pl.program_id(0) == 0)
     def _():
         out_ref[...] = jnp.zeros_like(out_ref)
@@ -291,98 +332,176 @@
     out_ref[...] += dot(act, wo_ref[...], NN)
     low = (back * slope).astype(BF16)
     dh_ref[...] += dot(low, wi_ref[...], NT)
-    dwi_ref[...] = dot(h_ref[...], low, TN).astype(BF16)
-    dwo_ref[...] = dot(act, g_ref[...], TN).astype(BF16)
-
-
-def mlp_both(grad, field, w_in, w_out, tile):
+    even = me_ref[0] % 2 == 0
+    if shares[0]:
+        store_shares(dot(h_ref[...], low, TN), shares[0], even, *grads[:2])
+    else:
+        grads[0][...] = dot(h_ref[...], low, TN).astype(BF16)
+    store_shares(dot(act, g_ref[...], TN), shares[1], even, *grads[-2:])
+
+
+def mlp_both(grad, field, w_in, w_out, me, devices, tile):
     rows, wide = field.shape
     hidden = w_out.shape[0]
-    whole = pl.BlockSpec((rows, wide), lambda i: (0, 0))
+    whole = pl.BlockSpec((rows, wide), lambda i: (0, 0), pipeline_mode=pl.Buffered(1))
+    total = pl.BlockSpec((rows, wide), lambda i: (0, 0))
     columns = pl.BlockSpec((wide, tile), lambda i: (0, i))
-    lines = pl.BlockSpec((tile, wide), lambda i: (i, 0))
-    return pl.pallas_call(
-        mlp_both_kernel,
+    in_rows, out_rows = (wide // devices, hidden // devices)
+    in_specs = [pl.BlockSpec((devices // 2, in_rows, tile), lambda i: (0, 0, i))] * 2
+    in_types = [share_type(devices, in_rows, hidden)] * 2
+    if in_rows % 16:
+        in_rows = 0
+        in_specs = [columns]
+        in_types = [jax.ShapeDtypeStruct((wide, hidden), BF16)]
+    out_block = pl.BlockSpec((tile // out_rows // 2, out_rows, wide), lambda i: (i, 0, 0))
+    outs = pl.pallas_call(
+        functools.partial(mlp_both_kernel, (in_rows, out_rows)),
         grid=(hidden // tile,),
-        in_specs=[whole, whole, columns, lines],
-        out_specs=[whole, whole, columns, lines],
+        in_specs=[SCALARS, whole, whole, columns, pl.BlockSpec((tile, wide), lambda i: (i, 0))],
+        out_specs=[total, total] + in_specs + [out_block] * 2,
         out_shape=[
             jax.ShapeDtypeStruct((rows, wide), F32),
             jax.ShapeDtypeStruct((rows, wide), F32),
-            jax.ShapeDtypeStruct((wide, hidden), BF16),
-            jax.ShapeDtypeStruct((hidden, wide), BF16),
-        ],
+        ]
+        + in_types
+        + [share_type(devices, out_rows, wide)] * 2,
         compiler_params=kernel_limits(60),
-        cost_estimate=estimate(12 * rows * wide * hidden, 8 * wide * hidden),
+        cost_estimate=estimate(14 * rows * wide * hidden, 8 * wide * hidden),
         name="mlp_both",
-    )(grad, field, w_in, w_out)
-
-
-def mlp_forward_kernel(rows, h_ref, wi_ref, wo_ref, act_ref, slope_ref, out_ref):
-    @pl.when(pl.program_id(0) == 0)
+    )(me, grad, field, w_in, w_out)
+    return (outs[0], outs[1], outs[2:-2], outs[-2:])
+
+
+def mlp_forward_kernel(plan_in, plan_out, tile, tiles, rows, me_ref, h_ref, *refs):
+    count = len(plan_in)
+    sources_in, sources_out = (refs[:count], refs[count : count + len(plan_out)])
+    act_ref, slope_ref, out_ref, wi_natural, wo_natural, wi_two, wo_all, sems = refs[
+        count + len(plan_out) :
+    ]
+    step = pl.program_id(0)
+    me = me_ref[0]
+
+    def load(number):
+        slot = number % 2
+        start_copies(
+            plan_in, me, sources_in, wi_two.at[slot], sems.at[slot], number * tile, (number + 1) * tile
+        )
+
+    def save(number, slot):
+        return pltpu.make_async_copy(
+            wi_two.at[slot],
+            wi_natural.at[:, pl.ds(pl.multiple_of(number * tile, tile), tile)],
+            sems.at[2 + slot],
+        )
+
+    @pl.when(step == 0)
     def _():
+        load(0)
+        start_copies(plan_out, me, sources_out, wo_all, sems.at[4])
         out_ref[...] = jnp.zeros_like(out_ref)
 
-    def body(index, carry):
-        spot = pl.ds(pl.multiple_of(index * rows, rows), rows)
-        act, slope = gelu_pair(dot(h_ref[spot, :], wi_ref[...], NN))
-        act = act.astype(BF16)
-        act_ref[spot, :] = act
-        slope_ref[spot, :] = slope.astype(BF16)
-        out_ref[spot, :] += dot(act, wo_ref[...], NN)
-        return carry
-
-    lax.fori_loop(0, h_ref.shape[0] // rows, body, 0)
-
-
-def mlp_forward(field, w_in, w_out, tile, step):
+    slot = step % 2
+    pltpu.make_async_copy(wi_two.at[slot], wi_two.at[slot], sems.at[slot]).wait()
+    save(step, slot).start()
+
+    @pl.when(step > 0)
+    def _():
+        save(step - 1, 1 - slot).wait()
+
+    for number in range(1, tiles):
+
+        @pl.when(step == number - 1)
+        def _():
+            load(number)
+
+    @pl.when(step == 0)
+    def _():
+        pltpu.make_async_copy(wo_all, wo_all, sems.at[4]).wait()
+        pltpu.make_async_copy(wo_all, wo_natural, sems.at[5]).start()
+
+    @pl.when(step * tile < wo_all.shape[0])
+    def _():
+        def body(index, carry):
+            spot = pl.ds(pl.multiple_of(index * rows, rows), rows)
+            act, slope = gelu_pair(dot(h_ref[spot, :], wi_two[slot], NN))
+            act = act.astype(BF16)
+            act_ref[spot, :] = act
+            slope_ref[spot, :] = slope.astype(BF16)
+            lines = pl.ds(pl.multiple_of(step * tile, tile), tile)
+            out_ref[spot, :] += dot(act, wo_all[lines, :], NN)
+            return carry
+
+        lax.fori_loop(0, h_ref.shape[0] // rows, body, 0)
+
+    @pl.when(step == tiles - 1)
+    def _():
+        save(step, slot).wait()
+        pltpu.make_async_copy(wo_all, wo_natural, sems.at[5]).wait()
+
+
+def mlp_forward(field, pieces_in, pieces_out, me, hidden, columns, tile, step):
+    plan_in, sources_in = pieces_in
+    plan_out, sources_out = pieces_out
     rows, wide = field.shape
-    hidden = w_out.shape[0]
-    whole = pl.BlockSpec((rows, wide), lambda i: (0, 0))
-    tiles = pl.BlockSpec((rows, tile), lambda i: (0, i))
+    last = hidden // tile - 1
+    whole = pl.BlockSpec((rows, wide), lambda i: (0, 0), pipeline_mode=pl.Buffered(1))
+    tiles = pl.BlockSpec((rows, tile), lambda i: (0, jnp.minimum(i, last)))
+    anywhere = pl.BlockSpec(memory_space=pl.ANY)
     return pl.pallas_call(
-        functools.partial(mlp_forward_kernel, step),
-        grid=(hidden // tile,),
-        in_specs=[
-            whole,
-            pl.BlockSpec((wide, tile), lambda i: (0, i)),
-            pl.BlockSpec((tile, wide), lambda i: (i, 0)),
-        ],
-        out_specs=[tiles, tiles, whole],
+        functools.partial(mlp_forward_kernel, plan_in, plan_out, tile, columns // tile, step),
+        grid=(columns // tile,),
+        in_specs=[pl.BlockSpec(memory_space=pltpu.SMEM), whole]
+        + [anywhere] * (len(sources_in) + len(sources_out)),
+        out_specs=[tiles, tiles, whole, anywhere, anywhere],
         out_shape=[
             jax.ShapeDtypeStruct((rows, hidden), BF16),
             jax.ShapeDtypeStruct((rows, hidden), BF16),
             jax.ShapeDtypeStruct((rows, wide), F32),
+            jax.ShapeDtypeStruct((wide, columns), BF16),
+            jax.ShapeDtypeStruct((hidden, wide), BF16),
+        ],
+        scratch_shapes=[
+            pltpu.VMEM((2, wide, tile), BF16),
+            pltpu.VMEM((hidden, wide), BF16),
+            pltpu.SemaphoreType.DMA((6,)),
         ],
         compiler_params=kernel_limits(60),
-        cost_estimate=estimate(6 * rows * wide * hidden, 4 * wide * hidden + 4 * rows * hidden),
+        cost_estimate=estimate(7 * rows * wide * hidden, 8 * wide * hidden + 4 * rows * hidden),
         name="mlp_forward",
-    )(field, w_in, w_out)
-
-
-def outer_kernel(left_ref, right_ref, out_ref):
-    out_ref[...] = dot(left_ref[...], right_ref[...], TN).astype(BF16)
-
-
-def outer_sum(left, right, tile):
+    )(me, field, *sources_in, *sources_out)
+
+
+def outer_kernel(shares, me_ref, left_ref, right_ref, mine_ref, theirs_ref):
+    value = dot(left_ref[...], right_ref[...], TN)
+    store_shares(value, shares, me_ref[0] % 2 == 0, mine_ref, theirs_ref)
+
+
+def outer_sum(left, right, me, share):
     rows, lines = left.shape
     columns = right.shape[1]
+    tile = 4 * share if share >= 192 else 16 * share
+    block = pl.BlockSpec((tile // share // 2, share, columns), lambda i: (i, 0, 0))
     return pl.pallas_call(
-        outer_kernel,
+        functools.partial(outer_kernel, share),
         grid=(lines // tile,),
         in_specs=[
+            SCALARS,
             pl.BlockSpec((rows, tile), lambda i: (0, i)),
-            pl.BlockSpec((rows, columns), lambda i: (0, 0)),
+            pl.BlockSpec((rows, columns), lambda i: (0, 0), pipeline_mode=pl.Buffered(1)),
         ],
-        out_specs=pl.BlockSpec((tile, columns), lambda i: (i, 0)),
-        out_shape=jax.ShapeDtypeStruct((lines, columns), BF16),
+        out_specs=[block] * 2,
+        out_shape=[share_type(lines // share, share, columns)] * 2,
         compiler_params=kernel_limits(48),
         cost_estimate=estimate(3 * rows * lines * columns, 2 * lines * columns),
         name="outer_sum",
-    )(left, right)
-
-
-def mlp_back_kernel(step, g_ref, h_ref, slope_ref, wi_ref, wo_ref, start_ref, dh_ref, dwi_ref, low_ref):
+    )(me, left, right)
+
+
+def mlp_back_kernel(
+    step, share, me_ref, g_ref, h_ref, slope_ref, wi_ref, wo_ref, start_ref, dh_ref, *refs
+):
+    *grads, low_ref = refs
+
     @pl.when(pl.program_id(0) == 0)
     def _():
         dh_ref[...] = start_ref[...]
@@ -396,23 +515,38 @@
         return carry
 
     lax.fori_loop(0, h_ref.shape[0] // step, body, 0)
-    block = 256
+    block = 384
+    even = me_ref[0] % 2 == 0
 
     def outer(index, carry):
         spot = pl.ds(pl.multiple_of(index * block, block), block)
-        dwi_ref[spot, :] = dot(h_ref[:, spot], low_ref[...], TN).astype(BF16)
+        value = dot(h_ref[:, spot], low_ref[...], TN)
+        if share:
+            pairs = block // share // 2
+            store_shares(value, share, even, *grads, pl.ds(index * pairs, pairs))
+        else:
+            grads[0][spot, :] = value.astype(BF16)
         return carry
 
-    lax.fori_loop(0, dwi_ref.shape[0] // block, outer, 0)
-
-
-def mlp_back(grad, field, slope, w_in, w_out, start, tile, step, first, last):
+    lax.fori_loop(0, h_ref.shape[1] // block, outer, 0)
+
+
+def mlp_back(grad, field, slope, w_in, w_out, start, me, devices, tile, step, first, last):
     rows, wide = field.shape
-    whole = pl.BlockSpec((rows, wide), lambda i: (0, 0))
-    return pl.pallas_call(
-        functools.partial(mlp_back_kernel, step),
+    width = (last - first) * tile
+    whole = pl.BlockSpec((rows, wide), lambda i: (0, 0), pipeline_mode=pl.Buffered(1))
+    share = wide // devices
+    grad_specs = [pl.BlockSpec((devices // 2, share, tile), lambda i: (0, 0, i))] * 2
+    grad_types = [share_type(devices, share, width)] * 2
+    if share % 16:
+        share = 0
+        grad_specs = [pl.BlockSpec((wide, tile), lambda i: (0, i))]
+        grad_types = [jax.ShapeDtypeStruct((wide, width), BF16)]
+    outs = pl.pallas_call(
+        functools.partial(mlp_back_kernel, step, share),
         grid=(last - first,),
         in_specs=[
+            SCALARS,
             whole,
             whole,
             pl.BlockSpec((rows, tile), lambda i: (0, i + first)),
@@ -420,18 +554,14 @@
             pl.BlockSpec((tile, wide), lambda i: (i + first, 0)),
             whole,
         ],
-        out_specs=[whole, pl.BlockSpec((wide, tile), lambda i: (0, i))],
-        out_shape=[
-            jax.ShapeDtypeStruct((rows, wide), F32),
-            jax.ShapeDtypeStruct((wide, (last - first) * tile), BF16),
-        ],
+        out_specs=[whole] + grad_specs,
+        out_shape=[jax.ShapeDtypeStruct((rows, wide), F32)] + grad_types,
         scratch_shapes=[pltpu.VMEM((rows, tile), BF16)],
         compiler_params=kernel_limits(60),
-        cost_estimate=estimate(
-            7 * rows * wide * tile * (last - first), 6 * wide * tile * (last - first)
-        ),
+        cost_estimate=estimate(7 * rows * wide * width, 6 * wide * width),
         name="mlp_back",
-    )(grad, field, slope, w_in, w_out, start)
+    )(me, grad, field, slope, w_in, w_out, start)
+    return (outs[0], outs[1:])
 
 
 def gate_kernel(
@@ -492,55 +622,197 @@
     return gathered
 
 
-def scatter_sum(partial, bit_order, devices, link_type=jnp.bfloat16):
-    bits = devices.bit_length() - 1
-    rest = partial.shape[1:]
-    field = partial.astype(link_type).reshape((2,) * bits + rest)
-    held = list(range(bits - 1, -1, -1))
-    for bit in bit_order:
-        axis = held.index(bit)
-        mine = own_bit(bit)
-        sent = lax.dynamic_index_in_dim(field, 1 - mine, axis, keepdims=False)
-        kept = lax.dynamic_index_in_dim(field, mine, axis, keepdims=False)
-        arrived = lax.ppermute(sent, "fsdp", bit_pairs(devices, bit))
-        total = kept.astype(jnp.float32) + arrived.astype(jnp.float32)
-        held.pop(axis)
-        field = total.astype(link_type) if held else total
-    return field
-
-
-def scatter_orders(devices):
+def after(values, earlier):
+    if not earlier:
+        return list(values)
+    return list(lax.optimization_barrier(tuple(values) + tuple(earlier))[: len(values)])
+
+
+def swap(block, bits, devices):
+    mask = sum(1 << bit for bit in bits)
+    return lax.ppermute(block, "fsdp", [(index, index ^ mask) for index in range(devices)])
+
+
+def axis_bits(devices):
     bits = devices.bit_length() - 1
     if bits == 5:
-        x_bits, y_bits, z_bits = (1,), (2,), (3, 4)
-    else:
-        span = (bits - 1 + 2) // 3
-        places = tuple(range(1, bits))
-        x_bits, y_bits, z_bits = places[:span], places[span : 2 * span], places[2 * span :]
-    return (
-        (0,) + y_bits + z_bits + x_bits,
-        (0,) + x_bits + z_bits + y_bits,
-        (0,) + y_bits + x_bits + z_bits,
-        (0,) + x_bits + y_bits + z_bits,
-    )
-
-
-def scatter_weight(gradient, devices, turn):
-    orders = scatter_orders(devices)
-    rows, columns = gradient.shape
-    split = gradient.astype(jnp.bfloat16).reshape(devices, rows // devices, columns)
-    third = columns // 3 // 128 * 128
-    cuts = (0, third, 2 * third, columns)
-    chosen = (orders[0], orders[1], orders[2 + turn % 2])
-    parts = [
-        scatter_sum(split[:, :, cuts[place] : cuts[place + 1]], chosen[place], devices)
-        for place in range(3)
-    ]
-    return jnp.concatenate(parts, axis=-1)
-
-
-def after(value, *earlier):
-    return lax.optimization_barrier((value,) + earlier)[0]
+        return ((1,), (2,), (3, 4))
+    span = (bits - 1 + 2) // 3
+    places = tuple(range(1, bits))
+    return (places[:span], places[span : 2 * span], places[2 * span :])
+
+
+def subsets(bits):
+    found = [()]
+    for bit in bits:
+        found = found + [each + (bit,) for each in found]
+    return found
+
+
+def mask_of(bits):
+    return sum(1 << bit for bit in bits)
+
+
+class Gatherer:
+    def __init__(self, devices):
+        self.devices = devices
+        self.x_bits, self.y_bits, self.z_bits = axis_bits(devices)
+        self.last = []
+        self.ends = []
+
+    def doubled(self, field, slots, bits):
+        for bit in bits:
+            other = swap(field, (bit,), self.devices)
+            field = jnp.concatenate((field, other), axis=0)
+            slots = slots + [slot ^ (1 << bit) for slot in slots]
+        return (field, slots)
+
+    def group(self, block, begin, end, middle):
+        rows = block.shape[0]
+        (own,) = after((block[None, :, begin:end],), self.last)
+        fields, slots = ([own], [0])
+        for bits in subsets(self.z_bits)[1:]:
+            fields.append(swap(own, bits, self.devices))
+            slots.append(mask_of(bits))
+        plan, sources, firsts, seconds = ([], [], [], [])
+        for first, last, left, right in (
+            (self.x_bits, self.y_bits, begin, middle),
+            (self.y_bits, self.x_bits, middle, end),
+        ):
+            field = jnp.concatenate(
+                [each[:, :, left - begin : right - begin] for each in fields], axis=0
+            )
+            (field,) = after((field,), self.ends)
+            firsts.append((*self.doubled(field, slots, first), last, left, right))
+        self.last = [each[0] for each in firsts]
+        self.ends = []
+        for field, its_slots, last, left, right in firsts:
+            held = [(field, its_slots)]
+            for bit in last + (0,):
+                if bit == 0:
+                    self.ends += [part for part, _ in held[1:]]
+                held = held + [
+                    (swap(part, (bit,), self.devices), [slot ^ (1 << bit) for slot in part_slots])
+                    for part, part_slots in held
+                ]
+            for part, part_slots in held:
+                sources.append(part)
+                plan.append((tuple(part_slots), rows, 0, left, right))
+        return (plan, sources)
+
+    def weight(self, block, groups):
+        plan, sources = ([], [])
+        rows = block.shape[0]
+        if rows % 16:
+            whole = lax.all_gather(block, "fsdp", axis=0, tiled=True)[None]
+            plan = [((None,), rows * self.devices, begin, begin, end) for begin, _, end in groups]
+            return (plan, [whole] * len(groups))
+        for begin, middle, end in groups:
+            more_plan, more_sources = self.group(block, begin, end, middle)
+            plan += more_plan
+            sources += more_sources
+        return (plan, sources)
+
+
+def take(field, axis, place):
+    return lax.dynamic_index_in_dim(field, place, axis, keepdims=False)
+
+
+def halved(field, held, bit, devices):
+    axis = held.index(bit)
+    mine = own_bit(bit)
+    arrived = swap(take(field, axis, 1 - mine), (bit,), devices)
+    return (take(field, axis, mine) + arrived, held[:axis] + held[axis + 1 :])
+
+
+class Scatterer:
+    def __init__(self, devices, *gradients):
+        x_bits, y_bits, z_bits = axis_bits(devices)
+        self.bits = devices.bit_length() - 1
+        self.orders = (y_bits + x_bits + z_bits, x_bits + y_bits + z_bits)
+        self.split = len(x_bits + y_bits)
+        self.shapes = [mine.shape[1:] for mine, _ in gradients]
+        self.width = math.gcd(*[shape[1] for shape in self.shapes])
+        self.stage = -1
+        self.kept = [mine for mine, _ in gradients]
+        self.sends = [(theirs, 0) for _, theirs in gradients]
+        self.result = None
+
+    def prepare(self, parts, held):
+        self.kept, self.sends = ([], [])
+        self.held = []
+        for place, part in enumerate(parts):
+            bit = self.orders[place][self.stage]
+            axis = held[place].index(bit)
+            mine = own_bit(bit)
+            self.kept.append(take(part, axis, mine))
+            self.sends.append((take(part, axis, 1 - mine), bit))
+            self.held.append(held[place][:axis] + held[place][axis + 1 :])
+
+    def receive(self, arrived):
+        totals = [
+            kept.astype(F32) + other.astype(F32) for kept, other in zip(self.kept, arrived)
+        ]
+        self.stage += 1
+        if self.stage == self.bits - 1:
+            (total,) = totals
+            self.sends, self.result = ([], [])
+            begin = 0
+            for rows, columns in self.shapes:
+                pieces = []
+                for _ in range(columns // self.width):
+                    pieces.append(total[begin : begin + rows])
+                    begin += rows
+                self.result.append(jnp.concatenate(pieces, axis=1))
+            return
+        parts = [total.astype(BF16) for total in totals]
+        if self.stage == 0:
+            blocks = []
+            for part in parts:
+                for begin in range(0, part.shape[-1], self.width):
+                    blocks.append(part[..., begin : begin + self.width])
+            field = blocks[0] if len(blocks) == 1 else jnp.concatenate(blocks, axis=1)
+            field = field.reshape((2,) * (self.bits - 1) + field.shape[1:])
+            middle = self.width // 2
+            parts = [field[..., :middle], field[..., middle:]]
+            self.held = [list(range(self.bits - 1, 0, -1))] * 2
+        if self.stage == self.split:
+            parts = [jnp.concatenate(parts, axis=-1)]
+        self.prepare(parts, self.held)
+
+
+class Ticks:
+    def __init__(self):
+        self.before = []
+
+    def run(self, groups, value, work):
+        groups = [group for group in groups if group.result is None]
+        sends = [each for group in groups for each in group.sends]
+        value, *blocks = after([value] + [block for block, _ in sends], self.before)
+        devices = lax.axis_size("fsdp")
+        arrived = [swap(block, (bit,), devices) for block, (_, bit) in zip(blocks, sends)]
+        outs = jax.tree.leaves(work(value))
+        done = after(outs + arrived, [])
+        if len(done) > 1:
+            done = list(lax.optimization_barrier(tuple(done)))
+        outs, arrived = (done[: len(outs)], done[len(outs) :])
+        begin = 0
+        for group in groups:
+            count = len(group.sends)
+            group.receive(arrived[begin : begin + count])
+            begin += count
+        self.before = outs[:1]
+        return outs
+
+    def finish(self, groups):
+        while any(group.result is None for group in groups):
+            self.run(groups, jnp.zeros((), F32), lambda value: value)
+
+
+def halves(gradient, devices):
+    pairs = gradient.reshape((devices // 2, 2) + gradient.shape[1:])
+    mine = own_bit(0)
+    return (take(pairs, 1, mine), take(pairs, 1, 1 - mine))
 
 
 def shards(
@@ -587,6 +859,7 @@
     gain_c, scale_c = (small_parts[1].reshape(C).astype(F32), small_parts[2].reshape(C).astype(F32))
     gain_a, gain_b = (small_parts[4].reshape(D).astype(F32), small_parts[5].reshape(D).astype(F32))
 
+    me = lax.axis_index("fsdp").astype(jnp.int32).reshape(1)
     def gathered(block):
         return lax.all_gather(block, "fsdp", axis=0, tiled=True)
 
@@ -597,92 +870,172 @@
     gate_out_all = vit_all[:, 5 * D :]
     up_all = gathered(w_up)
     down_all = gathered(w_down)
-    expand_all = gathered(jnp.concatenate((w_expand, w_adapt), axis=1))
-    adapt_all = expand_all[:, w_expand.shape[1] :]
-    shrink_all = gathered(w_shrink)
-
+    adapt_all = gathered(w_adapt)
     live = image_live.astype(F32)
     grad_joined_low = (grad_vit.astype(F32) * live).astype(BF16)
-
     patch_in = x_vit.astype(F32)
+
+    gatherer = Gatherer(devices)
+    expand_pieces = gatherer.weight(w_expand, [(0, D, 2 * D), (2 * D, 3 * D, 4 * D)])
+    conved = depthwise(after((x_hires,), gatherer.last)[0], seven_taps, KS, GRID_HR)
+    gatherer.ends.append(conved)
+    more_pieces = gatherer.weight(w_expand, [(4 * D, 5 * D, 6 * D)])
     normed_a, inverse_a = norm_rows(patch_in, 1e-05)
     normed_a_low = (normed_a * gain_a).astype(BF16)
+    normed_a_low = after((normed_a_low,), gatherer.last)[0]
     qkv_low = dot(normed_a_low, qkv_all, NN).astype(BF16)
     attended_low = attend(qkv_low)
+    gatherer.ends.append(attended_low)
+    shrink_pieces = gatherer.weight(w_shrink, [(0, C // 4, C // 2), (C // 2, 3 * C // 4, C)])
+    expand_pieces = tuple(one + two for one, two in zip(expand_pieces, more_pieces))
+
+    def shares(gradient):
+        return gradient.reshape(devices, gradient.shape[0] // devices, gradient.shape[1])
+
+    def split(gradient):
+        if len(gradient) == 2:
+            return tuple(gradient)
+        return halves(shares(gradient[0]), devices)
+
     resid_one = patch_in + dot(attended_low, out_all, NN)
     normed_b, inverse_b = norm_rows(resid_one, 1e-05)
     normed_b_low = (normed_b * gain_b).astype(BF16)
-    mlp_out, grad_b, d_up, d_down = mlp_both(grad_joined_low, normed_b_low, up_all, down_all, 1024)
+    normed_b_low = after((normed_b_low,), expand_pieces[1] + shrink_pieces[1])[0]
+    mlp_out, grad_b, d_up, d_down = mlp_both(
+        grad_joined_low, normed_b_low, up_all, down_all, me, devices, D
+    )
     resid_two = resid_one + mlp_out
     d_gain_two = jnp.sum(grad_b * normed_b, axis=0)
     grad_first = grad_joined_low.astype(F32) + norm_back(grad_b * gain_b, normed_b, inverse_b)
-    grad_first_low = grad_first.astype(BF16)
-    d_out = dot(attended_low, grad_first_low, TN).astype(BF16)
-    grad_att_low = dot(grad_first_low, out_all, NT).astype(BF16)
-    grad_qkv_low = jnp.concatenate(attend_back(qkv_low, grad_att_low), axis=1)
-    d_qkv = dot(normed_a_low, grad_qkv_low, TN).astype(BF16)
-    grad_a = dot(grad_qkv_low, qkv_all, NT)
-    d_gain_one = jnp.sum(grad_a * normed_a, axis=0)
-    grad_patches = grad_first + norm_back(grad_a * gain_a, normed_a, inverse_a)
-
-    conved = depthwise(x_hires, seven_taps, KS, GRID_HR)
+    ticks = Ticks()
+    sum_mlp = Scatterer(devices, split(d_up), split(d_down))
+
+    def attention_back(grad_first):
+        grad_first_low = grad_first.astype(BF16)
+        d_out = dot(attended_low, grad_first_low, TN).astype(BF16)
+        grad_att_low = dot(grad_first_low, out_all, NT).astype(BF16)
+        grad_qkv_low = jnp.concatenate(attend_back(qkv_low, grad_att_low), axis=1)
+        d_qkv = dot(normed_a_low, grad_qkv_low, TN).astype(BF16)
+        grad_a = dot(grad_qkv_low, qkv_all, NT)
+        d_gain_one = jnp.sum(grad_a * normed_a, axis=0)
+        grad_patches = grad_first + norm_back(grad_a * gain_a, normed_a, inverse_a)
+        return (grad_patches, d_gain_one, d_qkv, d_out)
+
+    grad_patches, d_gain_one, d_qkv, d_out = ticks.run([sum_mlp], grad_first, attention_back)
+    sum_attention = Scatterer(devices, split((d_qkv,)), split((d_out,)))
+
     normed_c, inverse_c = norm_rows(conved, 1e-06)
     normed_c_low = (normed_c * gain_c).astype(BF16)
-    activated, slope, shrunk = mlp_forward(normed_c_low, expand_all, shrink_all, 1024, 256)
-    hires_out = x_hires.astype(F32) + scale_c * shrunk
-    hires_next = (live * hires_out).astype(BF16)
+    tile = D
+    tiles = w_expand.shape[1] // tile
+
+    def network(field):
+        return mlp_forward(
+            field, expand_pieces, shrink_pieces, me, w_expand.shape[1], w_expand.shape[1], tile, 256
+        )
+
+    shrunk, activated, slope, expand_all, shrink_all = (
+        lambda outs: (outs[2], outs[0], outs[1], outs[3], outs[4])
+    )(ticks.run([sum_mlp, sum_attention], normed_c_low, network))
 
     table = pool_table(GRID_HR, GRID_LR)
     pool = jnp.einsum("ia,jb->ijab", table, table).reshape(GRID_LR**2, GRID_HR**2).astype(BF16)
-    pooled_low = dot(pool, hires_out.astype(BF16), NN).astype(BF16)
-    adapted = dot(pooled_low, adapt_all, NN)
-    mixed = depthwise(adapted, three_taps, KA, GRID_LR)
-    joined, grad_mixed, d_gate_in, d_gate_out = gate_both(
-        mixed, resid_two, grad_vit, image_live, gate_in_all, gate_out_all
+
+    def adapter(shrunk):
+        hires_out = x_hires.astype(F32) + scale_c * shrunk
+        pooled_low = dot(pool, hires_out.astype(BF16), NN).astype(BF16)
+        adapted = dot(pooled_low, adapt_all, NN)
+        mixed = depthwise(adapted, three_taps, KA, GRID_LR)
+        joined, grad_mixed, d_gate_in, d_gate_out = gate_both(
+            mixed, resid_two, grad_vit, image_live, gate_in_all, gate_out_all
+        )
+        hires_next = (live * hires_out).astype(BF16)
+        return (grad_mixed, d_gate_in, d_gate_out, joined, hires_next, pooled_low, adapted)
+
+    grad_mixed, d_gate_in, d_gate_out, joined, hires_next, pooled_low, adapted = ticks.run(
+        [sum_mlp, sum_attention], shrunk, adapter
     )
-    grad_adapted_low, d_conv_three = depthwise_back(
-        grad_mixed, adapted, jnp.zeros_like(adapted), three_taps, KA, GRID_LR, BF16
+
+    def adapter_back(grad_mixed):
+        grad_adapted_low, d_conv_three = depthwise_back(
+            grad_mixed, adapted, jnp.zeros(adapted.shape, BF16), three_taps, KA, GRID_LR, 0, D
+        )
+        d_adapt = dot(pooled_low, grad_adapted_low, TN).astype(BF16)
+        grad_pooled_low = dot(grad_adapted_low, adapt_all, NT).astype(BF16)
+        grad_hires_out = live * grad_hires.astype(F32) + dot(pool, grad_pooled_low, TN)
+        d_layer_scale = jnp.sum(grad_hires_out * shrunk, axis=0)
+        grad_shrunk_low = (grad_hires_out * scale_c).astype(BF16)
+        return (grad_shrunk_low, d_layer_scale, grad_hires_out, d_adapt, d_conv_three)
+
+    grad_shrunk_low, d_layer_scale, grad_hires_out, d_adapt, d_conv_three = ticks.run(
+        [sum_mlp, sum_attention], grad_mixed, adapter_back
     )
-    d_adapt = dot(pooled_low, grad_adapted_low, TN).astype(BF16)
-    grad_pooled_low = dot(grad_adapted_low, adapt_all, NT).astype(BF16)
-    grad_hires_out = live * grad_hires.astype(F32) + dot(pool, grad_pooled_low, TN)
-
-    d_layer_scale = jnp.sum(grad_hires_out * shrunk, axis=0)
-    grad_shrunk_low = (grad_hires_out * scale_c).astype(BF16)
-    d_shrink = outer_sum(activated, grad_shrunk_low, 512)
-    tile = 1024
-    tiles = activated.shape[1] // tile
-    grad_c, d_expand = mlp_back(
+    square = jnp.concatenate((shares(d_gate_in), shares(d_gate_out), shares(d_adapt)), axis=1)
+    sum_square = Scatterer(devices, halves(square, devices))
+
+    outs = ticks.run(
+        [sum_mlp, sum_attention, sum_square],
         grad_shrunk_low,
-        normed_c_low,
-        slope,
-        expand_all,
-        shrink_all,
-        jnp.zeros((x_hires.shape[0], C), F32),
-        tile,
-        256,
-        0,
-        tiles,
+        lambda grad: outer_sum(activated, grad, me, w_shrink.shape[0]),
     )
+    sum_shrink = Scatterer(devices, tuple(outs))
+    grad_c = jnp.zeros((x_hires.shape[0], C), F32)
+    beside = ([sum_attention, sum_square, sum_shrink], [sum_shrink], [sum_shrink, sum_square])
+    sums_expand = []
+    for part in range(3):
+        grad_c, *d_part = ticks.run(
+            list(beside[part]) + sums_expand[-1:],
+            grad_c,
+            lambda start, part=part: mlp_back(
+                grad_shrunk_low,
+                normed_c_low,
+                slope,
+                expand_all,
+                shrink_all,
+                start,
+                me,
+                devices,
+                tile,
+                256,
+                part * tiles // 3,
+                (part + 1) * tiles // 3,
+            ),
+        )
+        sums_expand.append(Scatterer(devices, split(d_part)))
     d_gain_three = jnp.sum(grad_c * normed_c, axis=0)
     grad_conved = norm_back(grad_c * gain_c, normed_c, inverse_c)
-    grad_hires_in, d_conv_seven = depthwise_back(
-        grad_conved, x_hires, grad_hires_out, seven_taps, KS, GRID_HR, F32
+    grad_hires_in = grad_hires_out
+    pieces_seven = []
+    width = C // 3
+    beside = (
+        [sum_shrink, sum_square, sums_expand[0], sums_expand[2]],
+        [sum_shrink, sums_expand[0], sums_expand[1]],
+        [sum_square, sums_expand[1], sums_expand[2]],
     )
-
-    def shares(gradient):
-        return gradient.reshape(devices, gradient.shape[0] // devices, gradient.shape[1])
-
-    g_down = scatter_weight(d_down, devices, 0)
-    g_up = scatter_weight(d_up, devices, 1)
-    g_square = scatter_weight(
-        jnp.concatenate((shares(d_out), shares(d_gate_in), shares(d_gate_out), shares(d_adapt)), axis=1).reshape(-1, D),
-        devices,
-        0,
-    )
-    g_qkv = scatter_weight(d_qkv, devices, 1)
-    g_shrink = scatter_weight(d_shrink, devices, 0)
-    g_expand = scatter_weight(d_expand, devices, 1)
+    for part in range(3):
+        grad_hires_in, taps_part = ticks.run(
+            beside[part],
+            grad_hires_in,
+            lambda base, part=part: depthwise_back(
+                grad_conved,
+                x_hires,
+                base,
+                seven_taps,
+                KS,
+                GRID_HR,
+                part * width,
+                (part + 1) * width,
+            ),
+        )
+        pieces_seven.append(taps_part)
+    d_conv_seven = jnp.concatenate(pieces_seven, axis=1)
+    ticks.finish([sum_mlp, sum_attention, sum_square, sum_shrink] + sums_expand)
+    g_up, g_down = sum_mlp.result
+    g_qkv, g_out = sum_attention.result
+    (g_square,) = sum_square.result
+    (g_shrink,) = sum_shrink.result
+    g_expand = jnp.concatenate([each.result[0] for each in sums_expand], axis=1)
+
     small_grads = jnp.concatenate(
         (
             d_conv_seven.reshape(KS * KS, devices, edge_c).swapaxes(0, 1).reshape(devices, -1),
@@ -694,7 +1047,10 @@
         ),
         axis=1,
     )
-    small_sums = scatter_sum(small_grads, scatter_orders(devices)[0], devices, F32)
+    small_sums = small_grads.reshape((2,) * (devices.bit_length() - 1) + small_grads.shape[1:])
+    held = list(range(devices.bit_length() - 2, -1, -1))
+    for bit in range(devices.bit_length() - 1):
+        small_sums, held = halved(small_sums, held, bit, devices)
     small_outs = [small_sums[marks[place] : marks[place + 1]] for place in range(6)]
     return (
         joined,
@@ -703,7 +1059,7 @@
         grad_hires_in,
         small_outs[4],
         g_qkv,
-        g_square[:edge_d],
+        g_out,
         small_outs[5],
         g_up,
         g_down,
@@ -712,10 +1068,10 @@
         g_expand,
         g_shrink,
         small_outs[2],
-        g_square[3 * edge_d :],
+        g_square[2 * edge_d :],
         small_outs[3].reshape(KA * KA, edge_d),
+        g_square[:edge_d],
         g_square[edge_d : 2 * edge_d],
-        g_square[2 * edge_d : 3 * edge_d],
     )
 
 

time: 1350 us -> 1150 us (0.85)
  waiting for transfers between devices: 532 us -> 233 us
  Pallas kernels: 386 us -> 428 us
  starting transfers between devices: 108 us -> 143 us
  other arithmetic: 107 us -> 131 us
    ppermute x95 -> x111, waiting for transfers between devices: 390 us -> 227 us  [swap(): lax.ppermute(block, 'fsdp', [(index, index ^ mask) for index in range(dev...]
    all_gather x5 -> x4, waiting for transfers between devices: 134 us -> 0.03 us  [gathered(): return lax.all_gather(block, 'fsdp', axis=0, tiled=True)]
    pallas_call x4 -> x6, Pallas kernels: 201 us -> 238 us  [the longest x3 107 us: mlp_back(): pl.pallas_call(functools.partial(mlp_back_kernel, step, share), grid=(las...]
    ppermute x95 -> x111, starting transfers between devices: 97.9 us -> 129 us  [swap(): lax.ppermute(block, 'fsdp', [(index, index ^ mask) for index in range(dev...]
    convert_element_type x72 -> x46, other arithmetic: 50.9 us -> 80 us  [the longest x43 75.6 us: receive(): parts = [total.astype(BF16) for total in totals]]
    unnamed x145 -> x364, local copies, waits for them, and re-layouts: 18.9 us -> 45.7 us
    squeeze x87 -> x26, local copies, waits for them, and re-layouts: 27.7 us -> 17.7 us  [take(): return lax.dynamic_index_in_dim(field, place, axis, keepdims=False)]
    pallas_call x2 -> x4, Pallas kernels: 85.4 us -> 90.5 us  [depthwise_back(): pl.pallas_call(functools.partial(depthwise_back_kernel, width, edge), gri...]
  transfers between devices with their start and end apart: 105 -> 120, of which waited for: 56 -> 35; matrix products, arithmetic and copies ran while one was open for 16% -> 19% of each run, Pallas kernels for 11% -> 33%
where the time goes in v2:
time: 1150 us; the launch traced here: 1140 us
  Pallas kernels  428 us (37%)
  waiting for transfers between devices  233 us (20%)
  starting transfers between devices  143 us (12%)
  local copies, waits for them, and re-layouts  137 us (12%)
  other arithmetic  131 us (11%)
  matrix products  55.1 us (5%)
  between operations  17.7 us (2%)
    ppermute x111, waiting for transfers between devices, swap(): lax.ppermute(block, 'fsdp', [(index, index ^ mask) for index in range(dev...  227 us
    ppermute x111, starting transfers between devices, swap(): lax.ppermute(block, 'fsdp', [(index, index ^ mask) for index in range(dev...  129 us
    pallas_call x3, Pallas kernels, mlp_back(): pl.pallas_call(functools.partial(mlp_back_kernel, step, share), grid=(las...  107 us
    pallas_call x4, Pallas kernels, depthwise_back(): pl.pallas_call(functools.partial(depthwise_back_kernel, width, edge), gri...  90.5 us
    convert_element_type x43, other arithmetic, receive(): parts = [total.astype(BF16) for total in totals]  75.6 us
    pallas_call x1, Pallas kernels, mlp_forward(): pl.pallas_call(functools.partial(mlp_forward_kernel, plan_in, plan_out, t...  62.2 us
    dot_general x10, matrix products, dot(): lax.dot_general(left, right, (dims, ((), ())), preferred_element_type=F32)  55.1 us
    unnamed x364, local copies, waits for them, and re-layouts  45.7 us
  transfers between devices with their start and end apart: 120, of which 35 were waited for; matrix products, arithmetic and copies ran while one was open for 19% of the time, Pallas kernels for 33%

profile of v2, /device:TPU:0, one launch (start us, length us, event | category | flops | bytes accessed | tf_op | source)
XLA Modules:
  0.0 1144.7 jit_solution(3032945692953759393)
XLA Ops:
  41.1 9.2 collective-permute-start.4
  51.1 10.7 collective-permute-start.10
  71.3 13.6 %collective-permute-done.11 = bf16[1,48,2048]{2,1,0:T(8,128)(2,1)S(1)} collective-permute-done((bf16[1,48,2048]{2,1,0:T(8,128)(2,1)S(1)}, bf16[1,48,2048]{2,1,0:T(8,128)(2,1)S(1)}, u32[]{:S(2)}, u32[]{:S(2)}) %collective-permute-start.11) | collective-permute-done | bytes 196640 | tf_op jit(solution)/shard_map/ppermute | solution.py:633
  119.0 36.5 %depthwise.2 = f32[1024,1536]{1,0:T(8,128)S(1)} custom-call(bf16[1024,1536]{1,0:T(8,128)(2,1)S(1)} %copy-done.2, bf16[49,1536]{1,0:T(8,128)(2,1)S(1)} %reshape.358.taps_ref), custom_call_target="tpu_custom_call" | custom-call | flops 46242201600 | bytes 12582912 | tf_op jit(solution)/shard_map/depthwise/pallas_call | solution.py:119
  180.4 22.0 %collective-permute-done.39 = bf16[1,192,768]{2,1,0:T(8,128)(2,1)S(1)} collective-permute-done((bf16[1,192,768]{2,1,0:T(8,128)(2,1)S(1)}, bf16[1,192,768]{2,1,0:T(8,128)(2,1)S(1)}, u32[]{:S(2)}, u32[]{:S(2)}) %collective-permute-start.39) | collective-permute-done | bytes 294944 | tf_op jit(solution)/shard_map/ppermute | solution.py:633
  209.5 15.3 %attend.1 = bf16[576,1024]{1,0:T(8,128)(2,1)S(1)} custom-call(bf16[576,3072]{1,0:T(8,128)(2,1)S(1)} %fusion.9.q_ref.k_ref.v_ref, bf16[576,3072]{1,0:T(8,128)(2,1)S(1)} %fusion.9.q_ref.k_ref.v_ref, bf16[576,3072]{1,0:T(8,128)(2,1)S(1)} %fusion.9.q_ref.k_ref.v_ref), custom_call_target="tpu_custom_call" | custom-call | flops 13589544960 | bytes 4718592 | tf_op jit(solution)/shard_map/attend/pallas_call | solution.py:236
  226.1 12.6 %collective-permute-done.45 = bf16[4,192,384]{2,1,0:T(8,128)(2,1)S(1)} collective-permute-done((bf16[4,192,384]{2,1,0:T(8,128)(2,1)S(1)}, bf16[4,192,384]{2,1,0:T(8,128)(2,1)S(1)}, u32[]{:S(2)}, u32[]{:S(2)}) %collective-permute-start.45) | collective-permute-done | bytes 589856 | tf_op jit(solution)/shard_map/ppermute | solution.py:633
  239.0 10.9 collective-permute-start.49
  257.9 8.8 collective-permute-done.49
  266.7 11.5 %collective-permute-done.50 = bf16[1,192,768]{2,1,0:T(8,128)(2,1)S(1)} collective-permute-done((bf16[1,192,768]{2,1,0:T(8,128)(2,1)S(1)}, bf16[1,192,768]{2,1,0:T(8,128)(2,1)S(1)}, u32[]{:S(2)}, u32[]{:S(2)}) %collective-permute-start.50) | collective-permute-done | bytes 294944 | tf_op jit(solution)/shard_map/ppermute | solution.py:633
  285.1 7.8 convert_element_type.693
  322.6 26.6 %collective-permute-done.57.refs_37_ = bf16[8,192,384]{2,1,0:T(8,128)(2,1)S(1)} collective-permute-done((bf16[8,192,384]{2,1,0:T(8,128)(2,1)S(1)}, bf16[8,192,384]{2,1,0:T(8,128)(2,1)S(1)}, u32[]{:S(2)}, u32[]{:S(2)}) %collective-permute-start.57) | collective-permute-done | bytes 1179680 | tf_op jit(solution)/shard_map/ppermute | solution.py:633
  359.0 43.1 %mlp_both.1 = (f32[576,1024]{1,0:T(8,128)}, f32[576,1024]{1,0:T(8,128)}, bf16[16,32,4096]{2,1,0:T(8,128)(2,1)}, bf16[16,32,4096]{2,1,0:T(8,128)(2,1)}, bf16[16,1...) custom-call(s32[1]{0:T(128)} %bitcast.1.me_ref, bf16[576,1024]{1,0:T(8,128)(2,1)} %multiply_convert_fusion.5.g_ref, ...), custom_call_target="tpu_custom_call" | custom-call | flops 33822867456 | bytes 33554432 | tf_op jit(solution)/shard_map/mlp_both/pallas_call | solution.py:357
  412.4 27.4 %attend_back.1 = (bf16[576,1024]{1,0:T(8,128)(2,1)S(1)}, bf16[576,1024]{1,0:T(8,128)(2,1)S(1)}, bf16[576,1024]{1,0:T(8,128)(2,1)S(1)}) custom-call(bf16[576,3072]{1,0:T(8,128)(2,1)} %copy-done.13, bf16[576,3072]{1,0:T(8,128)(2,1)} %copy-done.13, bf16[576,3072]{1,0:T(8,128)(2,1)} %copy-done.13, bf16[576,1024]{1,0:T(8,128)(2,1)S(1)} %fusion.58.g_ref), custom_call_target="tpu_custom_call" | custom-call | flops 23781703680 | bytes 8257536 | tf_op jit(solution)/shard_map/attend_back/pallas_call | solution.py:273
  483.7 62.2 %mlp_forward.1 = (bf16[1024,6144]{1,0:T(8,128)(2,1)}, bf16[1024,6144]{1,0:T(8,128)(2,1)}, f32[1024,1536]{1,0:T(8,128)}, bf16[1536,6144]{1,0:T(8,128)(2,1)}, bf16[6144,1536]{1,0:T(8,128)(2,1)}) custom-call(s32[1]{0:T(128)} %bitcast.1.me_ref, bf16[1024,1536]{1,0:T(8,128)(2,1)} %multiply_convert_fusion.3.h_ref, bf16[8,48,1024]{2,1,0:T(8,128)(2,1)} %copy-done.119, ...), custom_call_target="tpu_custom_call" | custom-call | flops 67645734912 | bytes 100663296 | tf_op jit(solution)/shard_map/mlp_forward/pallas_call | solution.py:450
  586.3 14.5 %gate_both.1 = (bf16[576,1024]{1,0:T(8,128)(2,1)}, f32[576,1024]{1,0:T(8,128)}, bf16[1024,1024]{1,0:T(8,128)(2,1)}, bf16[1024,1024]{1,0:T(8,128)(2,1)}) custom-call(f32[576,1024]{1,0:T(8,128)} %copy-done.12, f32[576,1024]{1,0:T(8,128)} %get-tuple-element.495.resid_ref, bf16[576,1024]{1,0:T(8,128)(2,1)} %gv_ref.1, s32[1]{0:T(128)S(6)} %copy.251.live_ref, ...), custom_call_target="tpu_custom_call" | custom-call | flops 12079595520 | bytes 17694720 | tf_op jit(solution)/shard_map/gate_both/pallas_call | solution.py:588
  600.8 13.6 %collective-permute-done.68 = bf16[2,2,2,128,512]{4,3,1,0,2:T(8,128)(2,1)} collective-permute-done((bf16[2,2,2,128,512]{4,3,1,0,2:T(8,128)(2,1)}, bf16[2,2,2,128,512]{4,3,1,0,2:T(8,128)(2,1)}, u32[]{:S(2)}, u32[]{:S(2)}) %collective-permute-start.68) | collective-permute-done | bytes 1048608 | tf_op jit(solution)/shard_map/ppermute | solution.py:633
  628.9 11.1 depthwise_back.4
  639.9 11.9 %multiply_reduce_fusion.2 = (f32[1536]{0:T(1024)S(1)}, bf16[1024,1536]{1,0:T(8,128)(2,1)}, f32[1024,1536]{1,0:T(8,128)}) fusion(f32[1024,1536]{1,0:T(8,128)} %get-tuple-element.262, f32[1536]{0:T(1024)S(1)} %copy-done.116, bf16[576,1024]{1,0:T(8,128)(2,1)} %convert_element_type.693, bf16[576,1024]{1,0:T(8,128)(2,1)S(1)} %get-tuple-element.281, ...), kind=kOutput, calls=%fused_computation.15 | convolution fusion | flops 3635771904 | bytes 24391684 | tf_op jit(solution)/shard_map/dot_general | solution.py:28
  668.6 25.7 %outer_sum.1 = (bf16[16,192,1536]{2,1,0:T(8,128)(2,1)}, bf16[16,192,1536]{2,1,0:T(8,128)(2,1)}) custom-call(s32[1]{0:T(128)} %bitcast.1.me_ref, bf16[1024,6144]{1,0:T(8,128)(2,1)} %get-tuple-element.261.left_ref, bf16[1024,1536]{1,0:T(8,128)(2,1)S(1)} %copy-done.6), custom_call_target="tpu_custom_call" | custom-call | flops 28991029248 | bytes 18874368 | tf_op jit(solution)/shard_map/outer_sum/pallas_call | solution.py:484
  713.6 35.5 %mlp_back.3 = (f32[1024,1536]{1,0:T(8,128)}, bf16[16,48,2048]{2,1,0:T(8,128)(2,1)}, bf16[16,48,2048]{2,1,0:T(8,128)(2,1)}) custom-call(s32[1]{0:T(128)} %bitcast.1.me_ref, bf16[1024,1536]{1,0:T(8,128)(2,1)} %get-tuple-element.297.right_ref.g_ref, bf16[1024,1536]{1,0:T(8,128)(2,1)} %multiply_convert_fusion.3.h_ref, ...), custom_call_target="tpu_custom_call" | custom-call | flops 22548578304 | bytes 18874368 | tf_op jit(solution)/shard_map/mlp_back/pallas_call | solution.py:545
  752.0 8.0 add_convert_fusion
  782.4 35.5 %mlp_back.4 = (f32[1024,1536]{1,0:T(8,128)}, bf16[16,48,2048]{2,1,0:T(8,128)(2,1)}, bf16[16,48,2048]{2,1,0:T(8,128)(2,1)}) custom-call(s32[1]{0:T(128)} %bitcast.1.me_ref, bf16[1024,1536]{1,0:T(8,128)(2,1)} %get-tuple-element.297.right_ref.g_ref, bf16[1024,1536]{1,0:T(8,128)(2,1)} %multiply_convert_fusion.3.h_ref, ...), custom_call_target="tpu_custom_call" | custom-call | flops 22548578304 | bytes 18874368 | tf_op jit(solution)/shard_map/mlp_back/pallas_call | solution.py:545
  817.9 10.2 collective-permute-done.80
  841.0 35.9 %mlp_back.5 = (f32[1024,1536]{1,0:T(8,128)}, bf16[16,48,2048]{2,1,0:T(8,128)(2,1)}, bf16[16,48,2048]{2,1,0:T(8,128)(2,1)}) custom-call(s32[1]{0:T(128)} %bitcast.1.me_ref, bf16[1024,1536]{1,0:T(8,128)(2,1)} %get-tuple-element.297.right_ref.g_ref, bf16[1024,1536]{1,0:T(8,128)(2,1)} %multiply_convert_fusion.3.h_ref, ...), custom_call_target="tpu_custom_call" | custom-call | flops 22548578304 | bytes 18874368 | tf_op jit(solution)/shard_map/mlp_back/pallas_call | solution.py:545
  903.7 27.1 %depthwise_back.5 = (f32[1024,1536]{1,0:T(8,128)}, f32[49,512]{1,0:T(8,128)S(1)}) custom-call(f32[1024,1536]{1,0:T(8,128)S(1)} %subtract_multiply_fusion.grad_ref, bf16[1024,1536]{1,0:T(8,128)(2,1)S(1)} %copy-done.4, f32[1024,1536]{1,0:T(8,128)} %get-tuple-element.349.base_ref, bf16[49,1536]{1,0:T(8,128)(2,1)S(1)} %reshape.358.taps_ref), custom_call_target="tpu_custom_call", output_to_operand_aliasing={{0}: (2, {})} | custom-call | flops 30828134400 | bytes 7340032 | tf_op jit(solution)/shard_map/depthwise_back/pallas_call | solution.py:190
  945.0 26.4 %depthwise_back.6 = (f32[1024,1536]{1,0:T(8,128)}, f32[49,512]{1,0:T(8,128)S(1)}) custom-call(f32[1024,1536]{1,0:T(8,128)S(1)} %bitcast.359, bf16[1024,1536]{1,0:T(8,128)(2,1)S(1)} %copy-done.5, f32[1024,1536]{1,0:T(8,128)} %get-tuple-element.363.base_ref, bf16[49,1536]{1,0:T(8,128)(2,1)S(1)} %reshape.358.taps_ref), custom_call_target="tpu_custom_call", output_to_operand_aliasing={{0}: (2, {})} | custom-call | flops 30828134400 | bytes 7340032 | tf_op jit(solution)/shard_map/depthwise_back/pallas_call | solution.py:190
  985.9 13.8 %collective-permute-done.94 = bf16[2,2,48,1024]{3,2,0,1:T(8,128)(2,1)S(1)} collective-permute-done((bf16[2,2,48,1024]{3,2,0,1:T(8,128)(2,1)S(1)}, bf16[2,2,48,1024]{3,2,0,1:T(8,128)(2,1)S(1)}, u32[]{:S(2)}, u32[]{:S(2)}) %collective-permute-start.94) | collective-permute-done | bytes 393248 | tf_op jit(solution)/shard_map/ppermute | solution.py:633
  1005.4 26.0 %depthwise_back.7 = (f32[1024,1536]{1,0:T(8,128)}, f32[49,512]{1,0:T(8,128)S(1)}) custom-call(f32[1024,1536]{1,0:T(8,128)S(1)} %bitcast.359, bf16[1024,1536]{1,0:T(8,128)(2,1)S(1)} %copy-done.5, f32[1024,1536]{1,0:T(8,128)} %get-tuple-element.377.base_ref, bf16[49,1536]{1,0:T(8,128)(2,1)S(1)} %reshape.358.taps_ref), custom_call_target="tpu_custom_call", output_to_operand_aliasing={{0}: (2, {})} | custom-call | flops 30828134400 | bytes 7340032 | tf_op jit(solution)/shard_map/depthwise_back/pallas_call | solution.py:190
  1037.8 9.0 collective-permute-done.98
  1046.7 11.6 %collective-permute-done.100 = bf16[2,2,48,1024]{3,2,0,1:T(8,128)(2,1)S(1)} collective-permute-done((bf16[2,2,48,1024]{3,2,0,1:T(8,128)(2,1)S(1)}, bf16[2,2,48,1024]{3,2,0,1:T(8,128)(2,1)S(1)}, u32[]{:S(2)}, u32[]{:S(2)}) %collective-permute-start.100) | collective-permute-done | bytes 393248 | tf_op jit(solution)/shard_map/ppermute | solution.py:633
  1111.7 13.8 %collective-permute-done.112 = bf16[48,2048]{1,0:T(8,128)(2,1)S(1)} collective-permute-done((bf16[48,2048]{1,0:T(8,128)(2,1)S(1)}, bf16[48,2048]{1,0:T(8,128)(2,1)S(1)}, u32[]{:S(2)}, u32[]{:S(2)}) %collective-permute-start.112) | collective-permute-done | bytes 196640 | tf_op jit(solution)/shard_map/ppermute | solution.py:633
  (849 shorter events, 479.3 us)
Async XLA Ops:
  7.3 195.3 %all-gather.5.cloned.1.call-start = ((), (), s32[]{:S(2)}) async-start(), calls=%async_computation | async-start | bytes 12976128 | tf_op jit(solution)/shard_map/all_gather | solution.py:864
  9.3 349.8 %all-gather.7.cloned.1.call-start = ((), (), s32[]{:S(2)}) async-start(), calls=%async_computation.1 | async-start | bytes 8650752 | tf_op jit(solution)/shard_map/all_gather | solution.py:864
  10.0 349.0 %all-gather.9.cloned.1.call-start = ((), (), s32[]{:S(2)}) async-start(), calls=%async_computation.2 | async-start | bytes 8650752 | tf_op jit(solution)/shard_map/all_gather | solution.py:864
  10.8 564.2 %all-gather.11.cloned.1.call-start = ((), (), s32[]{:S(2)}) async-start(), calls=%async_computation.3 | async-start | bytes 3244032 | tf_op jit(solution)/shard_map/all_gather | solution.py:864
  41.1 48.7 %collective-permute-start.4 = (bf16[16,2800]{1,0:T(8,128)(2,1)S(1)}, bf16[16,2800]{1,0:T(8,128)(2,1)S(1)}, u32[]{:S(2)}, u32[]{:S(2)}) collective-permute-start(bf16[16,2800]{1,0:T(8,128)(2,1)S(1)} %maximum_select_fusion.1), channel_id=1, source_target_pairs={{0,16},{1,17},{2,18},{3,19},{4,20},{5,21},{6,22},{7,23},{8,24},{9,... | collective-permute-start | bytes 268808 | tf_op jit(solution)/shard_map/ppermute | solution.py:615
  106.1 52.2 %collective-permute-start.17 = (bf16[1,48,2048]{2,1,0:T(8,128)(2,1)S(1)}, bf16[1,48,2048]{2,1,0:T(8,128)(2,1)S(1)}, u32[]{:S(2)}, u32[]{:S(2)}) collective-permute-start(bf16[1,48,2048]{2,1,0:T(8,128)(2,1)S(1)} %copy-done.85), channel_id=1, source_target_pairs={{0,8},{1,9},{2,10},{3,11},{4,12},{5,13},{6,14},{7,15},{8,0},{9,1},... | collective-permute-start | bytes 589832 | tf_op jit(solution)/shard_map/ppermute | solution.py:633
  110.3 48.0 %collective-permute-start.18 = (bf16[1,48,2048]{2,1,0:T(8,128)(2,1)S(1)}, bf16[1,48,2048]{2,1,0:T(8,128)(2,1)S(1)}, u32[]{:S(2)}, u32[]{:S(2)}) collective-permute-start(bf16[1,48,2048]{2,1,0:T(8,128)(2,1)S(1)} %copy-done.85), channel_id=1, source_target_pairs={{0,16},{1,17},{2,18},{3,19},{4,20},{5,21},{6,22},{7,23},{8,24},{9,... | collective-permute-start | bytes 589832 | tf_op jit(solution)/shard_map/ppermute | solution.py:633
  114.1 44.3 %collective-permute-start.19 = (bf16[1,48,2048]{2,1,0:T(8,128)(2,1)S(1)}, bf16[1,48,2048]{2,1,0:T(8,128)(2,1)S(1)}, u32[]{:S(2)}, u32[]{:S(2)}) collective-permute-start(bf16[1,48,2048]{2,1,0:T(8,128)(2,1)S(1)} %copy-done.85), channel_id=1, source_target_pairs={{0,24},{1,25},{2,26},{3,27},{4,28},{5,29},{6,30},{7,31},{8,16},{9,... | collective-permute-start | bytes 589832 | tf_op jit(solution)/shard_map/ppermute | solution.py:633
  114.2 44.4 %collective-permute-start.21 = (bf16[8,48,1024]{2,1,0:T(8,128)(2,1)}, bf16[8,48,1024]{2,1,0:T(8,128)(2,1)}, u32[]{:S(2)}, u32[]{:S(2)}) collective-permute-start(bf16[8,48,1024]{2,1,0:T(8,128)(2,1)} %constant_dynamic-update-slice_fusion.12.refs_12_), channel_id=1, source_target_pairs={{0,2},{1,3},{2,0},{3,1},{4,6},{5,7},{6,4},{7,5},{8,10},{9,11},{10,... | collective-permute-start | bytes 2359304 | tf_op jit(solution)/shard_map/ppermute | solution.py:633
  169.3 83.9 %collective-permute-start.26 = (bf16[8,48,1024]{2,1,0:T(8,128)(2,1)}, bf16[8,48,1024]{2,1,0:T(8,128)(2,1)}, u32[]{:S(2)}, u32[]{:S(2)}) collective-permute-start(bf16[8,48,1024]{2,1,0:T(8,128)(2,1)} %constant_dynamic-update-slice_fusion.5.refs_4_), channel_id=1, source_target_pairs={{0,1},{1,0},{2,3},{3,2},{4,5},{5,4},{6,7},{7,6},{8,9},{9,8},{10,11... | collective-permute-start | bytes 2359304 | tf_op jit(solution)/shard_map/ppermute | solution.py:633
  173.3 51.5 %collective-permute-start.35 = (bf16[8,48,1024]{2,1,0:T(8,128)(2,1)}, bf16[8,48,1024]{2,1,0:T(8,128)(2,1)}, u32[]{:S(2)}, u32[]{:S(2)}) collective-permute-start(bf16[8,48,1024]{2,1,0:T(8,128)(2,1)} %constant_dynamic-update-slice_fusion.16.refs_20_), channel_id=1, source_target_pairs={{0,2},{1,3},{2,0},{3,1},{4,6},{5,7},{6,4},{7,5},{8,10},{9,11},{10,... | collective-permute-start | bytes 2359304 | tf_op jit(solution)/shard_map/ppermute | solution.py:633
  180.3 44.5 %collective-permute-start.32 = (bf16[8,48,1024]{2,1,0:T(8,128)(2,1)}, bf16[8,48,1024]{2,1,0:T(8,128)(2,1)}, u32[]{:S(2)}, u32[]{:S(2)}) collective-permute-start(bf16[8,48,1024]{2,1,0:T(8,128)(2,1)} %constant_dynamic-update-slice_fusion.14.refs_16_), channel_id=1, source_target_pairs={{0,4},{1,5},{2,6},{3,7},{4,0},{5,1},{6,2},{7,3},{8,12},{9,13},{10,... | collective-permute-start | bytes 2359304 | tf_op jit(solution)/shard_map/ppermute | solution.py:633
  405.5 55.5 %collective-permute-start.60 = (bf16[16,32,4096]{2,1,0:T(8,128)(2,1)}, bf16[16,32,4096]{2,1,0:T(8,128)(2,1)}, u32[]{:S(2)}, u32[]{:S(2)}) collective-permute-start(bf16[16,32,4096]{2,1,0:T(8,128)(2,1)} %get-tuple-element.238), channel_id=1, source_target_pairs={{0,1},{1,0},{2,3},{3,2},{4,5},{5,4},{6,7},{7,6},{8,9},{9,8},{10,11... | collective-permute-start | bytes 12582920 | tf_op jit(solution)/shard_map/ppermute | solution.py:633
  405.6 55.4 %collective-permute-start.61 = (bf16[16,128,1024]{2,1,0:T(8,128)(2,1)}, bf16[16,128,1024]{2,1,0:T(8,128)(2,1)}, u32[]{:S(2)}, u32[]{:S(2)}) collective-permute-start(bf16[16,128,1024]{2,1,0:T(8,128)(2,1)} %get-tuple-element.239), channel_id=1, source_target_pairs={{0,1},{1,0},{2,3},{3,2},{4,5},{5,4},{6,7},{7,6},{8,9},{9,8},{10,11... | collective-permute-start | bytes 12582920 | tf_op jit(solution)/shard_map/ppermute | solution.py:633
  481.5 64.4 %collective-permute-start.64 = (bf16[16,32,3072]{2,1,0:T(8,128)(2,1)}, bf16[16,32,3072]{2,1,0:T(8,128)(2,1)}, u32[]{:S(2)}, u32[]{:S(2)}) collective-permute-start(bf16[16,32,3072]{2,1,0:T(8,128)(2,1)} %dynamic-slice_bitcast_fusion.1), channel_id=1, source_target_pairs={{0,1},{1,0},{2,3},{3,2},{4,5},{5,4},{6,7},{7,6},{8,9},{9,8},{10,11... | collective-permute-start | bytes 9437192 | tf_op jit(solution)/shard_map/ppermute | solution.py:633
  481.6 64.3 %collective-permute-start.62 = (bf16[2,2,2,256,512]{4,3,0,1,2:T(8,128)(2,1)}, bf16[2,2,2,256,512]{4,3,0,1,2:T(8,128)(2,1)}, u32[]{:S(2)}, u32[]{:S(2)}) collective-permute-start(bf16[2,2,2,256,512]{4,3,0,1,2:T(8,128)(2,1)} %bitcast.339), channel_id=1, source_target_pairs={{0,4},{1,5},{2,6},{3,7},{4,0},{5,1},{6,2},{7,3},{8,12},{9,13},{10,... | collective-permute-start | bytes 6291464 | tf_op jit(solution)/shard_map/ppermute | solution.py:633
  483.1 62.8 %collective-permute-start.63 = (bf16[2,2,2,256,512]{4,3,0,1,2:T(8,128)(2,1)}, bf16[2,2,2,256,512]{4,3,0,1,2:T(8,128)(2,1)}, u32[]{:S(2)}, u32[]{:S(2)}) collective-permute-start(bf16[2,2,2,256,512]{4,3,0,1,2:T(8,128)(2,1)} %bitcast.338), channel_id=1, source_target_pairs={{0,2},{1,3},{2,0},{3,1},{4,6},{5,7},{6,4},{7,5},{8,10},{9,11},{10,... | collective-permute-start | bytes 6291464 | tf_op jit(solution)/shard_map/ppermute | solution.py:633
  483.7 62.2 %collective-permute-start.65 = (bf16[16,32,1024]{2,1,0:T(8,128)(2,1)}, bf16[16,32,1024]{2,1,0:T(8,128)(2,1)}, u32[]{:S(2)}, u32[]{:S(2)}) collective-permute-start(bf16[16,32,1024]{2,1,0:T(8,128)(2,1)} %dynamic-slice_bitcast_fusion.7), channel_id=1, source_target_pairs={{0,1},{1,0},{2,3},{3,2},{4,5},{5,4},{6,7},{7,6},{8,9},{9,8},{10,11... | collective-permute-start | bytes 3145736 | tf_op jit(solution)/shard_map/ppermute | solution.py:633
  566.9 47.5 %collective-permute-start.68 = (bf16[2,2,2,128,512]{4,3,1,0,2:T(8,128)(2,1)}, bf16[2,2,2,128,512]{4,3,1,0,2:T(8,128)(2,1)}, u32[]{:S(2)}, u32[]{:S(2)}) collective-permute-start(bf16[2,2,2,128,512]{4,3,1,0,2:T(8,128)(2,1)} %bitcast.340), channel_id=1, source_target_pairs={{0,4},{1,5},{2,6},{3,7},{4,0},{5,1},{6,2},{7,3},{8,12},{9,13},{10,... | collective-permute-start | bytes 3145736 | tf_op jit(solution)/shard_map/ppermute | solution.py:633
  568.4 46.1 %collective-permute-start.69 = (bf16[2,2,2,128,512]{4,3,2,1,0:T(8,128)(2,1)}, bf16[2,2,2,128,512]{4,3,2,1,0:T(8,128)(2,1)}, u32[]{:S(2)}, u32[]{:S(2)}) collective-permute-start(bf16[2,2,2,128,512]{4,3,2,1,0:T(8,128)(2,1)} %dynamic-slice_bitcast_fusion.4), channel_id=1, source_target_pairs={{0,2},{1,3},{2,0},{3,1},{4,6},{5,7},{6,4},{7,5},{8,10},{9,11},{10,... | collective-permute-start | bytes 3145736 | tf_op jit(solution)/shard_map/ppermute | solution.py:633
  704.5 46.5 %collective-permute-start.79 = (bf16[16,192,1536]{2,1,0:T(8,128)(2,1)}, bf16[16,192,1536]{2,1,0:T(8,128)(2,1)}, u32[]{:S(2)}, u32[]{:S(2)}) collective-permute-start(bf16[16,192,1536]{2,1,0:T(8,128)(2,1)} %get-tuple-element.314), channel_id=1, source_target_pairs={{0,1},{1,0},{2,3},{3,2},{4,5},{5,4},{6,7},{7,6},{8,9},{9,8},{10,11... | collective-permute-start | bytes 28311560 | tf_op jit(solution)/shard_map/ppermute | solution.py:633
  707.6 43.5 %collective-permute-start.77 = (bf16[2,2,2,112,512]{4,3,1,0,2:T(8,128)(2,1)}, bf16[2,2,2,112,512]{4,3,1,0,2:T(8,128)(2,1)}, u32[]{:S(2)}, u32[]{:S(2)}) collective-permute-start(bf16[2,2,2,112,512]{4,3,1,0,2:T(8,128)(2,1)} %bitcast.341), channel_id=1, source_target_pairs={{0,4},{1,5},{2,6},{3,7},{4,0},{5,1},{6,2},{7,3},{8,12},{9,13},{10,... | collective-permute-start | bytes 2752520 | tf_op jit(solution)/shard_map/ppermute | solution.py:633
  708.2 42.9 %collective-permute-start.78 = (bf16[2,2,2,112,512]{4,3,2,1,0:T(8,128)(2,1)}, bf16[2,2,2,112,512]{4,3,2,1,0:T(8,128)(2,1)S(1)}, u32[]{:S(2)}, u32[]{:S(2)}) collective-permute-start(bf16[2,2,2,112,512]{4,3,2,1,0:T(8,128)(2,1)} %dynamic-slice_bitcast_fusion.8), channel_id=1, source_target_pairs={{0,2},{1,3},{2,0},{3,1},{4,6},{5,7},{6,4},{7,5},{8,10},{9,11},{10,... | collective-permute-start | bytes 2752520 | tf_op jit(solution)/shard_map/ppermute | solution.py:633
  709.7 41.4 %collective-permute-start.76 = (bf16[128,1024]{1,0:T(8,128)(2,1)}, bf16[128,1024]{1,0:T(8,128)(2,1)}, u32[]{:S(2)}, u32[]{:S(2)}) collective-permute-start(bf16[128,1024]{1,0:T(8,128)(2,1)} %dynamic-slice_bitcast_fusion.21), channel_id=1, source_target_pairs={{0,16},{1,17},{2,18},{3,19},{4,20},{5,21},{6,22},{7,23},{8,24},{9,... | collective-permute-start | bytes 786440 | tf_op jit(solution)/shard_map/ppermute | solution.py:633
  774.1 54.3 %collective-permute-start.82 = (bf16[16,48,2048]{2,1,0:T(8,128)(2,1)}, bf16[16,48,2048]{2,1,0:T(8,128)(2,1)}, u32[]{:S(2)}, u32[]{:S(2)}) collective-permute-start(bf16[16,48,2048]{2,1,0:T(8,128)(2,1)} %get-tuple-element.324), channel_id=1, source_target_pairs={{0,1},{1,0},{2,3},{3,2},{4,5},{5,4},{6,7},{7,6},{8,9},{9,8},{10,11... | collective-permute-start | bytes 9437192 | tf_op jit(solution)/shard_map/ppermute | solution.py:633
  774.1 54.0 %collective-permute-start.80 = (bf16[2,2,2,192,768]{4,3,0,1,2:T(8,128)(2,1)}, bf16[2,2,2,192,768]{4,3,0,1,2:T(8,128)(2,1)}, u32[]{:S(2)}, u32[]{:S(2)}) collective-permute-start(bf16[2,2,2,192,768]{4,3,0,1,2:T(8,128)(2,1)} %bitcast.337), channel_id=1, source_target_pairs={{0,4},{1,5},{2,6},{3,7},{4,0},{5,1},{6,2},{7,3},{8,12},{9,13},{10,... | collective-permute-start | bytes 7077896 | tf_op jit(solution)/shard_map/ppermute | solution.py:633
  774.7 53.7 %collective-permute-start.81 = (bf16[2,2,2,192,768]{4,3,0,1,2:T(8,128)(2,1)}, bf16[2,2,2,192,768]{4,3,0,1,2:T(8,128)(2,1)}, u32[]{:S(2)}, u32[]{:S(2)}) collective-permute-start(bf16[2,2,2,192,768]{4,3,0,1,2:T(8,128)(2,1)} %bitcast.336), channel_id=1, source_target_pairs={{0,2},{1,3},{2,0},{3,1},{4,6},{5,7},{6,4},{7,5},{8,10},{9,11},{10,... | collective-permute-start | bytes 7077896 | tf_op jit(solution)/shard_map/ppermute | solution.py:633
  836.9 48.6 %collective-permute-start.87 = (bf16[16,48,2048]{2,1,0:T(8,128)(2,1)}, bf16[16,48,2048]{2,1,0:T(8,128)(2,1)}, u32[]{:S(2)}, u32[]{:S(2)}) collective-permute-start(bf16[16,48,2048]{2,1,0:T(8,128)(2,1)} %get-tuple-element.339), channel_id=1, source_target_pairs={{0,1},{1,0},{2,3},{3,2},{4,5},{5,4},{6,7},{7,6},{8,9},{9,8},{10,11... | collective-permute-start | bytes 9437192 | tf_op jit(solution)/shard_map/ppermute | solution.py:633
  836.9 48.6 %collective-permute-start.83 = (bf16[2,2,192,768]{3,2,0,1:T(8,128)(2,1)}, bf16[2,2,192,768]{3,2,0,1:T(8,128)(2,1)}, u32[]{:S(2)}, u32[]{:S(2)}) collective-permute-start(bf16[2,2,192,768]{3,2,0,1:T(8,128)(2,1)} %dynamic-slice_bitcast_fusion.3), channel_id=1, source_target_pairs={{0,2},{1,3},{2,0},{3,1},{4,6},{5,7},{6,4},{7,5},{8,10},{9,11},{10,... | collective-permute-start | bytes 3538952 | tf_op jit(solution)/shard_map/ppermute | solution.py:633
  838.3 47.2 %collective-permute-start.84 = (bf16[2,2,192,768]{3,2,0,1:T(8,128)(2,1)}, bf16[2,2,192,768]{3,2,0,1:T(8,128)(2,1)}, u32[]{:S(2)}, u32[]{:S(2)}) collective-permute-start(bf16[2,2,192,768]{3,2,0,1:T(8,128)(2,1)} %dynamic-slice_bitcast_fusion.2), channel_id=1, source_target_pairs={{0,4},{1,5},{2,6},{3,7},{4,0},{5,1},{6,2},{7,3},{8,12},{9,13},{10,... | collective-permute-start | bytes 3538952 | tf_op jit(solution)/shard_map/ppermute | solution.py:633
  839.0 46.6 %collective-permute-start.85 = (bf16[2,2,112,512]{3,2,1,0:T(8,128)(2,1)}, bf16[2,2,112,512]{3,2,1,0:T(8,128)(2,1)}, u32[]{:S(2)}, u32[]{:S(2)}) collective-permute-start(bf16[2,2,112,512]{3,2,1,0:T(8,128)(2,1)} %dynamic-slice_bitcast_fusion.14), channel_id=1, source_target_pairs={{0,2},{1,3},{2,0},{3,1},{4,6},{5,7},{6,4},{7,5},{8,10},{9,11},{10,... | collective-permute-start | bytes 1376264 | tf_op jit(solution)/shard_map/ppermute | solution.py:633
  840.4 45.1 %collective-permute-start.86 = (bf16[2,2,112,512]{3,2,1,0:T(8,128)(2,1)S(1)}, bf16[2,2,112,512]{3,2,1,0:T(8,128)(2,1)}, u32[]{:S(2)}, u32[]{:S(2)}) collective-permute-start(bf16[2,2,112,512]{3,2,1,0:T(8,128)(2,1)S(1)} %copy-done.98), channel_id=1, source_target_pairs={{0,4},{1,5},{2,6},{3,7},{4,0},{5,1},{6,2},{7,3},{8,12},{9,13},{10,... | collective-permute-start | bytes 1376264 | tf_op jit(solution)/shard_map/ppermute | solution.py:633
  (254 other events, 3314.3 us)
Sparse Core Ops, SparseCore 0:
  11.5 133.6 all-gather.4
  148.1 90.7 all-gather.6
  241.8 102.6 all-gather.8
  347.2 58.0 all-gather.10

commit v3 on v2

--- a/solution.py
+++ b/solution.py
@@ -372,36 +372,31 @@
     return (outs[0], outs[1], outs[2:-2], outs[-2:])
 
 
-def mlp_forward_kernel(plan_in, plan_out, tile, tiles, rows, me_ref, h_ref, *refs):
-    count = len(plan_in)
-    sources_in, sources_out = (refs[:count], refs[count : count + len(plan_out)])
-    act_ref, slope_ref, out_ref, wi_natural, wo_natural, wi_two, wo_all, sems = refs[
-        count + len(plan_out) :
-    ]
+def expand_kernel(plan, tile, tiles, rows, me_ref, h_ref, *refs):
+    sources = refs[: len(plan)]
+    act_ref, slope_ref, natural, weights, sems = refs[len(plan) :]
     step = pl.program_id(0)
     me = me_ref[0]
 
     def load(number):
         slot = number % 2
         start_copies(
-            plan_in, me, sources_in, wi_two.at[slot], sems.at[slot], number * tile, (number + 1) * tile
+            plan, me, sources, weights.at[slot], sems.at[slot], number * tile, (number + 1) * tile
         )
 
     def save(number, slot):
         return pltpu.make_async_copy(
-            wi_two.at[slot],
-            wi_natural.at[:, pl.ds(pl.multiple_of(number * tile, tile), tile)],
+            weights.at[slot],
+            natural.at[:, pl.ds(pl.multiple_of(number * tile, tile), tile)],
             sems.at[2 + slot],
         )
 
     @pl.when(step == 0)
     def _():
         load(0)
-        start_copies(plan_out, me, sources_out, wo_all, sems.at[4])
-        out_ref[...] = jnp.zeros_like(out_ref)
 
     slot = step % 2
-    pltpu.make_async_copy(wi_two.at[slot], wi_two.at[slot], sems.at[slot]).wait()
+    pltpu.make_async_copy(weights.at[slot], weights.at[slot], sems.at[slot]).wait()
     save(step, slot).start()
 
     @pl.when(step > 0)
@@ -414,61 +409,114 @@
         def _():
             load(number)
 
-    @pl.when(step == 0)
-    def _():
-        pltpu.make_async_copy(wo_all, wo_all, sems.at[4]).wait()
-        pltpu.make_async_copy(wo_all, wo_natural, sems.at[5]).start()
-
-    @pl.when(step * tile < wo_all.shape[0])
-    def _():
-        def body(index, carry):
-            spot = pl.ds(pl.multiple_of(index * rows, rows), rows)
-            act, slope = gelu_pair(dot(h_ref[spot, :], wi_two[slot], NN))
-            act = act.astype(BF16)
-            act_ref[spot, :] = act
-            slope_ref[spot, :] = slope.astype(BF16)
-            lines = pl.ds(pl.multiple_of(step * tile, tile), tile)
-            out_ref[spot, :] += dot(act, wo_all[lines, :], NN)
-            return carry
-
-        lax.fori_loop(0, h_ref.shape[0] // rows, body, 0)
+    def body(index, carry):
+        spot = pl.ds(pl.multiple_of(index * rows, rows), rows)
+        act, slope = gelu_pair(dot(h_ref[spot, :], weights[slot], NN))
+        act_ref[spot, :] = act.astype(BF16)
+        slope_ref[spot, :] = slope.astype(BF16)
+        return carry
+
+    lax.fori_loop(0, h_ref.shape[0] // rows, body, 0)
 
     @pl.when(step == tiles - 1)
     def _():
         save(step, slot).wait()
-        pltpu.make_async_copy(wo_all, wo_natural, sems.at[5]).wait()
-
-
-def mlp_forward(field, pieces_in, pieces_out, me, hidden, columns, tile, step):
-    plan_in, sources_in = pieces_in
-    plan_out, sources_out = pieces_out
+
+
+def expand(field, pieces, me, hidden, tile, step):
+    plan, sources = pieces
     rows, wide = field.shape
-    last = hidden // tile - 1
     whole = pl.BlockSpec((rows, wide), lambda i: (0, 0), pipeline_mode=pl.Buffered(1))
-    tiles = pl.BlockSpec((rows, tile), lambda i: (0, jnp.minimum(i, last)))
-    anywhere = pl.BlockSpec(memory_space=pl.ANY)
+    tiles = pl.BlockSpec((rows, tile), lambda i: (0, i))
     return pl.pallas_call(
-        functools.partial(mlp_forward_kernel, plan_in, plan_out, tile, columns // tile, step),
-        grid=(columns // tile,),
-        in_specs=[pl.BlockSpec(memory_space=pltpu.SMEM), whole]
-        + [anywhere] * (len(sources_in) + len(sources_out)),
-        out_specs=[tiles, tiles, whole, anywhere, anywhere],
+        functools.partial(expand_kernel, plan, tile, hidden // tile, step),
+        grid=(hidden // tile,),
+        in_specs=[SCALARS, whole] + [ANYWHERE] * len(sources),
+        out_specs=[tiles, tiles, ANYWHERE],
         out_shape=[
             jax.ShapeDtypeStruct((rows, hidden), BF16),
             jax.ShapeDtypeStruct((rows, hidden), BF16),
-            jax.ShapeDtypeStruct((rows, wide), F32),
-            jax.ShapeDtypeStruct((wide, columns), BF16),
-            jax.ShapeDtypeStruct((hidden, wide), BF16),
+            jax.ShapeDtypeStruct((wide, hidden), BF16),
+        ],
+        scratch_shapes=[pltpu.VMEM((2, wide, tile), BF16), pltpu.SemaphoreType.DMA((4,))],
+        compiler_params=kernel_limits(60),
+        cost_estimate=estimate(4 * rows * wide * hidden, 4 * wide * hidden + 4 * rows * hidden),
+        name="expand",
+    )(me, field, *sources)
+
+
+def shrink_kernel(plan, width, me_ref, live_ref, a_ref, x_ref, scale_ref, *refs):
+    sources = refs[: len(plan)]
+    out_ref, low_ref, next_ref, natural, weights, sems = refs[len(plan) :]
+    live = live_ref[0].astype(F32)
+    step = pl.program_id(0)
+    parts = weights.shape[0]
+
+    @pl.when(step == 0)
+    def _():
+        for place in range(parts):
+            start_copies(
+                plan,
+                me_ref[0],
+                sources,
+                weights.at[place],
+                sems.at[place],
+                place * width,
+                (place + 1) * width,
+            )
+
+    pltpu.make_async_copy(weights.at[step], weights.at[step], sems.at[step]).wait()
+    save = pltpu.make_async_copy(
+        weights.at[step],
+        natural.at[:, pl.ds(pl.multiple_of(step * width, width), width)],
+        sems.at[parts],
+    )
+    save.start()
+    rows = 256
+
+    def body(index, carry):
+        spot = pl.ds(pl.multiple_of(index * rows, rows), rows)
+        value = dot(a_ref[spot, :], weights[step], NN)
+        out_ref[spot, :] = value
+        hires = x_ref[spot, :].astype(F32) + scale_ref[...] * value
+        low_ref[spot, :] = hires.astype(BF16)
+        next_ref[spot, :] = (live * hires).astype(BF16)
+        return carry
+
+    lax.fori_loop(0, a_ref.shape[0] // rows, body, 0)
+    save.wait()
+
+
+def shrink(act, field, scale, live, pieces, me, width):
+    plan, sources = pieces
+    rows, hidden = act.shape
+    columns = max(each[4] for each in plan)
+    return pl.pallas_call(
+        functools.partial(shrink_kernel, plan, width),
+        grid=(columns // width,),
+        in_specs=[
+            SCALARS,
+            SCALARS,
+            pl.BlockSpec((rows, hidden), lambda i: (0, 0), pipeline_mode=pl.Buffered(1)),
+            pl.BlockSpec((rows, width), lambda i: (0, i)),
+            pl.BlockSpec((1, width), lambda i: (0, i)),
+        ]
+        + [ANYWHERE] * len(sources),
+        out_specs=[pl.BlockSpec((rows, width), lambda i: (0, i))] * 3 + [ANYWHERE],
+        out_shape=[
+            jax.ShapeDtypeStruct((rows, columns), F32),
+            jax.ShapeDtypeStruct((rows, columns), BF16),
+            jax.ShapeDtypeStruct((rows, columns), BF16),
+            jax.ShapeDtypeStruct((hidden, columns), BF16),
         ],
         scratch_shapes=[
-            pltpu.VMEM((2, wide, tile), BF16),
-            pltpu.VMEM((hidden, wide), BF16),
-            pltpu.SemaphoreType.DMA((6,)),
+            pltpu.VMEM((columns // width, hidden, width), BF16),
+            pltpu.SemaphoreType.DMA((columns // width + 1,)),
         ],
         compiler_params=kernel_limits(60),
-        cost_estimate=estimate(7 * rows * wide * hidden, 8 * wide * hidden + 4 * rows * hidden),
-        name="mlp_forward",
-    )(me, field, *sources_in, *sources_out)
+        cost_estimate=estimate(3 * rows * hidden * columns, 6 * hidden * columns),
+        name="shrink",
+    )(me, live, act, field, scale, *sources)
 
 
 def outer_kernel(shares, me_ref, left_ref, right_ref, mine_ref, theirs_ref):
@@ -479,7 +527,11 @@
 def outer_sum(left, right, me, share):
     rows, lines = left.shape
     columns = right.shape[1]
+    if share % 16:
+        return halves(dot(left, right, TN).astype(BF16).reshape(-1, share, columns), lines // share)
     tile = 4 * share if share >= 192 else 16 * share
+    while lines % tile:
+        tile //= 2
     block = pl.BlockSpec((tile // share // 2, share, columns), lambda i: (i, 0, 0))
     return pl.pallas_call(
         functools.partial(outer_kernel, share),
@@ -497,14 +549,12 @@
     )(me, left, right)
 
 
-def mlp_back_kernel(
-    step, share, me_ref, g_ref, h_ref, slope_ref, wi_ref, wo_ref, start_ref, dh_ref, *refs
-):
-    *grads, low_ref = refs
+def mlp_back_kernel(step, share, begun, me_ref, g_ref, h_ref, slope_ref, wi_ref, wo_ref, *refs):
+    start_ref, dh_ref, *grads, low_ref = refs if begun else (None,) + refs
 
     @pl.when(pl.program_id(0) == 0)
     def _():
-        dh_ref[...] = start_ref[...]
+        dh_ref[...] = start_ref[...] if begun else jnp.zeros_like(dh_ref)
 
     def body(index, carry):
         spot = pl.ds(pl.multiple_of(index * step, step), step)
@@ -515,7 +565,7 @@
         return carry
 
     lax.fori_loop(0, h_ref.shape[0] // step, body, 0)
-    block = 384
+    block = h_ref.shape[1]
     even = me_ref[0] % 2 == 0
 
     def outer(index, carry):
@@ -543,7 +593,7 @@
         grad_specs = [pl.BlockSpec((wide, tile), lambda i: (0, i))]
         grad_types = [jax.ShapeDtypeStruct((wide, width), BF16)]
     outs = pl.pallas_call(
-        functools.partial(mlp_back_kernel, step, share),
+        functools.partial(mlp_back_kernel, step, share, start is not None),
         grid=(last - first,),
         in_specs=[
             SCALARS,
@@ -552,53 +602,57 @@
             pl.BlockSpec((rows, tile), lambda i: (0, i + first)),
             pl.BlockSpec((wide, tile), lambda i: (0, i + first)),
             pl.BlockSpec((tile, wide), lambda i: (i + first, 0)),
-            whole,
-        ],
+        ]
+        + ([] if start is None else [whole]),
         out_specs=[whole] + grad_specs,
         out_shape=[jax.ShapeDtypeStruct((rows, wide), F32)] + grad_types,
         scratch_shapes=[pltpu.VMEM((rows, tile), BF16)],
         compiler_params=kernel_limits(60),
         cost_estimate=estimate(7 * rows * wide * width, 6 * wide * width),
         name="mlp_back",
-    )(me, grad, field, slope, w_in, w_out, start)
+    )(me, grad, field, slope, w_in, w_out, *([] if start is None else [start]))
     return (outs[0], outs[1:])
 
 
-def gate_kernel(
-    mixed_ref, resid_ref, gv_ref, live_ref, wi_ref, wo_ref, joined_ref, dmix_ref, dwi_ref, dwo_ref
-):
+def gate_kernel(share, me_ref, live_ref, mixed_ref, gv_ref, w_ref, gated_ref, dmix_ref, *grads):
     live = live_ref[0].astype(F32)
     mixed = mixed_ref[...]
     mixed_low = mixed.astype(BF16)
-    act, slope = gelu_pair(dot(mixed_low, wi_ref[...], NN))
+    wide = mixed.shape[1]
+    wi, wo = (w_ref[:, :wide], w_ref[:, wide:])
+    act, slope = gelu_pair(dot(mixed_low, wi, NN))
     act = act.astype(BF16)
-    gate = jnp.tanh(dot(act, wo_ref[...], NN))
-    joined_ref[...] = (live * (resid_ref[...] + gate * mixed)).astype(BF16)
+    gate = jnp.tanh(dot(act, wo, NN))
+    gated_ref[...] = gate * mixed
     grad = live * gv_ref[...].astype(F32)
     logit = (grad * mixed * (1.0 - gate * gate)).astype(BF16)
-    dwo_ref[...] = dot(act, logit, TN).astype(BF16)
-    low = (dot(logit, wo_ref[...], NT) * slope).astype(BF16)
-    dwi_ref[...] = dot(mixed_low, low, TN).astype(BF16)
-    dmix_ref[...] = grad * gate + dot(low, wi_ref[...], NT)
-
-
-def gate_both(mixed, resid, grad, live, w_in, w_out):
+    low = (dot(logit, wo, NT) * slope).astype(BF16)
+    for place, (left, right) in enumerate(((mixed_low, low), (act, logit))):
+        lanes = slice(place * wide, (place + 1) * wide)
+        if share:
+            spot = (slice(None), slice(None), lanes)
+            store_shares(dot(left, right, TN), share, me_ref[0] % 2 == 0, *grads, spot)
+        else:
+            grads[0][:, lanes] = dot(left, right, TN).astype(BF16)
+    dmix_ref[...] = grad * gate + dot(low, wi, NT)
+
+
+def gate_both(mixed, grad, live, me, weights, devices):
     rows, wide = mixed.shape
-    place = pl.BlockSpec(memory_space=pltpu.VMEM)
+    share = wide // devices
+    grad_types = [share_type(devices, share, 2 * wide)] * 2
+    if share % 16:
+        share = 0
+        grad_types = [jax.ShapeDtypeStruct((wide, 2 * wide), BF16)]
     return pl.pallas_call(
-        gate_kernel,
-        in_specs=[place, place, place, pl.BlockSpec(memory_space=pltpu.SMEM), place, place],
-        out_specs=[place] * 4,
-        out_shape=[
-            jax.ShapeDtypeStruct((rows, wide), BF16),
-            jax.ShapeDtypeStruct((rows, wide), F32),
-            jax.ShapeDtypeStruct(w_in.shape, BF16),
-            jax.ShapeDtypeStruct(w_out.shape, BF16),
-        ],
+        functools.partial(gate_kernel, share),
+        in_specs=[SCALARS, SCALARS, LOCAL, LOCAL, LOCAL],
+        out_specs=[LOCAL] * (2 + len(grad_types)),
+        out_shape=[jax.ShapeDtypeStruct((rows, wide), F32)] * 2 + grad_types,
         compiler_params=kernel_limits(60),
-        cost_estimate=estimate(20 * rows * wide * w_in.shape[1], 30 * rows * wide),
+        cost_estimate=estimate(20 * rows * wide * wide, 30 * rows * wide),
         name="gate_both",
-    )(mixed, resid, grad, live, w_in, w_out)
+    )(me, live, mixed, grad, weights)
 
 
 def bit_pairs(devices, bit):
@@ -725,60 +779,129 @@
     return (take(field, axis, mine) + arrived, held[:axis] + held[axis + 1 :])
 
 
+def combine_kernel(parts, stacked, me_ref, *refs):
+    count = 4 * sum(len(widths) for widths in parts)
+    blocks, outs = (refs[:count], refs[count:])
+    sums = []
+    for widths in parts:
+        kept, sent = ([], [])
+        for _ in widths:
+            (a, b, c, d), blocks = (blocks[:4], blocks[4:])
+            kept.append((a[0].astype(F32) + b[0].astype(F32)).astype(BF16))
+            sent.append((c[0].astype(F32) + d[0].astype(F32)).astype(BF16))
+        sums.append((kept, sent))
+    if not stacked:
+        for place, pair in enumerate(sums):
+            for out_ref, values in zip(outs[2 * place : 2 * place + 2], pair):
+                begin = 0
+                for value in values:
+                    out_ref[0, :, begin : begin + value.shape[1]] = value
+                    begin += value.shape[1]
+        return
+    for which, out_ref in enumerate(outs):
+        line = 0
+        for pair in sums:
+            (value,) = pair[which]
+            rows, columns = value.shape
+            for begin in range(0, columns, stacked):
+                out_ref[0, line : line + rows, :] = value[:, begin : begin + stacked]
+                line += rows
+
+
+def combine(me, parts, stacked):
+    def spec(rows, width, bit, after_it, other, begin):
+        def index(slot, me_ref):
+            mine = (me_ref[0] >> bit) & 1
+            mine = 1 - mine if other else mine
+            return ((slot // after_it * 2 + mine) * after_it + slot % after_it, 0, begin // width)
+
+        return pl.BlockSpec((1, rows, width), index)
+
+    in_specs, operands, widths, shapes, moved = ([], [], [], [], 0)
+    for bit, before, after_it, segments in parts:
+        slots = before * after_it
+        for kept, arrived, begin, width in segments:
+            rows = kept.shape[1]
+            for other in (False, True):
+                in_specs += [spec(rows, width, bit, after_it, other, begin)] * 2
+                operands += [kept, arrived]
+            moved += 6 * slots * rows * width
+        widths.append([segment[3] for segment in segments])
+        shapes.append((rows, sum(widths[-1])))
+    if stacked:
+        total = sum(rows * columns // stacked for rows, columns in shapes)
+        shapes = [(total, stacked)]
+    out_specs, out_types = ([], [])
+    for shape in shapes:
+        out_specs += [pl.BlockSpec((1,) + shape, lambda slot, me_ref: (slot, 0, 0))] * 2
+        out_types += [jax.ShapeDtypeStruct((slots,) + shape, BF16)] * 2
+    outs = pl.pallas_call(
+        functools.partial(combine_kernel, widths, stacked),
+        grid_spec=pltpu.PrefetchScalarGridSpec(
+            num_scalar_prefetch=1,
+            grid=(slots,),
+            in_specs=in_specs,
+            out_specs=out_specs,
+        ),
+        out_shape=out_types,
+        compiler_params=kernel_limits(48),
+        cost_estimate=estimate(moved, 2 * moved),
+        name="combine",
+    )(me, *operands)
+    return list(zip(outs[::2], outs[1::2]))
+
+
 class Scatterer:
-    def __init__(self, devices, *gradients):
+    def __init__(self, devices, me, gradients, parts, early=False):
         x_bits, y_bits, z_bits = axis_bits(devices)
+        self.me = me
         self.bits = devices.bit_length() - 1
         self.orders = (y_bits + x_bits + z_bits, x_bits + y_bits + z_bits)
-        self.split = len(x_bits + y_bits)
-        self.shapes = [mine.shape[1:] for mine, _ in gradients]
-        self.width = math.gcd(*[shape[1] for shape in self.shapes])
+        self.split = 0 if early else len(x_bits + y_bits)
+        if early:
+            self.orders = (self.orders[0],) * 2
+        self.parts = parts
+        self.shapes = [
+            (gradients[part[0][0]][0].shape[1], sum(width for _, _, width in part)) for part in parts
+        ]
+        self.width = min(columns for _, columns in self.shapes)
         self.stage = -1
         self.kept = [mine for mine, _ in gradients]
         self.sends = [(theirs, 0) for _, theirs in gradients]
         self.result = None
 
-    def prepare(self, parts, held):
-        self.kept, self.sends = ([], [])
-        self.held = []
-        for place, part in enumerate(parts):
-            bit = self.orders[place][self.stage]
-            axis = held[place].index(bit)
-            mine = own_bit(bit)
-            self.kept.append(take(part, axis, mine))
-            self.sends.append((take(part, axis, 1 - mine), bit))
-            self.held.append(held[place][:axis] + held[place][axis + 1 :])
-
     def receive(self, arrived):
-        totals = [
-            kept.astype(F32) + other.astype(F32) for kept, other in zip(self.kept, arrived)
-        ]
+        pairs = list(zip(self.kept, arrived))
         self.stage += 1
         if self.stage == self.bits - 1:
-            (total,) = totals
+            total = pairs[0][0][0].astype(F32) + pairs[0][1][0].astype(F32)
             self.sends, self.result = ([], [])
-            begin = 0
+            line = 0
             for rows, columns in self.shapes:
                 pieces = []
                 for _ in range(columns // self.width):
-                    pieces.append(total[begin : begin + rows])
-                    begin += rows
+                    pieces.append(total[line : line + rows])
+                    line += rows
                 self.result.append(jnp.concatenate(pieces, axis=1))
             return
-        parts = [total.astype(BF16) for total in totals]
         if self.stage == 0:
-            blocks = []
-            for part in parts:
-                for begin in range(0, part.shape[-1], self.width):
-                    blocks.append(part[..., begin : begin + self.width])
-            field = blocks[0] if len(blocks) == 1 else jnp.concatenate(blocks, axis=1)
-            field = field.reshape((2,) * (self.bits - 1) + field.shape[1:])
-            middle = self.width // 2
-            parts = [field[..., :middle], field[..., middle:]]
+            segments = [
+                [(*pairs[place], begin, width) for place, begin, width in part]
+                for part in self.parts
+            ]
             self.held = [list(range(self.bits - 1, 0, -1))] * 2
-        if self.stage == self.split:
-            parts = [jnp.concatenate(parts, axis=-1)]
-        self.prepare(parts, self.held)
+        else:
+            segments = [[(*pair, 0, pair[0].shape[2])] for pair in pairs]
+        parts, helds = ([], [])
+        for order, held, its_segments in zip(self.orders, self.held, segments):
+            bit = order[self.stage]
+            axis = held.index(bit)
+            parts.append((bit, 2**axis, 2 ** (len(held) - axis - 1), its_segments))
+            helds.append(held[:axis] + held[axis + 1 :])
+        self.held = helds
+        sums = combine(self.me, parts, self.width if self.stage == self.split else 0)
+        self.kept = [kept for kept, _ in sums]
+        self.sends = [(sent, part[0]) for (_, sent), part in zip(sums, parts)]
 
 
 class Ticks:
@@ -863,31 +986,49 @@
     def gathered(block):
         return lax.all_gather(block, "fsdp", axis=0, tiled=True)
 
-    vit_all = gathered(jnp.concatenate((w_qkv, w_out, w_gate_in, w_gate_out), axis=1))
-    qkv_all = vit_all[:, : 3 * D]
-    out_all = vit_all[:, 3 * D : 4 * D]
-    gate_in_all = vit_all[:, 4 * D : 5 * D]
-    gate_out_all = vit_all[:, 5 * D :]
-    up_all = gathered(w_up)
-    down_all = gathered(w_down)
+    live = image_live.astype(F32)
+    vit_all = gathered(jnp.concatenate((w_qkv, w_out), axis=1))
+    qkv_all, out_all = (vit_all[:, : 3 * D], vit_all[:, 3 * D :])
+    gates_all = gathered(jnp.concatenate((w_gate_in, w_gate_out), axis=1))
     adapt_all = gathered(w_adapt)
-    live = image_live.astype(F32)
-    grad_joined_low = (grad_vit.astype(F32) * live).astype(BF16)
-    patch_in = x_vit.astype(F32)
-
+    tile = D
+    tiles = w_expand.shape[1] // tile
     gatherer = Gatherer(devices)
-    expand_pieces = gatherer.weight(w_expand, [(0, D, 2 * D), (2 * D, 3 * D, 4 * D)])
+    expand_pieces = gatherer.weight(w_expand, [(0, C, 2 * C)])
     conved = depthwise(after((x_hires,), gatherer.last)[0], seven_taps, KS, GRID_HR)
-    gatherer.ends.append(conved)
-    more_pieces = gatherer.weight(w_expand, [(4 * D, 5 * D, 6 * D)])
-    normed_a, inverse_a = norm_rows(patch_in, 1e-05)
-    normed_a_low = (normed_a * gain_a).astype(BF16)
-    normed_a_low = after((normed_a_low,), gatherer.last)[0]
-    qkv_low = dot(normed_a_low, qkv_all, NN).astype(BF16)
-    attended_low = attend(qkv_low)
-    gatherer.ends.append(attended_low)
-    shrink_pieces = gatherer.weight(w_shrink, [(0, C // 4, C // 2), (C // 2, 3 * C // 4, C)])
+    normed_c, inverse_c = norm_rows(conved, 1e-06)
+    normed_c_low = (normed_c * gain_c).astype(BF16)
+    gatherer.ends.append(normed_c_low)
+    more_pieces = gatherer.weight(w_expand, [(2 * C, 3 * C, 4 * C)])
     expand_pieces = tuple(one + two for one, two in zip(expand_pieces, more_pieces))
+
+    def attention(x_vit):
+        patch_in = x_vit.astype(F32)
+        normed_a, inverse_a = norm_rows(patch_in, 1e-05)
+        normed_a_low = (normed_a * gain_a).astype(BF16)
+        qkv_low = dot(normed_a_low, qkv_all, NN).astype(BF16)
+        attended_low = attend(qkv_low)
+        resid_one = patch_in + dot(attended_low, out_all, NN)
+        normed_b, inverse_b = norm_rows(resid_one, 1e-05)
+        normed_b_low = (normed_b * gain_b).astype(BF16)
+        return (
+            normed_b_low, qkv_low, attended_low, resid_one, normed_a, inverse_a, normed_b, inverse_b, normed_a_low
+        )
+
+    (
+        normed_b_low, qkv_low, attended_low, resid_one, normed_a, inverse_a, normed_b, inverse_b, normed_a_low
+    ) = attention(after((x_vit,), gatherer.last)[0])
+    gatherer.ends.append(normed_b_low)
+    shrink_pieces = gatherer.weight(w_shrink, [(0, C // 4, C // 2)])
+    field_c = after((normed_c_low,), gatherer.last)[0]
+    activated, slope, expand_all = expand(
+        field_c, expand_pieces, me, w_expand.shape[1], tile, 256
+    )
+    gatherer.ends.append(activated)
+    more_pieces = gatherer.weight(w_shrink, [(C // 2, 3 * C // 4, C)])
+    shrink_pieces = tuple(one + two for one, two in zip(shrink_pieces, more_pieces))
+    up_all = gathered(after((w_up,), gatherer.last)[0])
+    down_all = gathered(after((w_down,), gatherer.last)[0])
 
     def shares(gradient):
         return gradient.reshape(devices, gradient.shape[0] // devices, gradient.shape[1])
@@ -897,120 +1038,151 @@
             return tuple(gradient)
         return halves(shares(gradient[0]), devices)
 
-    resid_one = patch_in + dot(attended_low, out_all, NN)
-    normed_b, inverse_b = norm_rows(resid_one, 1e-05)
-    normed_b_low = (normed_b * gain_b).astype(BF16)
-    normed_b_low = after((normed_b_low,), expand_pieces[1] + shrink_pieces[1])[0]
-    mlp_out, grad_b, d_up, d_down = mlp_both(
-        grad_joined_low, normed_b_low, up_all, down_all, me, devices, D
-    )
-    resid_two = resid_one + mlp_out
-    d_gain_two = jnp.sum(grad_b * normed_b, axis=0)
-    grad_first = grad_joined_low.astype(F32) + norm_back(grad_b * gain_b, normed_b, inverse_b)
     ticks = Ticks()
-    sum_mlp = Scatterer(devices, split(d_up), split(d_down))
-
-    def attention_back(grad_first):
-        grad_first_low = grad_first.astype(BF16)
-        d_out = dot(attended_low, grad_first_low, TN).astype(BF16)
-        grad_att_low = dot(grad_first_low, out_all, NT).astype(BF16)
-        grad_qkv_low = jnp.concatenate(attend_back(qkv_low, grad_att_low), axis=1)
-        d_qkv = dot(normed_a_low, grad_qkv_low, TN).astype(BF16)
-        grad_a = dot(grad_qkv_low, qkv_all, NT)
-        d_gain_one = jnp.sum(grad_a * normed_a, axis=0)
-        grad_patches = grad_first + norm_back(grad_a * gain_a, normed_a, inverse_a)
-        return (grad_patches, d_gain_one, d_qkv, d_out)
-
-    grad_patches, d_gain_one, d_qkv, d_out = ticks.run([sum_mlp], grad_first, attention_back)
-    sum_attention = Scatterer(devices, split((d_qkv,)), split((d_out,)))
-
-    normed_c, inverse_c = norm_rows(conved, 1e-06)
-    normed_c_low = (normed_c * gain_c).astype(BF16)
-    tile = D
-    tiles = w_expand.shape[1] // tile
-
-    def network(field):
-        return mlp_forward(
-            field, expand_pieces, shrink_pieces, me, w_expand.shape[1], w_expand.shape[1], tile, 256
-        )
-
-    shrunk, activated, slope, expand_all, shrink_all = (
-        lambda outs: (outs[2], outs[0], outs[1], outs[3], outs[4])
-    )(ticks.run([sum_mlp, sum_attention], normed_c_low, network))
+
+    shrunk, hires_low, hires_next, shrink_all = ticks.run(
+        [],
+        activated,
+        lambda act: shrink(
+            act, x_hires, scale_c.reshape(1, C), image_live, shrink_pieces, me, C // 2
+        ),
+    )
 
     table = pool_table(GRID_HR, GRID_LR)
     pool = jnp.einsum("ia,jb->ijab", table, table).reshape(GRID_LR**2, GRID_HR**2).astype(BF16)
 
-    def adapter(shrunk):
-        hires_out = x_hires.astype(F32) + scale_c * shrunk
-        pooled_low = dot(pool, hires_out.astype(BF16), NN).astype(BF16)
+    def adapter(hires_low):
+        pooled_low = dot(pool, hires_low, NN).astype(BF16)
         adapted = dot(pooled_low, adapt_all, NN)
         mixed = depthwise(adapted, three_taps, KA, GRID_LR)
-        joined, grad_mixed, d_gate_in, d_gate_out = gate_both(
-            mixed, resid_two, grad_vit, image_live, gate_in_all, gate_out_all
+        gated, grad_mixed, *d_gates = gate_both(
+            mixed, grad_vit, image_live, me, gates_all, devices
         )
-        hires_next = (live * hires_out).astype(BF16)
-        return (grad_mixed, d_gate_in, d_gate_out, joined, hires_next, pooled_low, adapted)
-
-    grad_mixed, d_gate_in, d_gate_out, joined, hires_next, pooled_low, adapted = ticks.run(
-        [sum_mlp, sum_attention], shrunk, adapter
+        return (grad_mixed, gated, pooled_low, adapted, *d_gates)
+
+    grad_mixed, gated, pooled_low, adapted, *d_gates = ticks.run(
+        [], hires_low, adapter
     )
 
     def adapter_back(grad_mixed):
         grad_adapted_low, d_conv_three = depthwise_back(
             grad_mixed, adapted, jnp.zeros(adapted.shape, BF16), three_taps, KA, GRID_LR, 0, D
         )
-        d_adapt = dot(pooled_low, grad_adapted_low, TN).astype(BF16)
+        d_adapt = outer_sum(pooled_low, grad_adapted_low, me, edge_c)
         grad_pooled_low = dot(grad_adapted_low, adapt_all, NT).astype(BF16)
         grad_hires_out = live * grad_hires.astype(F32) + dot(pool, grad_pooled_low, TN)
         d_layer_scale = jnp.sum(grad_hires_out * shrunk, axis=0)
         grad_shrunk_low = (grad_hires_out * scale_c).astype(BF16)
-        return (grad_shrunk_low, d_layer_scale, grad_hires_out, d_adapt, d_conv_three)
-
-    grad_shrunk_low, d_layer_scale, grad_hires_out, d_adapt, d_conv_three = ticks.run(
-        [sum_mlp, sum_attention], grad_mixed, adapter_back
-    )
-    square = jnp.concatenate((shares(d_gate_in), shares(d_gate_out), shares(d_adapt)), axis=1)
-    sum_square = Scatterer(devices, halves(square, devices))
+        return (grad_shrunk_low, d_layer_scale, grad_hires_out, d_conv_three, *d_adapt)
+
+    grad_shrunk_low, d_layer_scale, grad_hires_out, d_conv_three, *d_adapt = ticks.run(
+        [], grad_mixed, adapter_back
+    )
+    sum_square = Scatterer(
+        devices,
+        me,
+        [split(d_gates), split(d_adapt)],
+        [[(0, 0, 2 * D)], [(1, 0, D)]],
+        early=True,
+    )
 
     outs = ticks.run(
-        [sum_mlp, sum_attention, sum_square],
+        [sum_square],
         grad_shrunk_low,
         lambda grad: outer_sum(activated, grad, me, w_shrink.shape[0]),
     )
-    sum_shrink = Scatterer(devices, tuple(outs))
-    grad_c = jnp.zeros((x_hires.shape[0], C), F32)
-    beside = ([sum_attention, sum_square, sum_shrink], [sum_shrink], [sum_shrink, sum_square])
+    sum_shrink = Scatterer(
+        devices, me, [tuple(outs)], [[(0, 0, C // 2)], [(0, C // 2, C // 2)]]
+    )
     sums_expand = []
-    for part in range(3):
-        grad_c, *d_part = ticks.run(
-            list(beside[part]) + sums_expand[-1:],
-            grad_c,
-            lambda start, part=part: mlp_back(
-                grad_shrunk_low,
+
+    def network_back(groups, grad_c, part):
+        value = grad_shrunk_low if grad_c is None else grad_c
+        sums, *d_part = ticks.run(
+            groups,
+            value,
+            lambda value: mlp_back(
+                value if grad_c is None else grad_shrunk_low,
                 normed_c_low,
                 slope,
                 expand_all,
                 shrink_all,
-                start,
+                None if grad_c is None else value,
                 me,
                 devices,
                 tile,
-                256,
-                part * tiles // 3,
-                (part + 1) * tiles // 3,
+                512,
+                part * tiles // 2,
+                (part + 1) * tiles // 2,
             ),
         )
-        sums_expand.append(Scatterer(devices, split(d_part)))
+        width = w_expand.shape[1] // 4
+        sums_expand.append(
+            Scatterer(devices, me, [split(d_part)], [[(0, 0, width)], [(0, width, width)]])
+        )
+        return sums
+
+    grad_c = network_back([sum_square, sum_shrink], None, 0)
+
+    grad_joined_low = (grad_vit.astype(F32) * live).astype(BF16)
+
+    def network_both(field):
+        mlp_out, grad_b, d_up, d_down = mlp_both(
+            grad_joined_low, field, up_all, down_all, me, devices, D
+        )
+        return (mlp_out, grad_b, *d_up, *d_down)
+
+    mlp_out, grad_b, *d_hidden = ticks.run(
+        [sum_shrink, sums_expand[0]], normed_b_low, network_both
+    )
+    sum_mlp = Scatterer(
+        devices,
+        me,
+        [split(d_hidden[:-2]), split(d_hidden[-2:])],
+        [[(0, 0, w_up.shape[1])], [(1, 0, D)]],
+    )
+    joined = (live * (resid_one + mlp_out + gated)).astype(BF16)
+    d_gain_two = jnp.sum(grad_b * normed_b, axis=0)
+    grad_first = grad_joined_low.astype(F32) + norm_back(grad_b * gain_b, normed_b, inverse_b)
+    grad_c = network_back([sum_shrink, sum_mlp, sum_square], grad_c, 1)
+
+    def attention_back(grad_first):
+        grad_first_low = grad_first.astype(BF16)
+        grad_att_low = dot(grad_first_low, out_all, NT).astype(BF16)
+        d_out = outer_sum(attended_low, grad_first_low, me, edge_d)
+        return (*attend_back(qkv_low, grad_att_low), *d_out)
+
+    *grads_three, out_mine, out_theirs = ticks.run(
+        [sum_mlp, sum_shrink, sums_expand[1], sum_square], grad_first, attention_back
+    )
+
+    def projection_back(grad_queries):
+        grad_qkv_low = jnp.concatenate((grad_queries, *grads_three[1:]), axis=1)
+        d_qkv = outer_sum(normed_a_low, grad_qkv_low, me, edge_d)
+        grad_a = dot(grad_qkv_low, qkv_all, NT)
+        d_gain_one = jnp.sum(grad_a * normed_a, axis=0)
+        grad_patches = grad_first + norm_back(grad_a * gain_a, normed_a, inverse_a)
+        return (grad_patches, d_gain_one, *d_qkv)
+
+    grad_patches, d_gain_one, *d_qkv = ticks.run(
+        [sums_expand[0], sum_mlp, sum_shrink], grads_three[0], projection_back
+    )
+    sum_attention = Scatterer(
+        devices,
+        me,
+        [tuple(d_qkv), (out_mine, out_theirs)],
+        [[(0, 0, 2 * D)], [(0, 2 * D, D), (1, 0, D)]],
+    )
+
     d_gain_three = jnp.sum(grad_c * normed_c, axis=0)
     grad_conved = norm_back(grad_c * gain_c, normed_c, inverse_c)
     grad_hires_in = grad_hires_out
     pieces_seven = []
     width = C // 3
     beside = (
-        [sum_shrink, sum_square, sums_expand[0], sums_expand[2]],
-        [sum_shrink, sums_expand[0], sums_expand[1]],
-        [sum_square, sums_expand[1], sums_expand[2]],
+        [sums_expand[1], sums_expand[0], sum_mlp],
+        [sum_attention, sums_expand[1], sum_mlp],
+        [sum_attention] + sums_expand,
     )
     for part in range(3):
         grad_hires_in, taps_part = ticks.run(
@@ -1029,13 +1201,7 @@
         )
         pieces_seven.append(taps_part)
     d_conv_seven = jnp.concatenate(pieces_seven, axis=1)
-    ticks.finish([sum_mlp, sum_attention, sum_square, sum_shrink] + sums_expand)
-    g_up, g_down = sum_mlp.result
-    g_qkv, g_out = sum_attention.result
-    (g_square,) = sum_square.result
-    (g_shrink,) = sum_shrink.result
-    g_expand = jnp.concatenate([each.result[0] for each in sums_expand], axis=1)
-
+    ticks.run([sum_attention, sum_square] + sums_expand, jnp.zeros((), F32), lambda value: value)
     small_grads = jnp.concatenate(
         (
             d_conv_seven.reshape(KS * KS, devices, edge_c).swapaxes(0, 1).reshape(devices, -1),
@@ -1047,6 +1213,13 @@
         ),
         axis=1,
     )
+    small_grads = after((small_grads,), ticks.before)[0]
+    ticks.finish([sum_attention, sum_mlp, sum_shrink, sum_square] + sums_expand)
+    g_up, g_down = sum_mlp.result
+    g_attention = jnp.concatenate(sum_attention.result, axis=1)
+    g_gates, g_adapt = sum_square.result
+    g_shrink = jnp.concatenate(sum_shrink.result, axis=1)
+    g_expand = jnp.concatenate([part for each in sums_expand for part in each.result], axis=1)
     small_sums = small_grads.reshape((2,) * (devices.bit_length() - 1) + small_grads.shape[1:])
     held = list(range(devices.bit_length() - 2, -1, -1))
     for bit in range(devices.bit_length() - 1):
@@ -1058,8 +1231,8 @@
         grad_patches,
         grad_hires_in,
         small_outs[4],
-        g_qkv,
-        g_out,
+        g_attention[:, : 3 * D],
+        g_attention[:, 3 * D :],
         small_outs[5],
         g_up,
         g_down,
@@ -1068,10 +1241,10 @@
         g_expand,
         g_shrink,
         small_outs[2],
-        g_square[2 * edge_d :],
+        g_adapt,
         small_outs[3].reshape(KA * KA, edge_d),
-        g_square[:edge_d],
-        g_square[edge_d : 2 * edge_d],
+        g_gates[:, :D],
+        g_gates[:, D:],
     )
 
 

time: 1150 us -> 1060 us (0.922)
  Pallas kernels: 428 us -> 520 us
  other arithmetic: 131 us -> 53.8 us
  starting transfers between devices: 143 us -> 97.2 us
  local copies, waits for them, and re-layouts: 137 us -> 113 us
  waiting for transfers between devices: 233 us -> 214 us
  matrix products: 55.1 us -> 42.4 us
    pallas_call x5 -> x29, Pallas kernels: 184 us -> 262 us  [the longest x24 88.9 us: combine(): pl.pallas_call(functools.partial(combine_kernel, widths, stacked), grid_s...]
    convert_element_type x46 -> x3, other arithmetic: 80.1 us -> 1.97 us  [the longest x1 1.38 us: attention(): normed_b_low = (normed_b * gain_b).astype(BF16)]
    ppermute x111 -> x92, starting transfers between devices: 129 us -> 90 us  [swap(): lax.ppermute(block, 'fsdp', [(index, index ^ mask) for index in range(dev...]
    ppermute x111 -> x92, waiting for transfers between devices: 227 us -> 196 us  [swap(): lax.ppermute(block, 'fsdp', [(index, index ^ mask) for index in range(dev...]
    squeeze x26 -> x0, local copies, waits for them, and re-layouts: 17.7 us -> none  [take(): return lax.dynamic_index_in_dim(field, place, axis, keepdims=False)]
    pallas_call x1 -> x4, Pallas kernels: 25.7 us -> 40.8 us  [outer_sum(): pl.pallas_call(functools.partial(outer_kernel, share), grid=(lines // til...]
    dynamic_slice x17 -> x5, local copies, waits for them, and re-layouts: 15.7 us -> 0.68 us  [take(): return lax.dynamic_index_in_dim(field, place, axis, keepdims=False)]
    ppermute x5, waiting for transfers between devices: 4 us -> 17.2 us  [gather_small(): other = lax.ppermute(gathered, 'fsdp', bit_pairs(devices, bit))]
  transfers between devices with their start and end apart: 120 -> 102, of which waited for: 35 -> 30; matrix products, arithmetic and copies ran while one was open for 19% -> 14% of each run, Pallas kernels for 33% -> 44%
where the time goes in v3:
time: 1060 us
  Pallas kernels  520 us (49%)
  waiting for transfers between devices  214 us (20%)
  local copies, waits for them, and re-layouts  113 us (11%)
  starting transfers between devices  97.2 us (9%)
  other arithmetic  53.8 us (5%)
  matrix products  42.4 us (4%)
  between operations  16.7 us (2%)
    ppermute x92, waiting for transfers between devices, swap(): lax.ppermute(block, 'fsdp', [(index, index ^ mask) for index in range(dev...  196 us
    ppermute x92, starting transfers between devices, swap(): lax.ppermute(block, 'fsdp', [(index, index ^ mask) for index in range(dev...  90 us
    pallas_call x4, Pallas kernels, depthwise_back(): pl.pallas_call(functools.partial(depthwise_back_kernel, width, edge), gri...  89.3 us
    pallas_call x24, Pallas kernels, combine(): pl.pallas_call(functools.partial(combine_kernel, widths, stacked), grid_s...  88.9 us
    pallas_call x2, Pallas kernels, mlp_back(): pl.pallas_call(functools.partial(mlp_back_kernel, step, share, start is n...  87.1 us
    unnamed x280, local copies, waits for them, and re-layouts  58.3 us
    pallas_call x1, Pallas kernels, mlp_both(): pl.pallas_call(functools.partial(mlp_both_kernel, (in_rows, out_rows)), g...  42.8 us
    dot_general x7, matrix products, dot(): lax.dot_general(left, right, (dims, ((), ())), preferred_element_type=F32)  42.4 us
  transfers between devices with their start and end apart: 102, of which 30 were waited for; matrix products, arithmetic and copies ran while one was open for 14% of the time, Pallas kernels for 44%

profile of v3, /device:TPU:0, one launch (start us, length us, event | category | flops | bytes accessed | tf_op | source)
XLA Modules:
  0.0 1056.8 jit_solution(7895410827551423995)
XLA Ops:
  31.9 15.5 %collective-permute-done.13 = bf16[8,2800]{1,0:T(8,128)(2,1)S(1)} collective-permute-done((bf16[8,2800]{1,0:T(8,128)(2,1)S(1)}, bf16[8,2800]{1,0:T(8,128)(2,1)S(1)}, u32[]{:S(2)}, u32[]{:S(2)}) %collective-permute-start.13) | collective-permute-done | bytes 44832 | tf_op jit(solution)/shard_map/ppermute | solution.py:669
  66.1 8.9 collective-permute-done.3
  85.3 36.5 %depthwise.2 = f32[1024,1536]{1,0:T(8,128)S(1)} custom-call(bf16[1024,1536]{1,0:T(8,128)(2,1)S(1)} %copy-done.53, bf16[49,1536]{1,0:T(8,128)(2,1)S(1)} %reshape.281.taps_ref), custom_call_target="tpu_custom_call" | custom-call | flops 46242201600 | bytes 12582912 | tf_op jit(solution)/shard_map/depthwise/pallas_call | solution.py:119
  144.6 8.7 collective-permute-done.15
  162.9 9.2 collective-permute-done.19
  172.1 12.9 %collective-permute-start.17 = (bf16[1,192,768]{2,1,0:T(8,128)(2,1)S(1)}, bf16[1,192,768]{2,1,0:T(8,128)(2,1)S(1)}, u32[]{:S(2)}, u32[]{:S(2)}) collective-permute-start(bf16[1,192,768]{2,1,0:T(8,128)(2,1)S(1)} %copy-done.88), channel_id=1, source_target_pairs={{0,8},{1,9},{2,10},{3,11},{4,12},{5,13},{6,14},{7,15},{8,0},{9,1},... | collective-permute-start | bytes 884744 | tf_op jit(solution)/shard_map/ppermute | solution.py:687
  192.9 12.2 %collective-permute-done.17 = bf16[1,192,768]{2,1,0:T(8,128)(2,1)S(1)} collective-permute-done((bf16[1,192,768]{2,1,0:T(8,128)(2,1)S(1)}, bf16[1,192,768]{2,1,0:T(8,128)(2,1)S(1)}, u32[]{:S(2)}, u32[]{:S(2)}) %collective-permute-start.17) | collective-permute-done | bytes 294944 | tf_op jit(solution)/shard_map/ppermute | solution.py:687
  213.4 15.5 %attend.1.left_ref = bf16[576,1024]{1,0:T(8,128)(2,1)S(1)} custom-call(bf16[576,3072]{1,0:T(8,128)(2,1)S(1)} %fusion.5.q_ref.k_ref.v_ref, bf16[576,3072]{1,0:T(8,128)(2,1)S(1)} %fusion.5.q_ref.k_ref.v_ref, bf16[576,3072]{1,0:T(8,128)(2,1)S(1)} %fusion.5.q_ref.k_ref.v_ref), custom_call_target="tpu_custom_call" | custom-call | flops 13589544960 | bytes 4718592 | tf_op jit(solution)/shard_map/attend/pallas_call | solution.py:236
  236.9 15.0 %collective-permute-done.22 = bf16[4,192,384]{2,1,0:T(8,128)(2,1)S(1)} collective-permute-done((bf16[4,192,384]{2,1,0:T(8,128)(2,1)S(1)}, bf16[4,192,384]{2,1,0:T(8,128)(2,1)S(1)}, u32[]{:S(2)}, u32[]{:S(2)}) %collective-permute-start.22) | collective-permute-done | bytes 589856 | tf_op jit(solution)/shard_map/ppermute | solution.py:687
  261.4 38.3 %expand.1 = (bf16[1024,6144]{1,0:T(8,128)(2,1)}, bf16[1024,6144]{1,0:T(8,128)(2,1)}, bf16[1536,6144]{1,0:T(8,128)(2,1)}) custom-call(s32[1]{0:T(128)} %bitcast.4.me_ref, bf16[1024,1536]{1,0:T(8,128)(2,1)} %multiply_convert_fusion.2.h_ref, bf16[8,48,1536]{2,1,0:T(8,128)(2,1)} %constant_dynamic-update-slice_fusion.refs_0_, ...), custom_call_target="tpu_custom_call" | custom-call | flops 38654705664 | bytes 62914560 | tf_op jit(solution)/shard_map/expand/pallas_call | solution.py:431
  311.6 10.1 collective-permute-done.41
  330.0 27.3 %collective-permute-done.46.refs_13_ = bf16[8,192,384]{2,1,0:T(8,128)(2,1)} collective-permute-done((bf16[8,192,384]{2,1,0:T(8,128)(2,1)S(1)}, bf16[8,192,384]{2,1,0:T(8,128)(2,1)}, u32[]{:S(2)}, u32[]{:S(2)}) %collective-permute-start.46) | collective-permute-done | bytes 1179680 | tf_op jit(solution)/shard_map/ppermute | solution.py:687
  372.8 32.7 %shrink.1 = (f32[1024,1536]{1,0:T(8,128)}, bf16[1024,1536]{1,0:T(8,128)(2,1)}, bf16[1024,1536]{1,0:T(8,128)(2,1)}, bf16[6144,1536]{1,0:T(8,128)(2,1)}) custom-call(s32[1]{0:T(128)} %bitcast.4.me_ref, s32[1]{0:T(128)S(6)} %copy.100.live_ref, bf16[1024,6144]{1,0:T(8,128)(2,1)} %get-tuple-element.290.a_ref.left_ref, bf16[1024,1536]{1,0:T(8,128)(2,1)} %field_ref.6, ...), custom_call_target="tpu_custom_call" | custom-call | flops 28991029248 | bytes 56623104 | tf_op jit(solution)/shard_map/shrink/pallas_call | solution.py:494
  422.3 14.9 %gate_both.1 = (f32[576,1024]{1,0:T(8,128)}, f32[576,1024]{1,0:T(8,128)}, bf16[16,32,2048]{2,1,0:T(8,128)(2,1)}, bf16[16,32,2048]{2,1,0:T(8,128)(2,1)}) custom-call(s32[1]{0:T(128)} %bitcast.4.me_ref, s32[1]{0:T(128)S(6)} %copy.100.live_ref, f32[576,1024]{1,0:T(8,128)} %copy-done.71, bf16[576,1024]{1,0:T(8,128)(2,1)} %gv_ref.1, ...), custom_call_target="tpu_custom_call" | custom-call | flops 12079595520 | bytes 17694720 | tf_op jit(solution)/shard_map/gate_both/pallas_call | solution.py:647
  440.7 11.0 %depthwise_back.4 = (bf16[576,1024]{1,0:T(8,128)(2,1)S(1)}, f32[9,1024]{1,0:T(8,128)S(1)}) custom-call(f32[576,1024]{1,0:T(8,128)S(1)} %copy-done.73, f32[576,1024]{1,0:T(8,128)S(1)} %copy-done.68, bf16[576,1024]{1,0:T(8,128)(2,1)S(1)} %broadcast_in_dim.17.base_ref, bf16[9,1024]{1,0:T(8,128)(2,1)S(1)} %reshape.284.taps_ref), custom_call_target="tpu_custom_call", output_to_operand_aliasing={{0}: (2, {})} | custom-call | flops 6370099200 | bytes 8257536 | tf_op jit(solution)/shard_map/depthwise_back/pallas_call | solution.py:190
  456.2 12.0 %multiply_reduce_fusion.2 = (f32[1536]{0:T(1024)S(1)}, bf16[1024,1536]{1,0:T(8,128)(2,1)}, f32[1024,1536]{1,0:T(8,128)}) fusion(f32[1024,1536]{1,0:T(8,128)} %get-tuple-element.295, f32[1536]{0:T(1024)S(1)} %reshape.300, bf16[576,1024]{1,0:T(8,128)(2,1)} %copy-done.89, bf16[576,1024]{1,0:T(8,128)(2,1)S(1)} %get-tuple-element.303.right_ref, ...), kind=kOutput, calls=%fused_computation.4 | convolution fusion | flops 3635771904 | bytes 24391684 | tf_op jit(solution)/shard_map/dot_general | solution.py:28
  470.8 25.8 %outer_sum.5 = (bf16[16,192,1536]{2,1,0:T(8,128)(2,1)}, bf16[16,192,1536]{2,1,0:T(8,128)(2,1)}) custom-call(s32[1]{0:T(128)} %bitcast.4.me_ref, bf16[1024,6144]{1,0:T(8,128)(2,1)} %get-tuple-element.290.a_ref.left_ref, bf16[1024,1536]{1,0:T(8,128)(2,1)S(1)} %copy-done.64), custom_call_target="tpu_custom_call" | custom-call | flops 28991029248 | bytes 18874368 | tf_op jit(solution)/shard_map/outer_sum/pallas_call | solution.py:536
  506.0 42.4 %mlp_back.2 = (f32[1024,1536]{1,0:T(8,128)}, bf16[16,48,3072]{2,1,0:T(8,128)(2,1)}, bf16[16,48,3072]{2,1,0:T(8,128)(2,1)}) custom-call(s32[1]{0:T(128)} %bitcast.4.me_ref, bf16[1024,1536]{1,0:T(8,128)(2,1)} %get-tuple-element.323.right_ref.g_ref, bf16[1024,1536]{1,0:T(8,128)(2,1)} %multiply_convert_fusion.2.h_ref, ...), custom_call_target="tpu_custom_call" | custom-call | flops 33822867456 | bytes 28311552 | tf_op jit(solution)/shard_map/mlp_back/pallas_call | solution.py:595
  548.4 10.4 combine.25
  571.1 42.8 %mlp_both.1 = (f32[576,1024]{1,0:T(8,128)}, f32[576,1024]{1,0:T(8,128)}, bf16[16,32,4096]{2,1,0:T(8,128)(2,1)}, bf16[16,32,4096]{2,1,0:T(8,128)(2,1)}, bf16[16,1...) custom-call(s32[1]{0:T(128)} %bitcast.4.me_ref, bf16[576,1024]{1,0:T(8,128)(2,1)} %multiply_convert_fusion.5.g_ref, ...), custom_call_target="tpu_custom_call" | custom-call | flops 33822867456 | bytes 33554432 | tf_op jit(solution)/shard_map/mlp_both/pallas_call | solution.py:357
  628.8 44.7 %mlp_back.3 = (f32[1024,1536]{1,0:T(8,128)}, bf16[16,48,3072]{2,1,0:T(8,128)(2,1)}, bf16[16,48,3072]{2,1,0:T(8,128)(2,1)}) custom-call(s32[1]{0:T(128)} %bitcast.4.me_ref, bf16[1024,1536]{1,0:T(8,128)(2,1)} %get-tuple-element.323.right_ref.g_ref, bf16[1024,1536]{1,0:T(8,128)(2,1)} %multiply_convert_fusion.2.h_ref, ...), custom_call_target="tpu_custom_call" | custom-call | flops 33822867456 | bytes 28311552 | tf_op jit(solution)/shard_map/mlp_back/pallas_call | solution.py:595
  690.4 8.4 collective-permute-done.60.refs_1_.refs_3_
  701.6 10.0 combine.28
  723.5 27.5 %attend_back.1 = (bf16[576,1024]{1,0:T(8,128)(2,1)S(1)}, bf16[576,1024]{1,0:T(8,128)(2,1)S(1)}, bf16[576,1024]{1,0:T(8,128)(2,1)S(1)}) custom-call(bf16[576,3072]{1,0:T(8,128)(2,1)} %copy-done.72, bf16[576,3072]{1,0:T(8,128)(2,1)} %copy-done.72, bf16[576,3072]{1,0:T(8,128)(2,1)} %copy-done.72, bf16[576,1024]{1,0:T(8,128)(2,1)S(1)} %fusion.27.g_ref), custom_call_target="tpu_custom_call" | custom-call | flops 23781703680 | bytes 8257536 | tf_op jit(solution)/shard_map/attend_back/pallas_call | solution.py:273
  783.2 8.4 fusion.19
  807.4 9.3 outer_sum.7
  818.3 10.2 collective-permute-done.66.refs_1_.refs_3_
  847.5 26.0 %depthwise_back.5 = (f32[1024,1536]{1,0:T(8,128)}, f32[49,512]{1,0:T(8,128)S(1)}) custom-call(f32[1024,1536]{1,0:T(8,128)S(1)} %bitcast.91, bf16[1024,1536]{1,0:T(8,128)(2,1)S(1)} %copy-done.54, f32[1024,1536]{1,0:T(8,128)} %get-tuple-element.441.base_ref, bf16[49,1536]{1,0:T(8,128)(2,1)S(1)} %copy-done.49), custom_call_target="tpu_custom_call", output_to_operand_aliasing={{0}: (2, {})} | custom-call | flops 30828134400 | bytes 7340032 | tf_op jit(solution)/shard_map/depthwise_back/pallas_call | solution.py:190
  897.5 26.0 %depthwise_back.6 = (f32[1024,1536]{1,0:T(8,128)}, f32[49,512]{1,0:T(8,128)S(1)}) custom-call(f32[1024,1536]{1,0:T(8,128)S(1)} %bitcast.93, bf16[1024,1536]{1,0:T(8,128)(2,1)S(1)} %copy-done.55, f32[1024,1536]{1,0:T(8,128)} %get-tuple-element.461.base_ref, bf16[49,1536]{1,0:T(8,128)(2,1)S(1)} %copy-done.50), custom_call_target="tpu_custom_call", output_to_operand_aliasing={{0}: (2, {})} | custom-call | flops 30828134400 | bytes 7340032 | tf_op jit(solution)/shard_map/depthwise_back/pallas_call | solution.py:190
  938.7 26.3 %depthwise_back.7 = (f32[1024,1536]{1,0:T(8,128)}, f32[49,512]{1,0:T(8,128)S(1)}) custom-call(f32[1024,1536]{1,0:T(8,128)S(1)} %bitcast.93, bf16[1024,1536]{1,0:T(8,128)(2,1)S(1)} %copy-done.56, f32[1024,1536]{1,0:T(8,128)} %get-tuple-element.486.base_ref, bf16[49,1536]{1,0:T(8,128)(2,1)S(1)} %copy-done.50), custom_call_target="tpu_custom_call", output_to_operand_aliasing={{0}: (2, {})} | custom-call | flops 30828134400 | bytes 7340032 | tf_op jit(solution)/shard_map/depthwise_back/pallas_call | solution.py:190
  988.5 22.7 %collective-permute-done.87 = bf16[1,112,1024]{2,1,0:T(8,128)(2,1)} collective-permute-done((bf16[1,112,1024]{2,1,0:T(8,128)(2,1)}, bf16[1,112,1024]{2,1,0:T(8,128)(2,1)}, u32[]{:S(2)}, u32[]{:S(2)}) %collective-permute-start.87) | collective-permute-done | bytes 229408 | tf_op jit(solution)/shard_map/ppermute | solution.py:687
  1038.5 9.9 collective-permute-done.96
  (649 shorter events, 408.5 us)
Async XLA Ops:
  7.2 199.4 %all-gather.6.cloned.1.call-start = ((), (), s32[]{:S(2)}) async-start(), calls=%async_computation | async-start | bytes 8650752 | tf_op jit(solution)/shard_map/all_gather | solution.py:987
  9.0 400.4 %all-gather.8.cloned.1.call-start = ((), (), s32[]{:S(2)}) async-start(), calls=%async_computation.1 | async-start | bytes 3244032 | tf_op jit(solution)/shard_map/all_gather | solution.py:987
  9.8 412.5 %all-gather.10.cloned.1.call-start = ((), (), s32[]{:S(2)}) async-start(), calls=%async_computation.2 | async-start | bytes 4325376 | tf_op jit(solution)/shard_map/all_gather | solution.py:987
  25.2 545.9 %all-gather.12.cloned.1.call-start = ((), (), s32[]{:S(2)}) async-start(), calls=%async_computation.3 | async-start | bytes 8650752 | tf_op jit(solution)/shard_map/all_gather | solution.py:987
  78.9 57.2 %collective-permute-start.7 = (bf16[1,48,3072]{2,1,0:T(8,128)(2,1)}, bf16[1,48,3072]{2,1,0:T(8,128)(2,1)}, u32[]{:S(2)}, u32[]{:S(2)}) collective-permute-start(bf16[1,48,3072]{2,1,0:T(8,128)(2,1)} %get-tuple-element.281), channel_id=1, source_target_pairs={{0,24},{1,25},{2,26},{3,27},{4,28},{5,29},{6,30},{7,31},{8,16},{9,... | collective-permute-start | bytes 884744 | tf_op jit(solution)/shard_map/ppermute | solution.py:687
  82.2 54.9 %collective-permute-start.6 = (bf16[1,48,3072]{2,1,0:T(8,128)(2,1)}, bf16[1,48,3072]{2,1,0:T(8,128)(2,1)}, u32[]{:S(2)}, u32[]{:S(2)}) collective-permute-start(bf16[1,48,3072]{2,1,0:T(8,128)(2,1)} %get-tuple-element.281), channel_id=1, source_target_pairs={{0,16},{1,17},{2,18},{3,19},{4,20},{5,21},{6,22},{7,23},{8,24},{9,... | collective-permute-start | bytes 884744 | tf_op jit(solution)/shard_map/ppermute | solution.py:687
  82.2 55.9 %collective-permute-start.5 = (bf16[1,48,3072]{2,1,0:T(8,128)(2,1)}, bf16[1,48,3072]{2,1,0:T(8,128)(2,1)}, u32[]{:S(2)}, u32[]{:S(2)}) collective-permute-start(bf16[1,48,3072]{2,1,0:T(8,128)(2,1)} %get-tuple-element.281), channel_id=1, source_target_pairs={{0,8},{1,9},{2,10},{3,11},{4,12},{5,13},{6,14},{7,15},{8,0},{9,1},... | collective-permute-start | bytes 884744 | tf_op jit(solution)/shard_map/ppermute | solution.py:687
  83.3 56.0 %collective-permute-start.9 = (bf16[8,48,1536]{2,1,0:T(8,128)(2,1)}, bf16[8,48,1536]{2,1,0:T(8,128)(2,1)}, u32[]{:S(2)}, u32[]{:S(2)}) collective-permute-start(bf16[8,48,1536]{2,1,0:T(8,128)(2,1)} %constant_dynamic-update-slice_fusion.5.refs_4_), channel_id=1, source_target_pairs={{0,2},{1,3},{2,0},{3,1},{4,6},{5,7},{6,4},{7,5},{8,10},{9,11},{10,... | collective-permute-start | bytes 3538952 | tf_op jit(solution)/shard_map/ppermute | solution.py:687
  83.6 55.7 %collective-permute-start.8 = (bf16[8,48,1536]{2,1,0:T(8,128)(2,1)}, bf16[8,48,1536]{2,1,0:T(8,128)(2,1)}, u32[]{:S(2)}, u32[]{:S(2)}) collective-permute-start(bf16[8,48,1536]{2,1,0:T(8,128)(2,1)} %constant_dynamic-update-slice_fusion.refs_0_), channel_id=1, source_target_pairs={{0,4},{1,5},{2,6},{3,7},{4,0},{5,1},{6,2},{7,3},{8,12},{9,13},{10,... | collective-permute-start | bytes 3538952 | tf_op jit(solution)/shard_map/ppermute | solution.py:687
  141.6 94.6 %collective-permute-start.26 = (bf16[8,48,1536]{2,1,0:T(8,128)(2,1)}, bf16[8,48,1536]{2,1,0:T(8,128)(2,1)}, u32[]{:S(2)}, u32[]{:S(2)}) collective-permute-start(bf16[8,48,1536]{2,1,0:T(8,128)(2,1)} %constant_dynamic-update-slice_fusion.5.refs_4_), channel_id=1, source_target_pairs={{0,1},{1,0},{2,3},{3,2},{4,5},{5,4},{6,7},{7,6},{8,9},{9,8},{10,11... | collective-permute-start | bytes 3538952 | tf_op jit(solution)/shard_map/ppermute | solution.py:687
  141.7 94.6 %collective-permute-start.24 = (bf16[8,48,1536]{2,1,0:T(8,128)(2,1)}, bf16[8,48,1536]{2,1,0:T(8,128)(2,1)}, u32[]{:S(2)}, u32[]{:S(2)}) collective-permute-start(bf16[8,48,1536]{2,1,0:T(8,128)(2,1)} %constant_dynamic-update-slice_fusion.refs_0_), channel_id=1, source_target_pairs={{0,1},{1,0},{2,3},{3,2},{4,5},{5,4},{6,7},{7,6},{8,9},{9,8},{10,11... | collective-permute-start | bytes 3538952 | tf_op jit(solution)/shard_map/ppermute | solution.py:687
  143.7 93.1 %collective-permute-start.27 = (bf16[8,48,1536]{2,1,0:T(8,128)(2,1)}, bf16[8,48,1536]{2,1,0:T(8,128)(2,1)}, u32[]{:S(2)}, u32[]{:S(2)}) collective-permute-start(bf16[8,48,1536]{2,1,0:T(8,128)(2,1)} %collective-permute-done.9.refs_5_), channel_id=1, source_target_pairs={{0,1},{1,0},{2,3},{3,2},{4,5},{5,4},{6,7},{7,6},{8,9},{9,8},{10,11... | collective-permute-start | bytes 3538952 | tf_op jit(solution)/shard_map/ppermute | solution.py:687
  254.4 46.4 %collective-permute-start.40 = (bf16[1,192,768]{2,1,0:T(8,128)(2,1)S(1)}, bf16[1,192,768]{2,1,0:T(8,128)(2,1)S(1)}, u32[]{:S(2)}, u32[]{:S(2)}) collective-permute-start(bf16[1,192,768]{2,1,0:T(8,128)(2,1)S(1)} %copy-done.87), channel_id=1, source_target_pairs={{0,24},{1,25},{2,26},{3,27},{4,28},{5,29},{6,30},{7,31},{8,16},{9,... | collective-permute-start | bytes 884744 | tf_op jit(solution)/shard_map/ppermute | solution.py:687
  258.4 49.8 %collective-permute-start.35 = (bf16[8,192,384]{2,1,0:T(8,128)(2,1)S(1)}, bf16[8,192,384]{2,1,0:T(8,128)(2,1)S(1)}, u32[]{:S(2)}, u32[]{:S(2)}) collective-permute-start(bf16[8,192,384]{2,1,0:T(8,128)(2,1)S(1)} %constant_dynamic-update-slice_fusion.16.refs_4_), channel_id=1, source_target_pairs={{0,2},{1,3},{2,0},{3,1},{4,6},{5,7},{6,4},{7,5},{8,10},{9,11},{10,... | collective-permute-start | bytes 3538952 | tf_op jit(solution)/shard_map/ppermute | solution.py:687
  260.4 47.7 %collective-permute-start.32 = (bf16[8,192,384]{2,1,0:T(8,128)(2,1)}, bf16[8,192,384]{2,1,0:T(8,128)(2,1)}, u32[]{:S(2)}, u32[]{:S(2)}) collective-permute-start(bf16[8,192,384]{2,1,0:T(8,128)(2,1)} %constant_dynamic-update-slice_fusion.14.refs_0_), channel_id=1, source_target_pairs={{0,4},{1,5},{2,6},{3,7},{4,0},{5,1},{6,2},{7,3},{8,12},{9,13},{10,... | collective-permute-start | bytes 3538952 | tf_op jit(solution)/shard_map/ppermute | solution.py:687
  323.3 247.8 %all-gather.14.cloned.1.call-start = ((), (), s32[]{:S(2)}) async-start(), calls=%async_computation.4 | async-start | bytes 8650752 | tf_op jit(solution)/shard_map/all_gather | solution.py:987
  327.1 45.6 %collective-permute-start.34 = (bf16[8,192,384]{2,1,0:T(8,128)(2,1)}, bf16[8,192,384]{2,1,0:T(8,128)(2,1)}, u32[]{:S(2)}, u32[]{:S(2)}) collective-permute-start(bf16[8,192,384]{2,1,0:T(8,128)(2,1)} %collective-permute-done.32.refs_1_), channel_id=1, source_target_pairs={{0,1},{1,0},{2,3},{3,2},{4,5},{5,4},{6,7},{7,6},{8,9},{9,8},{10,11... | collective-permute-start | bytes 3538952 | tf_op jit(solution)/shard_map/ppermute | solution.py:687
  328.1 44.6 %collective-permute-start.47 = (bf16[8,192,384]{2,1,0:T(8,128)(2,1)S(1)}, bf16[8,192,384]{2,1,0:T(8,128)(2,1)}, u32[]{:S(2)}, u32[]{:S(2)}) collective-permute-start(bf16[8,192,384]{2,1,0:T(8,128)(2,1)S(1)} %constant_dynamic-update-slice_fusion.20.refs_12_), channel_id=1, source_target_pairs={{0,1},{1,0},{2,3},{3,2},{4,5},{5,4},{6,7},{7,6},{8,9},{9,8},{10,11... | collective-permute-start | bytes 3538952 | tf_op jit(solution)/shard_map/ppermute | solution.py:687
  561.6 57.3 %collective-permute-start.55 = (bf16[16,48,3072]{2,1,0:T(8,128)(2,1)}, bf16[16,48,3072]{2,1,0:T(8,128)(2,1)}, u32[]{:S(2)}, u32[]{:S(2)}) collective-permute-start(bf16[16,48,3072]{2,1,0:T(8,128)(2,1)} %get-tuple-element.348), channel_id=1, source_target_pairs={{0,1},{1,0},{2,3},{3,2},{4,5},{5,4},{6,7},{7,6},{8,9},{9,8},{10,11... | collective-permute-start | bytes 14155784 | tf_op jit(solution)/shard_map/ppermute | solution.py:687
  564.5 53.9 %collective-permute-start.53 = (bf16[8,192,768]{2,1,0:T(8,128)(2,1)}, bf16[8,192,768]{2,1,0:T(8,128)(2,1)}, u32[]{:S(2)}, u32[]{:S(2)}) collective-permute-start(bf16[8,192,768]{2,1,0:T(8,128)(2,1)} %copy-done.57), channel_id=1, source_target_pairs={{0,4},{1,5},{2,6},{3,7},{4,0},{5,1},{6,2},{7,3},{8,12},{9,13},{10,... | collective-permute-start | bytes 7077896 | tf_op jit(solution)/shard_map/ppermute | solution.py:687
  565.1 53.7 %collective-permute-start.54 = (bf16[8,192,768]{2,1,0:T(8,128)(2,1)}, bf16[8,192,768]{2,1,0:T(8,128)(2,1)}, u32[]{:S(2)}, u32[]{:S(2)}) collective-permute-start(bf16[8,192,768]{2,1,0:T(8,128)(2,1)} %get-tuple-element.347), channel_id=1, source_target_pairs={{0,2},{1,3},{2,0},{3,1},{4,6},{5,7},{6,4},{7,5},{8,10},{9,11},{10,... | collective-permute-start | bytes 7077896 | tf_op jit(solution)/shard_map/ppermute | solution.py:687
  625.6 73.2 %collective-permute-start.56 = (bf16[4,192,768]{2,1,0:T(8,128)(2,1)}, bf16[4,192,768]{2,1,0:T(8,128)(2,1)}, u32[]{:S(2)}, u32[]{:S(2)}) collective-permute-start(bf16[4,192,768]{2,1,0:T(8,128)(2,1)} %get-tuple-element.369), channel_id=1, source_target_pairs={{0,2},{1,3},{2,0},{3,1},{4,6},{5,7},{6,4},{7,5},{8,10},{9,11},{10,... | collective-permute-start | bytes 3538952 | tf_op jit(solution)/shard_map/ppermute | solution.py:687
  627.0 71.8 %collective-permute-start.57 = (bf16[4,192,768]{2,1,0:T(8,128)(2,1)}, bf16[4,192,768]{2,1,0:T(8,128)(2,1)}, u32[]{:S(2)}, u32[]{:S(2)}) collective-permute-start(bf16[4,192,768]{2,1,0:T(8,128)(2,1)} %get-tuple-element.370), channel_id=1, source_target_pairs={{0,4},{1,5},{2,6},{3,7},{4,0},{5,1},{6,2},{7,3},{8,12},{9,13},{10,... | collective-permute-start | bytes 3538952 | tf_op jit(solution)/shard_map/ppermute | solution.py:687
  628.3 70.5 %collective-permute-start.58 = (bf16[16,32,4096]{2,1,0:T(8,128)(2,1)}, bf16[16,32,4096]{2,1,0:T(8,128)(2,1)}, u32[]{:S(2)}, u32[]{:S(2)}) collective-permute-start(bf16[16,32,4096]{2,1,0:T(8,128)(2,1)} %get-tuple-element.371), channel_id=1, source_target_pairs={{0,1},{1,0},{2,3},{3,2},{4,5},{5,4},{6,7},{7,6},{8,9},{9,8},{10,11... | collective-permute-start | bytes 12582920 | tf_op jit(solution)/shard_map/ppermute | solution.py:687
  628.3 70.5 %collective-permute-start.59 = (bf16[16,128,1024]{2,1,0:T(8,128)(2,1)}, bf16[16,128,1024]{2,1,0:T(8,128)(2,1)}, u32[]{:S(2)}, u32[]{:S(2)}) collective-permute-start(bf16[16,128,1024]{2,1,0:T(8,128)(2,1)} %get-tuple-element.372), channel_id=1, source_target_pairs={{0,1},{1,0},{2,3},{3,2},{4,5},{5,4},{6,7},{7,6},{8,9},{9,8},{10,11... | collective-permute-start | bytes 12582920 | tf_op jit(solution)/shard_map/ppermute | solution.py:687
  715.6 53.3 %collective-permute-start.65 = (bf16[2,112,1024]{2,1,0:T(8,128)(2,1)}, bf16[2,112,1024]{2,1,0:T(8,128)(2,1)}, u32[]{:S(2)}, u32[]{:S(2)}) collective-permute-start(bf16[2,112,1024]{2,1,0:T(8,128)(2,1)} %get-tuple-element.399), channel_id=1, source_target_pairs={{0,8},{1,9},{2,10},{3,11},{4,12},{5,13},{6,14},{7,15},{8,0},{9,1},... | collective-permute-start | bytes 1376264 | tf_op jit(solution)/shard_map/ppermute | solution.py:687
  715.8 53.1 %collective-permute-start.63 = (bf16[2,384,768]{2,1,0:T(8,128)(2,1)}, bf16[2,384,768]{2,1,0:T(8,128)(2,1)S(1)}, u32[]{:S(2)}, u32[]{:S(2)}) collective-permute-start(bf16[2,384,768]{2,1,0:T(8,128)(2,1)} %get-tuple-element.397), channel_id=1, source_target_pairs={{0,8},{1,9},{2,10},{3,11},{4,12},{5,13},{6,14},{7,15},{8,0},{9,1},... | collective-permute-start | bytes 3538952 | tf_op jit(solution)/shard_map/ppermute | solution.py:687
  717.9 51.1 %collective-permute-start.61 = (bf16[8,32,4096]{2,1,0:T(8,128)(2,1)}, bf16[8,32,4096]{2,1,0:T(8,128)(2,1)}, u32[]{:S(2)}, u32[]{:S(2)}) collective-permute-start(bf16[8,32,4096]{2,1,0:T(8,128)(2,1)} %get-tuple-element.395), channel_id=1, source_target_pairs={{0,4},{1,5},{2,6},{3,7},{4,0},{5,1},{6,2},{7,3},{8,12},{9,13},{10,... | collective-permute-start | bytes 6291464 | tf_op jit(solution)/shard_map/ppermute | solution.py:687
  718.6 50.4 %collective-permute-start.62 = (bf16[8,128,1024]{2,1,0:T(8,128)(2,1)}, bf16[8,128,1024]{2,1,0:T(8,128)(2,1)}, u32[]{:S(2)}, u32[]{:S(2)}) collective-permute-start(bf16[8,128,1024]{2,1,0:T(8,128)(2,1)} %get-tuple-element.396), channel_id=1, source_target_pairs={{0,2},{1,3},{2,0},{3,1},{4,6},{5,7},{6,4},{7,5},{8,10},{9,11},{10,... | collective-permute-start | bytes 6291464 | tf_op jit(solution)/shard_map/ppermute | solution.py:687
  719.3 49.7 %collective-permute-start.64 = (bf16[16,48,3072]{2,1,0:T(8,128)(2,1)}, bf16[16,48,3072]{2,1,0:T(8,128)(2,1)}, u32[]{:S(2)}, u32[]{:S(2)}) collective-permute-start(bf16[16,48,3072]{2,1,0:T(8,128)(2,1)} %get-tuple-element.398), channel_id=1, source_target_pairs={{0,1},{1,0},{2,3},{3,2},{4,5},{5,4},{6,7},{7,6},{8,9},{9,8},{10,11... | collective-permute-start | bytes 14155784 | tf_op jit(solution)/shard_map/ppermute | solution.py:687
  779.7 48.9 %collective-permute-start.66 = (bf16[8,48,1536]{2,1,0:T(8,128)(2,1)}, bf16[8,48,1536]{2,1,0:T(8,128)(2,1)S(1)}, u32[]{:S(2)}, u32[]{:S(2)}) collective-permute-start(bf16[8,48,1536]{2,1,0:T(8,128)(2,1)} %get-tuple-element.419), channel_id=1, source_target_pairs={{0,4},{1,5},{2,6},{3,7},{4,0},{5,1},{6,2},{7,3},{8,12},{9,13},{10,... | collective-permute-start | bytes 3538952 | tf_op jit(solution)/shard_map/ppermute | solution.py:687
  780.1 49.5 %collective-permute-start.67 = (bf16[8,48,1536]{2,1,0:T(8,128)(2,1)}, bf16[8,48,1536]{2,1,0:T(8,128)(2,1)}, u32[]{:S(2)}, u32[]{:S(2)}) collective-permute-start(bf16[8,48,1536]{2,1,0:T(8,128)(2,1)} %get-tuple-element.420), channel_id=1, source_target_pairs={{0,2},{1,3},{2,0},{3,1},{4,6},{5,7},{6,4},{7,5},{8,10},{9,11},{10,... | collective-permute-start | bytes 3538952 | tf_op jit(solution)/shard_map/ppermute | solution.py:687
  (203 other events, 3359.4 us)
Sparse Core Ops, SparseCore 0:
  10.9 119.8 all-gather.5
  133.7 72.1 all-gather.7
  209.3 78.9 all-gather.9
  323.4 78.6 all-gather.11
  404.8 76.0 all-gather.13

commit v4 on v3

--- a/solution.py
+++ b/solution.py
@@ -3,6 +3,7 @@
 
 import jax
 import jax.numpy as jnp
+import numpy as np
 from jax import lax
 from jax.experimental import pallas as pl
 from jax.experimental.pallas import tpu as pltpu
@@ -56,13 +57,14 @@
     return (values * cdf, cdf + values * density)
 
 
-def pool_table(fine_cells, coarse_cells):
-    coarse_index = jnp.arange(coarse_cells, dtype=jnp.int32)[:, None]
-    fine_index = jnp.arange(fine_cells, dtype=jnp.int32)[None, :]
+def pool_matrix(fine_cells, coarse_cells):
+    coarse_index = np.arange(coarse_cells)[:, None]
+    fine_index = np.arange(fine_cells)[None, :]
     window_start = coarse_index * fine_cells // coarse_cells
     window_end = ((coarse_index + 1) * fine_cells + coarse_cells - 1) // coarse_cells
-    inside = ((fine_index >= window_start) & (fine_index < window_end)).astype(jnp.float32)
-    return inside / jnp.sum(inside, axis=1, keepdims=True)
+    inside = ((fine_index >= window_start) & (fine_index < window_end)).astype(np.float32)
+    table = inside / np.sum(inside, axis=1, keepdims=True)
+    return jnp.asarray(np.kron(table, table), BF16)
 
 
 def fill_shifted(shifted, field, width, edge):
@@ -1048,8 +1050,7 @@
         ),
     )
 
-    table = pool_table(GRID_HR, GRID_LR)
-    pool = jnp.einsum("ia,jb->ijab", table, table).reshape(GRID_LR**2, GRID_HR**2).astype(BF16)
+    pool = pool_matrix(GRID_HR, GRID_LR)
 
     def adapter(hires_low):
         pooled_low = dot(pool, hires_low, NN).astype(BF16)

time: 1060 us -> 1050 us (level)
    unnamed x280 -> x278, local copies, waits for them, and re-layouts: 58.3 us -> 57.4 us
  transfers between devices with their start and end apart: 102 -> 102, of which waited for: 30 -> 31; matrix products, arithmetic and copies ran while one was open for 14% -> 13% of each run, Pallas kernels for 44% -> 45%
where the time goes in v4:
time: 1050 us
  Pallas kernels  520 us (50%)
  waiting for transfers between devices  216 us (21%)
  local copies, waits for them, and re-layouts  104 us (10%)
  starting transfers between devices  96.2 us (9%)
  other arithmetic  50.2 us (5%)
  matrix products  42.9 us (4%)
  between operations  16.7 us (2%)
    ppermute x92, waiting for transfers between devices, swap(): lax.ppermute(block, 'fsdp', [(index, index ^ mask) for index in range(dev...  198 us
    pallas_call x4, Pallas kernels, depthwise_back(): pl.pallas_call(functools.partial(depthwise_back_kernel, width, edge), gri...  89.3 us
    ppermute x92, starting transfers between devices, swap(): lax.ppermute(block, 'fsdp', [(index, index ^ mask) for index in range(dev...  89 us
    pallas_call x24, Pallas kernels, combine(): pl.pallas_call(functools.partial(combine_kernel, widths, stacked), grid_s...  89 us
    pallas_call x2, Pallas kernels, mlp_back(): pl.pallas_call(functools.partial(mlp_back_kernel, step, share, start is n...  87.2 us
    unnamed x278, local copies, waits for them, and re-layouts  57.4 us
    dot_general x7, matrix products, dot(): lax.dot_general(left, right, (dims, ((), ())), preferred_element_type=F32)  42.9 us
    pallas_call x1, Pallas kernels, mlp_both(): pl.pallas_call(functools.partial(mlp_both_kernel, (in_rows, out_rows)), g...  42.7 us
  transfers between devices with their start and end apart: 102, of which 31 were waited for; matrix products, arithmetic and copies ran while one was open for 13% of the time, Pallas kernels for 45%

profile of v4, /device:TPU:0, one launch (start us, length us, event | category | flops | bytes accessed | tf_op | source)
XLA Modules:
  0.0 1046.1 jit_solution(17301103254369601311)
XLA Ops:
  31.9 15.4 %collective-permute-done.13 = bf16[8,2800]{1,0:T(8,128)(2,1)S(1)} collective-permute-done((bf16[8,2800]{1,0:T(8,128)(2,1)S(1)}, bf16[8,2800]{1,0:T(8,128)(2,1)S(1)}, u32[]{:S(2)}, u32[]{:S(2)}) %collective-permute-start.13) | collective-permute-done | bytes 44832 | tf_op jit(solution)/shard_map/ppermute | solution.py:671
  66.1 8.9 collective-permute-done.3
  85.3 36.5 %depthwise.2 = f32[1024,1536]{1,0:T(8,128)S(1)} custom-call(bf16[1024,1536]{1,0:T(8,128)(2,1)S(1)} %copy-done.53, bf16[49,1536]{1,0:T(8,128)(2,1)S(1)} %reshape.231.taps_ref), custom_call_target="tpu_custom_call" | custom-call | flops 46242201600 | bytes 12582912 | tf_op jit(solution)/shard_map/depthwise/pallas_call | solution.py:121
  144.6 8.7 collective-permute-done.15
  162.9 9.2 collective-permute-done.19
  172.1 12.9 %collective-permute-start.17 = (bf16[1,192,768]{2,1,0:T(8,128)(2,1)S(1)}, bf16[1,192,768]{2,1,0:T(8,128)(2,1)S(1)}, u32[]{:S(2)}, u32[]{:S(2)}) collective-permute-start(bf16[1,192,768]{2,1,0:T(8,128)(2,1)S(1)} %copy-done.88), channel_id=1, source_target_pairs={{0,8},{1,9},{2,10},{3,11},{4,12},{5,13},{6,14},{7,15},{8,0},{9,1},... | collective-permute-start | bytes 884744 | tf_op jit(solution)/shard_map/ppermute | solution.py:689
  192.8 12.3 %collective-permute-done.17 = bf16[1,192,768]{2,1,0:T(8,128)(2,1)S(1)} collective-permute-done((bf16[1,192,768]{2,1,0:T(8,128)(2,1)S(1)}, bf16[1,192,768]{2,1,0:T(8,128)(2,1)S(1)}, u32[]{:S(2)}, u32[]{:S(2)}) %collective-permute-start.17) | collective-permute-done | bytes 294944 | tf_op jit(solution)/shard_map/ppermute | solution.py:689
  213.4 15.5 %attend.1.left_ref = bf16[576,1024]{1,0:T(8,128)(2,1)S(1)} custom-call(bf16[576,3072]{1,0:T(8,128)(2,1)S(1)} %fusion.4.q_ref.k_ref.v_ref, bf16[576,3072]{1,0:T(8,128)(2,1)S(1)} %fusion.4.q_ref.k_ref.v_ref, bf16[576,3072]{1,0:T(8,128)(2,1)S(1)} %fusion.4.q_ref.k_ref.v_ref), custom_call_target="tpu_custom_call" | custom-call | flops 13589544960 | bytes 4718592 | tf_op jit(solution)/shard_map/attend/pallas_call | solution.py:238
  236.9 15.0 %collective-permute-done.22 = bf16[4,192,384]{2,1,0:T(8,128)(2,1)S(1)} collective-permute-done((bf16[4,192,384]{2,1,0:T(8,128)(2,1)S(1)}, bf16[4,192,384]{2,1,0:T(8,128)(2,1)S(1)}, u32[]{:S(2)}, u32[]{:S(2)}) %collective-permute-start.22) | collective-permute-done | bytes 589856 | tf_op jit(solution)/shard_map/ppermute | solution.py:689
  261.4 38.3 %expand.1 = (bf16[1024,6144]{1,0:T(8,128)(2,1)}, bf16[1024,6144]{1,0:T(8,128)(2,1)}, bf16[1536,6144]{1,0:T(8,128)(2,1)}) custom-call(s32[1]{0:T(128)} %bitcast.4.me_ref, bf16[1024,1536]{1,0:T(8,128)(2,1)} %multiply_convert_fusion.1.h_ref, bf16[8,48,1536]{2,1,0:T(8,128)(2,1)} %constant_dynamic-update-slice_fusion.refs_0_, ...), custom_call_target="tpu_custom_call" | custom-call | flops 38654705664 | bytes 62914560 | tf_op jit(solution)/shard_map/expand/pallas_call | solution.py:433
  310.8 10.9 %collective-permute-done.41 = bf16[4,192,384]{2,1,0:T(8,128)(2,1)S(1)} collective-permute-done((bf16[4,192,384]{2,1,0:T(8,128)(2,1)S(1)}, bf16[4,192,384]{2,1,0:T(8,128)(2,1)S(1)}, u32[]{:S(2)}, u32[]{:S(2)}) %collective-permute-start.41) | collective-permute-done | bytes 589856 | tf_op jit(solution)/shard_map/ppermute | solution.py:689
  331.5 25.6 %collective-permute-done.46.refs_13_ = bf16[8,192,384]{2,1,0:T(8,128)(2,1)} collective-permute-done((bf16[8,192,384]{2,1,0:T(8,128)(2,1)S(1)}, bf16[8,192,384]{2,1,0:T(8,128)(2,1)}, u32[]{:S(2)}, u32[]{:S(2)}) %collective-permute-start.46) | collective-permute-done | bytes 1179680 | tf_op jit(solution)/shard_map/ppermute | solution.py:689
  362.0 33.0 %shrink.1 = (f32[1024,1536]{1,0:T(8,128)}, bf16[1024,1536]{1,0:T(8,128)(2,1)}, bf16[1024,1536]{1,0:T(8,128)(2,1)}, bf16[6144,1536]{1,0:T(8,128)(2,1)}) custom-call(s32[1]{0:T(128)} %bitcast.4.me_ref, s32[1]{0:T(128)S(6)} %copy.101.live_ref, bf16[1024,6144]{1,0:T(8,128)(2,1)} %get-tuple-element.290.a_ref.left_ref, bf16[1024,1536]{1,0:T(8,128)(2,1)} %field_ref.6, ...), custom_call_target="tpu_custom_call" | custom-call | flops 28991029248 | bytes 56623104 | tf_op jit(solution)/shard_map/shrink/pallas_call | solution.py:496
  412.4 14.9 %gate_both.1 = (f32[576,1024]{1,0:T(8,128)}, f32[576,1024]{1,0:T(8,128)}, bf16[16,32,2048]{2,1,0:T(8,128)(2,1)}, bf16[16,32,2048]{2,1,0:T(8,128)(2,1)}) custom-call(s32[1]{0:T(128)} %bitcast.4.me_ref, s32[1]{0:T(128)S(6)} %copy.101.live_ref, f32[576,1024]{1,0:T(8,128)} %copy-done.71, bf16[576,1024]{1,0:T(8,128)(2,1)} %gv_ref.1, ...), custom_call_target="tpu_custom_call" | custom-call | flops 12079595520 | bytes 17694720 | tf_op jit(solution)/shard_map/gate_both/pallas_call | solution.py:649
  430.9 11.0 %depthwise_back.4 = (bf16[576,1024]{1,0:T(8,128)(2,1)S(1)}, f32[9,1024]{1,0:T(8,128)S(1)}) custom-call(f32[576,1024]{1,0:T(8,128)S(1)} %copy-done.73, f32[576,1024]{1,0:T(8,128)S(1)} %copy-done.70, bf16[576,1024]{1,0:T(8,128)(2,1)S(1)} %broadcast_in_dim.17.base_ref, bf16[9,1024]{1,0:T(8,128)(2,1)S(1)} %reshape.234.taps_ref), custom_call_target="tpu_custom_call", output_to_operand_aliasing={{0}: (2, {})} | custom-call | flops 6370099200 | bytes 8257536 | tf_op jit(solution)/shard_map/depthwise_back/pallas_call | solution.py:192
  446.4 11.9 %multiply_reduce_fusion.2 = (f32[1536]{0:T(1024)S(1)}, bf16[1024,1536]{1,0:T(8,128)(2,1)}, f32[1024,1536]{1,0:T(8,128)}) fusion(f32[1024,1536]{1,0:T(8,128)} %get-tuple-element.295, f32[1536]{0:T(1024)S(1)} %reshape.250, bf16[576,1024]{1,0:T(8,128)(2,1)} %constant.75.clone, bf16[576,1024]{1,0:T(8,128)(2,1)S(1)} %get-tuple-element.303.right_ref, ...), kind=kOutput, calls=%fused_computation.3 | convolution fusion | flops 3635771904 | bytes 24391684 | tf_op jit(solution)/shard_map/dot_general | solution.py:29
  460.8 25.9 %outer_sum.5 = (bf16[16,192,1536]{2,1,0:T(8,128)(2,1)}, bf16[16,192,1536]{2,1,0:T(8,128)(2,1)}) custom-call(s32[1]{0:T(128)} %bitcast.4.me_ref, bf16[1024,6144]{1,0:T(8,128)(2,1)} %get-tuple-element.290.a_ref.left_ref, bf16[1024,1536]{1,0:T(8,128)(2,1)S(1)} %copy-done.66), custom_call_target="tpu_custom_call" | custom-call | flops 28991029248 | bytes 18874368 | tf_op jit(solution)/shard_map/outer_sum/pallas_call | solution.py:538
  495.3 42.6 %mlp_back.2 = (f32[1024,1536]{1,0:T(8,128)}, bf16[16,48,3072]{2,1,0:T(8,128)(2,1)}, bf16[16,48,3072]{2,1,0:T(8,128)(2,1)}) custom-call(s32[1]{0:T(128)} %bitcast.4.me_ref, bf16[1024,1536]{1,0:T(8,128)(2,1)} %get-tuple-element.323.right_ref.g_ref, bf16[1024,1536]{1,0:T(8,128)(2,1)} %multiply_convert_fusion.1.h_ref, ...), custom_call_target="tpu_custom_call" | custom-call | flops 33822867456 | bytes 28311552 | tf_op jit(solution)/shard_map/mlp_back/pallas_call | solution.py:597
  537.9 10.4 combine.25
  561.5 42.7 %mlp_both.1 = (f32[576,1024]{1,0:T(8,128)}, f32[576,1024]{1,0:T(8,128)}, bf16[16,32,4096]{2,1,0:T(8,128)(2,1)}, bf16[16,32,4096]{2,1,0:T(8,128)(2,1)}, bf16[16,1...) custom-call(s32[1]{0:T(128)} %bitcast.4.me_ref, bf16[576,1024]{1,0:T(8,128)(2,1)} %multiply_convert_fusion.4.g_ref, ...), custom_call_target="tpu_custom_call" | custom-call | flops 33822867456 | bytes 33554432 | tf_op jit(solution)/shard_map/mlp_both/pallas_call | solution.py:359
  618.2 44.7 %mlp_back.3 = (f32[1024,1536]{1,0:T(8,128)}, bf16[16,48,3072]{2,1,0:T(8,128)(2,1)}, bf16[16,48,3072]{2,1,0:T(8,128)(2,1)}) custom-call(s32[1]{0:T(128)} %bitcast.4.me_ref, bf16[1024,1536]{1,0:T(8,128)(2,1)} %get-tuple-element.323.right_ref.g_ref, bf16[1024,1536]{1,0:T(8,128)(2,1)} %multiply_convert_fusion.1.h_ref, ...), custom_call_target="tpu_custom_call" | custom-call | flops 33822867456 | bytes 28311552 | tf_op jit(solution)/shard_map/mlp_back/pallas_call | solution.py:597
  667.7 8.3 combine.31
  691.0 10.0 combine.28
  713.4 27.5 %attend_back.1 = (bf16[576,1024]{1,0:T(8,128)(2,1)S(1)}, bf16[576,1024]{1,0:T(8,128)(2,1)S(1)}, bf16[576,1024]{1,0:T(8,128)(2,1)S(1)}) custom-call(bf16[576,3072]{1,0:T(8,128)(2,1)} %copy-done.72, bf16[576,3072]{1,0:T(8,128)(2,1)} %copy-done.72, bf16[576,3072]{1,0:T(8,128)(2,1)} %copy-done.72, bf16[576,1024]{1,0:T(8,128)(2,1)S(1)} %fusion.26.g_ref), custom_call_target="tpu_custom_call" | custom-call | flops 23781703680 | bytes 8257536 | tf_op jit(solution)/shard_map/attend_back/pallas_call | solution.py:275
  771.8 8.4 fusion.18
  796.0 9.3 outer_sum.7
  806.9 11.3 %collective-permute-done.66.refs_1_.refs_3_ = bf16[8,48,1536]{2,1,0:T(8,128)(2,1)S(1)} collective-permute-done((bf16[8,48,1536]{2,1,0:T(8,128)(2,1)}, bf16[8,48,1536]{2,1,0:T(8,128)(2,1)S(1)}, u32[]{:S(2)}, u32[]{:S(2)}) %collective-permute-start.66) | collective-permute-done | bytes 1179680 | tf_op jit(solution)/shard_map/ppermute | solution.py:689
  837.1 26.0 %depthwise_back.5 = (f32[1024,1536]{1,0:T(8,128)}, f32[49,512]{1,0:T(8,128)S(1)}) custom-call(f32[1024,1536]{1,0:T(8,128)S(1)} %bitcast.88, bf16[1024,1536]{1,0:T(8,128)(2,1)S(1)} %copy-done.54, f32[1024,1536]{1,0:T(8,128)} %get-tuple-element.441.base_ref, bf16[49,1536]{1,0:T(8,128)(2,1)S(1)} %copy-done.49), custom_call_target="tpu_custom_call", output_to_operand_aliasing={{0}: (2, {})} | custom-call | flops 30828134400 | bytes 7340032 | tf_op jit(solution)/shard_map/depthwise_back/pallas_call | solution.py:192
  886.8 26.0 %depthwise_back.6 = (f32[1024,1536]{1,0:T(8,128)}, f32[49,512]{1,0:T(8,128)S(1)}) custom-call(f32[1024,1536]{1,0:T(8,128)S(1)} %bitcast.90, bf16[1024,1536]{1,0:T(8,128)(2,1)S(1)} %copy-done.55, f32[1024,1536]{1,0:T(8,128)} %get-tuple-element.461.base_ref, bf16[49,1536]{1,0:T(8,128)(2,1)S(1)} %copy-done.50), custom_call_target="tpu_custom_call", output_to_operand_aliasing={{0}: (2, {})} | custom-call | flops 30828134400 | bytes 7340032 | tf_op jit(solution)/shard_map/depthwise_back/pallas_call | solution.py:192
  928.6 26.3 %depthwise_back.7 = (f32[1024,1536]{1,0:T(8,128)}, f32[49,512]{1,0:T(8,128)S(1)}) custom-call(f32[1024,1536]{1,0:T(8,128)S(1)} %bitcast.90, bf16[1024,1536]{1,0:T(8,128)(2,1)S(1)} %copy-done.56, f32[1024,1536]{1,0:T(8,128)} %get-tuple-element.486.base_ref, bf16[49,1536]{1,0:T(8,128)(2,1)S(1)} %copy-done.50), custom_call_target="tpu_custom_call", output_to_operand_aliasing={{0}: (2, {})} | custom-call | flops 30828134400 | bytes 7340032 | tf_op jit(solution)/shard_map/depthwise_back/pallas_call | solution.py:192
  977.1 23.4 %collective-permute-done.87 = bf16[1,112,1024]{2,1,0:T(8,128)(2,1)} collective-permute-done((bf16[1,112,1024]{2,1,0:T(8,128)(2,1)}, bf16[1,112,1024]{2,1,0:T(8,128)(2,1)}, u32[]{:S(2)}, u32[]{:S(2)}) %collective-permute-start.87) | collective-permute-done | bytes 229408 | tf_op jit(solution)/shard_map/ppermute | solution.py:689
  1027.3 10.4 collective-permute-done.96
  (642 shorter events, 396.1 us)
Async XLA Ops:
  7.2 199.4 %all-gather.6.cloned.1.call-start = ((), (), s32[]{:S(2)}) async-start(), calls=%async_computation | async-start | bytes 8650752 | tf_op jit(solution)/shard_map/all_gather | solution.py:989
  9.0 390.4 %all-gather.8.cloned.1.call-start = ((), (), s32[]{:S(2)}) async-start(), calls=%async_computation.1 | async-start | bytes 3244032 | tf_op jit(solution)/shard_map/all_gather | solution.py:989
  9.8 402.6 %all-gather.10.cloned.1.call-start = ((), (), s32[]{:S(2)}) async-start(), calls=%async_computation.2 | async-start | bytes 4325376 | tf_op jit(solution)/shard_map/all_gather | solution.py:989
  25.2 536.3 %all-gather.12.cloned.1.call-start = ((), (), s32[]{:S(2)}) async-start(), calls=%async_computation.3 | async-start | bytes 8650752 | tf_op jit(solution)/shard_map/all_gather | solution.py:989
  78.9 57.2 %collective-permute-start.7 = (bf16[1,48,3072]{2,1,0:T(8,128)(2,1)}, bf16[1,48,3072]{2,1,0:T(8,128)(2,1)}, u32[]{:S(2)}, u32[]{:S(2)}) collective-permute-start(bf16[1,48,3072]{2,1,0:T(8,128)(2,1)} %get-tuple-element.281), channel_id=1, source_target_pairs={{0,24},{1,25},{2,26},{3,27},{4,28},{5,29},{6,30},{7,31},{8,16},{9,... | collective-permute-start | bytes 884744 | tf_op jit(solution)/shard_map/ppermute | solution.py:689
  82.2 54.9 %collective-permute-start.6 = (bf16[1,48,3072]{2,1,0:T(8,128)(2,1)}, bf16[1,48,3072]{2,1,0:T(8,128)(2,1)}, u32[]{:S(2)}, u32[]{:S(2)}) collective-permute-start(bf16[1,48,3072]{2,1,0:T(8,128)(2,1)} %get-tuple-element.281), channel_id=1, source_target_pairs={{0,16},{1,17},{2,18},{3,19},{4,20},{5,21},{6,22},{7,23},{8,24},{9,... | collective-permute-start | bytes 884744 | tf_op jit(solution)/shard_map/ppermute | solution.py:689
  82.2 55.9 %collective-permute-start.5 = (bf16[1,48,3072]{2,1,0:T(8,128)(2,1)}, bf16[1,48,3072]{2,1,0:T(8,128)(2,1)}, u32[]{:S(2)}, u32[]{:S(2)}) collective-permute-start(bf16[1,48,3072]{2,1,0:T(8,128)(2,1)} %get-tuple-element.281), channel_id=1, source_target_pairs={{0,8},{1,9},{2,10},{3,11},{4,12},{5,13},{6,14},{7,15},{8,0},{9,1},... | collective-permute-start | bytes 884744 | tf_op jit(solution)/shard_map/ppermute | solution.py:689
  83.3 56.0 %collective-permute-start.9 = (bf16[8,48,1536]{2,1,0:T(8,128)(2,1)}, bf16[8,48,1536]{2,1,0:T(8,128)(2,1)}, u32[]{:S(2)}, u32[]{:S(2)}) collective-permute-start(bf16[8,48,1536]{2,1,0:T(8,128)(2,1)} %constant_dynamic-update-slice_fusion.5.refs_4_), channel_id=1, source_target_pairs={{0,2},{1,3},{2,0},{3,1},{4,6},{5,7},{6,4},{7,5},{8,10},{9,11},{10,... | collective-permute-start | bytes 3538952 | tf_op jit(solution)/shard_map/ppermute | solution.py:689
  83.6 55.7 %collective-permute-start.8 = (bf16[8,48,1536]{2,1,0:T(8,128)(2,1)}, bf16[8,48,1536]{2,1,0:T(8,128)(2,1)}, u32[]{:S(2)}, u32[]{:S(2)}) collective-permute-start(bf16[8,48,1536]{2,1,0:T(8,128)(2,1)} %constant_dynamic-update-slice_fusion.refs_0_), channel_id=1, source_target_pairs={{0,4},{1,5},{2,6},{3,7},{4,0},{5,1},{6,2},{7,3},{8,12},{9,13},{10,... | collective-permute-start | bytes 3538952 | tf_op jit(solution)/shard_map/ppermute | solution.py:689
  141.6 94.7 %collective-permute-start.26 = (bf16[8,48,1536]{2,1,0:T(8,128)(2,1)}, bf16[8,48,1536]{2,1,0:T(8,128)(2,1)}, u32[]{:S(2)}, u32[]{:S(2)}) collective-permute-start(bf16[8,48,1536]{2,1,0:T(8,128)(2,1)} %constant_dynamic-update-slice_fusion.5.refs_4_), channel_id=1, source_target_pairs={{0,1},{1,0},{2,3},{3,2},{4,5},{5,4},{6,7},{7,6},{8,9},{9,8},{10,11... | collective-permute-start | bytes 3538952 | tf_op jit(solution)/shard_map/ppermute | solution.py:689
  141.7 94.6 %collective-permute-start.24 = (bf16[8,48,1536]{2,1,0:T(8,128)(2,1)}, bf16[8,48,1536]{2,1,0:T(8,128)(2,1)}, u32[]{:S(2)}, u32[]{:S(2)}) collective-permute-start(bf16[8,48,1536]{2,1,0:T(8,128)(2,1)} %constant_dynamic-update-slice_fusion.refs_0_), channel_id=1, source_target_pairs={{0,1},{1,0},{2,3},{3,2},{4,5},{5,4},{6,7},{7,6},{8,9},{9,8},{10,11... | collective-permute-start | bytes 3538952 | tf_op jit(solution)/shard_map/ppermute | solution.py:689
  143.7 93.1 %collective-permute-start.27 = (bf16[8,48,1536]{2,1,0:T(8,128)(2,1)}, bf16[8,48,1536]{2,1,0:T(8,128)(2,1)}, u32[]{:S(2)}, u32[]{:S(2)}) collective-permute-start(bf16[8,48,1536]{2,1,0:T(8,128)(2,1)} %collective-permute-done.9.refs_5_), channel_id=1, source_target_pairs={{0,1},{1,0},{2,3},{3,2},{4,5},{5,4},{6,7},{7,6},{8,9},{9,8},{10,11... | collective-permute-start | bytes 3538952 | tf_op jit(solution)/shard_map/ppermute | solution.py:689
  254.4 46.4 %collective-permute-start.40 = (bf16[1,192,768]{2,1,0:T(8,128)(2,1)S(1)}, bf16[1,192,768]{2,1,0:T(8,128)(2,1)S(1)}, u32[]{:S(2)}, u32[]{:S(2)}) collective-permute-start(bf16[1,192,768]{2,1,0:T(8,128)(2,1)S(1)} %copy-done.87), channel_id=1, source_target_pairs={{0,24},{1,25},{2,26},{3,27},{4,28},{5,29},{6,30},{7,31},{8,16},{9,... | collective-permute-start | bytes 884744 | tf_op jit(solution)/shard_map/ppermute | solution.py:689
  257.3 43.5 %collective-permute-start.39 = (bf16[1,192,768]{2,1,0:T(8,128)(2,1)S(1)}, bf16[1,192,768]{2,1,0:T(8,128)(2,1)S(1)}, u32[]{:S(2)}, u32[]{:S(2)}) collective-permute-start(bf16[1,192,768]{2,1,0:T(8,128)(2,1)S(1)} %copy-done.87), channel_id=1, source_target_pairs={{0,16},{1,17},{2,18},{3,19},{4,20},{5,21},{6,22},{7,23},{8,24},{9,... | collective-permute-start | bytes 884744 | tf_op jit(solution)/shard_map/ppermute | solution.py:689
  258.3 49.7 %collective-permute-start.35 = (bf16[8,192,384]{2,1,0:T(8,128)(2,1)S(1)}, bf16[8,192,384]{2,1,0:T(8,128)(2,1)S(1)}, u32[]{:S(2)}, u32[]{:S(2)}) collective-permute-start(bf16[8,192,384]{2,1,0:T(8,128)(2,1)S(1)} %constant_dynamic-update-slice_fusion.16.refs_4_), channel_id=1, source_target_pairs={{0,2},{1,3},{2,0},{3,1},{4,6},{5,7},{6,4},{7,5},{8,10},{9,11},{10,... | collective-permute-start | bytes 3538952 | tf_op jit(solution)/shard_map/ppermute | solution.py:689
  260.4 47.6 %collective-permute-start.32 = (bf16[8,192,384]{2,1,0:T(8,128)(2,1)}, bf16[8,192,384]{2,1,0:T(8,128)(2,1)}, u32[]{:S(2)}, u32[]{:S(2)}) collective-permute-start(bf16[8,192,384]{2,1,0:T(8,128)(2,1)} %constant_dynamic-update-slice_fusion.14.refs_0_), channel_id=1, source_target_pairs={{0,4},{1,5},{2,6},{3,7},{4,0},{5,1},{6,2},{7,3},{8,12},{9,13},{10,... | collective-permute-start | bytes 3538952 | tf_op jit(solution)/shard_map/ppermute | solution.py:689
  323.2 238.3 %all-gather.14.cloned.1.call-start = ((), (), s32[]{:S(2)}) async-start(), calls=%async_computation.4 | async-start | bytes 8650752 | tf_op jit(solution)/shard_map/all_gather | solution.py:989
  494.2 43.7 %collective-permute-start.52 = (bf16[16,192,1536]{2,1,0:T(8,128)(2,1)}, bf16[16,192,1536]{2,1,0:T(8,128)(2,1)}, u32[]{:S(2)}, u32[]{:S(2)}) collective-permute-start(bf16[16,192,1536]{2,1,0:T(8,128)(2,1)} %get-tuple-element.331), channel_id=1, source_target_pairs={{0,1},{1,0},{2,3},{3,2},{4,5},{5,4},{6,7},{7,6},{8,9},{9,8},{10,11... | collective-permute-start | bytes 28311560 | tf_op jit(solution)/shard_map/ppermute | solution.py:689
  551.0 57.7 %collective-permute-start.55 = (bf16[16,48,3072]{2,1,0:T(8,128)(2,1)}, bf16[16,48,3072]{2,1,0:T(8,128)(2,1)}, u32[]{:S(2)}, u32[]{:S(2)}) collective-permute-start(bf16[16,48,3072]{2,1,0:T(8,128)(2,1)} %get-tuple-element.348), channel_id=1, source_target_pairs={{0,1},{1,0},{2,3},{3,2},{4,5},{5,4},{6,7},{7,6},{8,9},{9,8},{10,11... | collective-permute-start | bytes 14155784 | tf_op jit(solution)/shard_map/ppermute | solution.py:689
  554.1 53.8 %collective-permute-start.53 = (bf16[8,192,768]{2,1,0:T(8,128)(2,1)}, bf16[8,192,768]{2,1,0:T(8,128)(2,1)}, u32[]{:S(2)}, u32[]{:S(2)}) collective-permute-start(bf16[8,192,768]{2,1,0:T(8,128)(2,1)} %copy-done.57), channel_id=1, source_target_pairs={{0,4},{1,5},{2,6},{3,7},{4,0},{5,1},{6,2},{7,3},{8,12},{9,13},{10,... | collective-permute-start | bytes 7077896 | tf_op jit(solution)/shard_map/ppermute | solution.py:689
  555.1 53.7 %collective-permute-start.54 = (bf16[8,192,768]{2,1,0:T(8,128)(2,1)}, bf16[8,192,768]{2,1,0:T(8,128)(2,1)}, u32[]{:S(2)}, u32[]{:S(2)}) collective-permute-start(bf16[8,192,768]{2,1,0:T(8,128)(2,1)} %get-tuple-element.347), channel_id=1, source_target_pairs={{0,2},{1,3},{2,0},{3,1},{4,6},{5,7},{6,4},{7,5},{8,10},{9,11},{10,... | collective-permute-start | bytes 7077896 | tf_op jit(solution)/shard_map/ppermute | solution.py:689
  615.6 72.6 %collective-permute-start.56 = (bf16[4,192,768]{2,1,0:T(8,128)(2,1)}, bf16[4,192,768]{2,1,0:T(8,128)(2,1)}, u32[]{:S(2)}, u32[]{:S(2)}) collective-permute-start(bf16[4,192,768]{2,1,0:T(8,128)(2,1)} %get-tuple-element.369), channel_id=1, source_target_pairs={{0,2},{1,3},{2,0},{3,1},{4,6},{5,7},{6,4},{7,5},{8,10},{9,11},{10,... | collective-permute-start | bytes 3538952 | tf_op jit(solution)/shard_map/ppermute | solution.py:689
  617.2 70.9 %collective-permute-start.57 = (bf16[4,192,768]{2,1,0:T(8,128)(2,1)}, bf16[4,192,768]{2,1,0:T(8,128)(2,1)}, u32[]{:S(2)}, u32[]{:S(2)}) collective-permute-start(bf16[4,192,768]{2,1,0:T(8,128)(2,1)} %get-tuple-element.370), channel_id=1, source_target_pairs={{0,4},{1,5},{2,6},{3,7},{4,0},{5,1},{6,2},{7,3},{8,12},{9,13},{10,... | collective-permute-start | bytes 3538952 | tf_op jit(solution)/shard_map/ppermute | solution.py:689
  617.7 70.5 %collective-permute-start.58 = (bf16[16,32,4096]{2,1,0:T(8,128)(2,1)}, bf16[16,32,4096]{2,1,0:T(8,128)(2,1)}, u32[]{:S(2)}, u32[]{:S(2)}) collective-permute-start(bf16[16,32,4096]{2,1,0:T(8,128)(2,1)} %get-tuple-element.371), channel_id=1, source_target_pairs={{0,1},{1,0},{2,3},{3,2},{4,5},{5,4},{6,7},{7,6},{8,9},{9,8},{10,11... | collective-permute-start | bytes 12582920 | tf_op jit(solution)/shard_map/ppermute | solution.py:689
  617.7 70.5 %collective-permute-start.59 = (bf16[16,128,1024]{2,1,0:T(8,128)(2,1)}, bf16[16,128,1024]{2,1,0:T(8,128)(2,1)}, u32[]{:S(2)}, u32[]{:S(2)}) collective-permute-start(bf16[16,128,1024]{2,1,0:T(8,128)(2,1)} %get-tuple-element.372), channel_id=1, source_target_pairs={{0,1},{1,0},{2,3},{3,2},{4,5},{5,4},{6,7},{7,6},{8,9},{9,8},{10,11... | collective-permute-start | bytes 12582920 | tf_op jit(solution)/shard_map/ppermute | solution.py:689
  705.0 53.9 %collective-permute-start.65 = (bf16[2,112,1024]{2,1,0:T(8,128)(2,1)}, bf16[2,112,1024]{2,1,0:T(8,128)(2,1)}, u32[]{:S(2)}, u32[]{:S(2)}) collective-permute-start(bf16[2,112,1024]{2,1,0:T(8,128)(2,1)} %get-tuple-element.399), channel_id=1, source_target_pairs={{0,8},{1,9},{2,10},{3,11},{4,12},{5,13},{6,14},{7,15},{8,0},{9,1},... | collective-permute-start | bytes 1376264 | tf_op jit(solution)/shard_map/ppermute | solution.py:689
  705.2 53.7 %collective-permute-start.63 = (bf16[2,384,768]{2,1,0:T(8,128)(2,1)}, bf16[2,384,768]{2,1,0:T(8,128)(2,1)S(1)}, u32[]{:S(2)}, u32[]{:S(2)}) collective-permute-start(bf16[2,384,768]{2,1,0:T(8,128)(2,1)} %get-tuple-element.397), channel_id=1, source_target_pairs={{0,8},{1,9},{2,10},{3,11},{4,12},{5,13},{6,14},{7,15},{8,0},{9,1},... | collective-permute-start | bytes 3538952 | tf_op jit(solution)/shard_map/ppermute | solution.py:689
  707.2 51.7 %collective-permute-start.61 = (bf16[8,32,4096]{2,1,0:T(8,128)(2,1)}, bf16[8,32,4096]{2,1,0:T(8,128)(2,1)}, u32[]{:S(2)}, u32[]{:S(2)}) collective-permute-start(bf16[8,32,4096]{2,1,0:T(8,128)(2,1)} %get-tuple-element.395), channel_id=1, source_target_pairs={{0,4},{1,5},{2,6},{3,7},{4,0},{5,1},{6,2},{7,3},{8,12},{9,13},{10,... | collective-permute-start | bytes 6291464 | tf_op jit(solution)/shard_map/ppermute | solution.py:689
  708.9 50.1 %collective-permute-start.62 = (bf16[8,128,1024]{2,1,0:T(8,128)(2,1)}, bf16[8,128,1024]{2,1,0:T(8,128)(2,1)}, u32[]{:S(2)}, u32[]{:S(2)}) collective-permute-start(bf16[8,128,1024]{2,1,0:T(8,128)(2,1)} %get-tuple-element.396), channel_id=1, source_target_pairs={{0,2},{1,3},{2,0},{3,1},{4,6},{5,7},{6,4},{7,5},{8,10},{9,11},{10,... | collective-permute-start | bytes 6291464 | tf_op jit(solution)/shard_map/ppermute | solution.py:689
  709.3 49.7 %collective-permute-start.64 = (bf16[16,48,3072]{2,1,0:T(8,128)(2,1)}, bf16[16,48,3072]{2,1,0:T(8,128)(2,1)}, u32[]{:S(2)}, u32[]{:S(2)}) collective-permute-start(bf16[16,48,3072]{2,1,0:T(8,128)(2,1)} %get-tuple-element.398), channel_id=1, source_target_pairs={{0,1},{1,0},{2,3},{3,2},{4,5},{5,4},{6,7},{7,6},{8,9},{9,8},{10,11... | collective-permute-start | bytes 14155784 | tf_op jit(solution)/shard_map/ppermute | solution.py:689
  768.3 49.8 %collective-permute-start.66 = (bf16[8,48,1536]{2,1,0:T(8,128)(2,1)}, bf16[8,48,1536]{2,1,0:T(8,128)(2,1)S(1)}, u32[]{:S(2)}, u32[]{:S(2)}) collective-permute-start(bf16[8,48,1536]{2,1,0:T(8,128)(2,1)} %get-tuple-element.419), channel_id=1, source_target_pairs={{0,4},{1,5},{2,6},{3,7},{4,0},{5,1},{6,2},{7,3},{8,12},{9,13},{10,... | collective-permute-start | bytes 3538952 | tf_op jit(solution)/shard_map/ppermute | solution.py:689
  769.7 49.5 %collective-permute-start.67 = (bf16[8,48,1536]{2,1,0:T(8,128)(2,1)}, bf16[8,48,1536]{2,1,0:T(8,128)(2,1)}, u32[]{:S(2)}, u32[]{:S(2)}) collective-permute-start(bf16[8,48,1536]{2,1,0:T(8,128)(2,1)} %get-tuple-element.420), channel_id=1, source_target_pairs={{0,2},{1,3},{2,0},{3,1},{4,6},{5,7},{6,4},{7,5},{8,10},{9,11},{10,... | collective-permute-start | bytes 3538952 | tf_op jit(solution)/shard_map/ppermute | solution.py:689
  (202 other events, 3294.1 us)
Sparse Core Ops, SparseCore 0:
  10.9 119.8 all-gather.5
  133.7 72.1 all-gather.7
  209.3 78.9 all-gather.9
  323.3 78.5 all-gather.11
  404.6 76.0 all-gather.13
